TPU v7x, 32 devices: a whole 2x2x4 slice. The times are simulated.
32 devices in a mesh: dp: 8 (over z, y), mem: 4 (over x, core).
Axes of the slice: x: 2, y: 2, z: 4, core: 2. Of those that a mesh axis runs over, the one named last changes fastest.
Arguments:
- tokens: bfloat16 [16384, 1024], P(('dp', 'mem')), may hold values from -6 to 6
- norm_gains: bfloat16 [2, 1024], P(None, ('dp', 'mem')), may hold values from 0.099609375 to 1.8984375
- norm_shifts: bfloat16 [2, 1024], P(None, ('dp', 'mem')), may hold values from -1.796875 to 1.796875
- w_qkv: bfloat16 [1024, 3072], P(('dp', 'mem')), may hold values from -0.1875 to 0.1875
- w_out: bfloat16 [1024, 1024], P(('dp', 'mem')), may hold values from -1.5 to 1.5
- w_up: bfloat16 [1024, 4096], P(('dp', 'mem')), may hold values from -0.1875 to 0.1875
- w_down: bfloat16 [4096, 1024], P(('dp', 'mem')), may hold values from -0.09375 to 0.09375
- rel_table: float32 [32, 8], replicated, may hold values from -3 to 3
- gate_bias: float32 [8], replicated, may hold values from -2 to 2
- xl_cache: bfloat16 [16384, 2048], P(('dp', 'mem')), may hold values from -6 to 6
- memory: bfloat16 [65536, 8, 256], P(('dp', 'mem')), may hold values from -6 to 6
- slot_index: int32 [16384, 8, 32], P('dp', None, 'mem'), may hold values from 0 to 8191, as said below
- seg_len: int32 [32], P(('dp', 'mem')), may hold values from 64 to 512, as said below
- cotangent: bfloat16 [16384, 1024], P(('dp', 'mem')), may hold values from -6 to 6
Outputs:
- layer_out: bfloat16 [16384, 1024], P(('dp', 'mem'))
- grad_tokens: float32 [16384, 1024], P(('dp', 'mem'))
- grad_gains: float32 [2, 1024], P(None, ('dp', 'mem'))
- grad_shifts: float32 [2, 1024], P(None, ('dp', 'mem'))
- grad_qkv: float32 [1024, 3072], P(('dp', 'mem'))
- grad_wout: float32 [1024, 1024], P(('dp', 'mem'))
- grad_up: float32 [1024, 4096], P(('dp', 'mem'))
- grad_down: float32 [4096, 1024], P(('dp', 'mem'))
- grad_table: float32 [32, 8], replicated
- grad_gate: float32 [8], replicated
Inputs may be any that keep to these rules, and one draw needn't show every extreme that they name: `slot_index`: columns m * 8 to (m + 1) * 8 - 1 of a token's row hold slots m * 2048 to (m + 1) * 2048 - 1 of its group, for each m below 4. `seg_len`: some segment has all 512 tokens.
All inputs are finite; a program needn't handle non-finite values.
Results may differ from a plain program's by a relative error of at most 0.01.
Values may be sent and summed in bfloat16 or wider, within the bound.
A program may use at most 448 MiB of HBM per device.

v0:
```python
import jax
import jax.numpy as jnp
import numpy as np
from jax import lax
from jax.sharding import PartitionSpec as P

H = 8
HD = 128
W = 512
BUCKETS = 32


EPSILON = 1e-05
HIGHEST = lax.Precision.HIGHEST
NEGATIVE = -1e30


def bucket_table(window, buckets):
    distance = np.arange(2 * window)
    exact_count = buckets // 2
    log_bucket = exact_count + np.floor(
        np.log(np.maximum(distance, 1) / exact_count) / np.log(128.0 / exact_count) * exact_count
    )
    bucket = np.where(distance < exact_count, distance, np.minimum(log_bucket, buckets - 1)).astype(
        np.int32
    )
    relative = np.maximum(np.arange(window)[:, None] - np.arange(2 * window)[None, :] + window, 0)
    return bucket[relative]


def norm_forward(values, gain_row, shift_row):
    center = values - jnp.mean(values, axis=-1, keepdims=True)
    inverse = lax.rsqrt(jnp.mean(center * center, axis=-1, keepdims=True) + EPSILON)
    scaled = center * inverse
    return (scaled * gain_row + shift_row, scaled, inverse)


def norm_backward(grad_normed, scaled, inverse, gain_row):
    grad_scaled = grad_normed * gain_row
    mean_grad = jnp.mean(grad_scaled, axis=-1, keepdims=True)
    mean_cross = jnp.mean(grad_scaled * scaled, axis=-1, keepdims=True)
    return inverse * (grad_scaled - mean_grad - scaled * mean_cross)


def segment_mask(length):
    row_ids = lax.broadcasted_iota(jnp.int32, (W, 2 * W), 0)
    col_ids = lax.broadcasted_iota(jnp.int32, (W, 2 * W), 1)
    return (row_ids - col_ids + W >= 0) & ((col_ids < W) | (col_ids - W < length))


def local_scores(query_heads, key_all, bias_full, allowed):
    raw_scores = jnp.einsum(
        "ihd,chd->hic", query_heads, key_all, preferred_element_type=jnp.float32
    )
    return jnp.where(allowed[None], raw_scores * HD ** (-0.5) + bias_full, NEGATIVE)


def local_forward(query_heads, key_all, value_all, bias_full, allowed):
    scores = local_scores(query_heads, key_all, bias_full, allowed)
    lse_local = jax.nn.logsumexp(scores, axis=-1, keepdims=True)
    weights = jnp.exp(scores - lse_local).astype(jnp.bfloat16)
    local_out = jnp.einsum("hic,chd->ihd", weights, value_all, preferred_element_type=jnp.float32)
    return (local_out, lse_local)


def local_backward(query_heads, key_all, value_all, bias_full, allowed, lse_local, grad_local):
    scores = local_scores(query_heads, key_all, bias_full, allowed)
    weights = jnp.exp(scores - lse_local)
    grad_weights = jnp.einsum(
        "ihd,chd->hic", grad_local, value_all, preferred_element_type=jnp.float32
    )
    grad_scores = weights * (grad_weights - jnp.sum(weights * grad_weights, axis=-1, keepdims=True))
    low_grad = grad_scores.astype(jnp.bfloat16)
    grad_query = jnp.einsum(
        "hic,chd->ihd", low_grad, key_all, preferred_element_type=jnp.float32
    ) * HD ** (-0.5)
    grad_key = jnp.einsum(
        "hic,ihd->chd", low_grad[:, :, W:], query_heads, preferred_element_type=jnp.float32
    ) * HD ** (-0.5)
    grad_value = jnp.einsum(
        "hic,ihd->chd",
        weights.astype(jnp.bfloat16)[:, :, W:],
        grad_local,
        preferred_element_type=jnp.float32,
    )
    return (grad_query, grad_key, grad_value, grad_scores)


def slot_counts(slot_part, slot_total):
    slot_ids = lax.broadcasted_iota(jnp.int32, (1, 1, slot_total), 2)
    counts = jnp.zeros(slot_part.shape[:2] + (slot_total,), jnp.float32)
    for column in range(slot_part.shape[2]):
        counts = counts + (slot_part[:, :, column, None] == slot_ids).astype(jnp.float32)
    return counts


def part_scores(query_heads, slot_part, keys_part):
    counts = slot_counts(slot_part, keys_part.shape[0])
    raw = jnp.einsum(
        "bhd,shd->bhs", query_heads, keys_part, preferred_element_type=jnp.float32
    ) * HD ** (-0.5)
    scores = jnp.where(counts > 0, raw, NEGATIVE)
    part_lse = jax.nn.logsumexp(scores, axis=-1, b=counts)
    probs = counts * jnp.exp(scores - part_lse[..., None])
    return (probs, part_lse)


def recall_parts(query_heads, slot_rows, table_parts):
    probs, part_lse = part_scores(query_heads, slot_rows[:, :, 0], table_parts[0, :, :, :HD])
    outs = [
        jnp.einsum(
            "bhs,shd->bhd",
            probs.astype(jnp.bfloat16),
            table_parts[0, :, :, HD:],
            preferred_element_type=jnp.float32,
        )
    ]
    totals = [part_lse]
    return (jnp.stack(outs, axis=2), jnp.stack(totals, axis=2))


def recall_grad(query_heads, slot_rows, table_parts, grad_recalled, grad_delta, total_lse):
    grad_query = jnp.zeros(query_heads.shape, jnp.float32)
    keys_part = table_parts[0, :, :, :HD]
    values_part = table_parts[0, :, :, HD:]
    probs, part_lse = part_scores(query_heads, slot_rows[:, :, 0], keys_part)
    part_out = jnp.einsum(
        "bhs,shd->bhd", probs.astype(jnp.bfloat16), values_part, preferred_element_type=jnp.float32
    )
    part_share = jnp.exp(part_lse - total_lse)
    grad_along = jnp.einsum(
        "bhd,shd->bhs", grad_recalled, values_part.astype(jnp.float32), precision=HIGHEST
    )
    expected = jnp.sum(probs * grad_along, axis=-1, keepdims=True)
    own_part = jnp.sum(grad_recalled * part_out, axis=-1)
    grad_scores = (
        probs * part_share[..., None] * (grad_along - expected + (own_part - grad_delta)[..., None])
    )
    grad_query = grad_query + jnp.einsum(
        "bhs,shd->bhd", grad_scores, keys_part.astype(jnp.float32), precision=HIGHEST
    ) * HD ** (-0.5)
    return grad_query


def combine_parts(part_out, part_lse, axis_index):
    total_lse = jax.nn.logsumexp(part_lse, axis=axis_index, keepdims=True)
    part_share = jnp.exp(part_lse - total_lse)
    return (
        jnp.sum(part_share[..., None] * part_out, axis=axis_index),
        jnp.squeeze(total_lse, axis_index),
    )


def local(
    tokens,
    norm_gains,
    norm_shifts,
    w_qkv,
    w_out,
    w_up,
    w_down,
    rel_table,
    gate_bias,
    xl_cache,
    memory,
    slot_index,
    seg_len,
    cotangent,
):
    full_gains, full_shifts, full_qkv, full_out, full_up, full_down = (
        lax.all_gather(norm_gains, ("dp", "mem"), axis=1, tiled=True),
        lax.all_gather(norm_shifts, ("dp", "mem"), axis=1, tiled=True),
        lax.all_gather(w_qkv, ("dp", "mem"), axis=0, tiled=True),
        lax.all_gather(w_out, ("dp", "mem"), axis=0, tiled=True),
        lax.all_gather(w_up, ("dp", "mem"), axis=0, tiled=True),
        lax.all_gather(w_down, ("dp", "mem"), axis=0, tiled=True),
    )
    model_width = tokens.shape[1]
    tok_count = tokens.shape[0]
    segments = tok_count // W
    groups = lax.axis_size("mem")
    slot_count = memory.shape[0]
    inputs = tokens.astype(jnp.float32)
    gain_rows = full_gains.astype(jnp.float32)
    shift_rows = full_shifts.astype(jnp.float32)
    normed_one, scaled_one, inverse_one = norm_forward(inputs, gain_rows[0], shift_rows[0])
    normed_one = normed_one.astype(jnp.bfloat16)
    projected = jnp.dot(normed_one, full_qkv, preferred_element_type=jnp.float32).astype(
        jnp.bfloat16
    )
    queries = projected[:, :model_width].reshape(tok_count, H, HD)
    seg_keys = jnp.concatenate(
        [
            xl_cache[:, :model_width].reshape(segments, W, H, HD),
            projected[:, model_width : 2 * model_width].reshape(segments, W, H, HD),
        ],
        axis=1,
    )
    seg_values = jnp.concatenate(
        [
            xl_cache[:, model_width:].reshape(segments, W, H, HD),
            projected[:, 2 * model_width :].reshape(segments, W, H, HD),
        ],
        axis=1,
    )
    query_segs = queries.reshape(segments, W, H, HD)
    bucket_of = jnp.asarray(bucket_table(W, BUCKETS))
    bias_full = jnp.zeros((H, W, 2 * W), jnp.float32)
    for bucket in range(BUCKETS):
        bias_full = bias_full + jnp.where(
            (bucket_of == bucket)[None], rel_table[bucket][:, None, None], 0.0
        )

    def forward_segment(segment_inputs):
        query_heads, keys_seg, values_seg, length = segment_inputs
        return local_forward(query_heads, keys_seg, values_seg, bias_full, segment_mask(length))

    local_out, lse_local = lax.map(forward_segment, (query_segs, seg_keys, seg_values, seg_len))
    local_flat = local_out.reshape(tok_count, H, HD)
    table_parts = memory.reshape(1, slot_count, H, 2 * HD)
    ask_queries = lax.all_gather(queries, "mem", axis=0, tiled=True)
    slot_rows = (slot_index - lax.axis_index("mem") * slot_count).reshape(
        slot_index.shape[0], H, 1, -1
    )
    blocks = ask_queries.shape[0] // W
    query_blocks = ask_queries.reshape(blocks, W, H, HD)
    row_blocks = slot_rows.reshape((blocks, W) + slot_rows.shape[1:])

    def forward_block(block_inputs):
        query_block, row_block = block_inputs
        return recall_parts(query_block, row_block, table_parts)

    part_out, part_lse = lax.map(forward_block, (query_blocks, row_blocks))
    sent_out = part_out.reshape(groups, tok_count, H, HD)
    sent_lse = part_lse.reshape(groups, tok_count, H)
    back_parts, back_lse = (
        lax.all_to_all(sent_out, "mem", split_axis=0, concat_axis=0, tiled=True),
        lax.all_to_all(sent_lse, "mem", split_axis=0, concat_axis=0, tiled=True),
    )
    recalled, total_lse = combine_parts(back_parts, back_lse, 0)
    gate_open = jax.nn.sigmoid(gate_bias)
    mixed = gate_open[:, None] * recalled + (1.0 - gate_open[:, None]) * local_flat
    mixed_low = mixed.reshape(tok_count, model_width).astype(jnp.bfloat16)
    attended = inputs + jnp.dot(mixed_low, full_out, preferred_element_type=jnp.float32)
    normed_two, scaled_two, inverse_two = norm_forward(attended, gain_rows[1], shift_rows[1])
    normed_two = normed_two.astype(jnp.bfloat16)
    up_pre = jnp.dot(normed_two, full_up, preferred_element_type=jnp.float32)
    hidden = jax.nn.gelu(up_pre).astype(jnp.bfloat16)
    output = attended + jnp.dot(hidden, full_down, preferred_element_type=jnp.float32)
    back_gains, back_qkv, back_out, back_up, back_down = (
        lax.all_gather(norm_gains, ("dp", "mem"), axis=1, tiled=True),
        lax.all_gather(w_qkv, ("dp", "mem"), axis=0, tiled=True),
        lax.all_gather(w_out, ("dp", "mem"), axis=0, tiled=True),
        lax.all_gather(w_up, ("dp", "mem"), axis=0, tiled=True),
        lax.all_gather(w_down, ("dp", "mem"), axis=0, tiled=True),
    )
    back_gain_rows = back_gains.astype(jnp.float32)
    grad_output = cotangent.astype(jnp.float32)
    grad_down = jnp.einsum("tf,td->fd", hidden, cotangent, preferred_element_type=jnp.float32)
    grad_hidden = jnp.einsum("td,fd->tf", cotangent, back_down, preferred_element_type=jnp.float32)
    grad_up_pre = jax.vjp(jax.nn.gelu, up_pre)[1](grad_hidden)[0].astype(jnp.bfloat16)
    grad_up = jnp.einsum("td,tf->df", normed_two, grad_up_pre, preferred_element_type=jnp.float32)
    grad_normed_two = jnp.einsum(
        "tf,df->td", grad_up_pre, back_up, preferred_element_type=jnp.float32
    )
    grad_attended = grad_output + norm_backward(
        grad_normed_two, scaled_two, inverse_two, back_gain_rows[1]
    )
    attended_low = grad_attended.astype(jnp.bfloat16)
    grad_wout = jnp.einsum("td,te->de", mixed_low, attended_low, preferred_element_type=jnp.float32)
    grad_mixed = jnp.einsum(
        "te,de->td", attended_low, back_out, preferred_element_type=jnp.float32
    ).reshape(tok_count, H, HD)
    grad_gate = (
        jnp.sum(grad_mixed * (recalled - local_flat), axis=(0, 2)) * gate_open * (1.0 - gate_open)
    )
    grad_local = ((1.0 - gate_open[:, None]) * grad_mixed).astype(jnp.bfloat16)
    grad_recalled = gate_open[:, None] * grad_mixed
    grad_delta = jnp.sum(grad_recalled * recalled, axis=-1)

    def backward_block(block_inputs):
        query_block, row_block, grad_block, delta_block, total_block = block_inputs
        return recall_grad(
            query_block, row_block, table_parts, grad_block, delta_block, total_block
        )

    ask_grad, ask_delta, ask_total = (
        lax.all_gather(grad_recalled, "mem", axis=0, tiled=True),
        lax.all_gather(grad_delta, "mem", axis=0, tiled=True),
        lax.all_gather(total_lse, "mem", axis=0, tiled=True),
    )
    grad_parts = lax.map(
        backward_block,
        (
            query_blocks,
            row_blocks,
            ask_grad.reshape(blocks, W, H, HD),
            ask_delta.reshape(blocks, W, H),
            ask_total.reshape(blocks, W, H),
        ),
    )
    returned = lax.all_to_all(grad_parts, "mem", split_axis=0, concat_axis=0, tiled=True)
    grad_query_memory = jnp.sum(returned, axis=0)

    def backward_segment(score_total, segment_inputs):
        query_heads, keys_seg, values_seg, length, lse_seg, grad_seg = segment_inputs
        grad_query, grad_key, grad_value, grad_scores = local_backward(
            query_heads, keys_seg, values_seg, bias_full, segment_mask(length), lse_seg, grad_seg
        )
        return (score_total + grad_scores, (grad_query, grad_key, grad_value))

    score_total, (grad_query_local, grad_keys, grad_values) = lax.scan(
        backward_segment,
        jnp.zeros((H, W, 2 * W), jnp.float32),
        (
            query_segs,
            seg_keys,
            seg_values,
            seg_len,
            lse_local,
            grad_local.reshape(segments, W, H, HD),
        ),
    )
    table_rows = []
    for bucket in range(BUCKETS):
        table_rows.append(
            jnp.sum(jnp.where((bucket_of == bucket)[None], score_total, 0.0), axis=(1, 2))
        )
    grad_table = jnp.stack(table_rows, axis=0)
    grad_query = grad_query_local.reshape(tok_count, H, HD) + grad_query_memory
    grad_qkv_low = jnp.concatenate(
        [
            grad_query.reshape(tok_count, model_width),
            grad_keys.reshape(tok_count, model_width),
            grad_values.reshape(tok_count, model_width),
        ],
        axis=1,
    ).astype(jnp.bfloat16)
    grad_wqkv = jnp.einsum(
        "td,te->de", normed_one, grad_qkv_low, preferred_element_type=jnp.float32
    )
    grad_normed_one = jnp.einsum(
        "te,de->td", grad_qkv_low, back_qkv, preferred_element_type=jnp.float32
    )
    grad_tokens = grad_attended + norm_backward(
        grad_normed_one, scaled_one, inverse_one, back_gain_rows[0]
    )
    grad_gains = jnp.stack(
        [
            jnp.sum(grad_normed_one * scaled_one, axis=0),
            jnp.sum(grad_normed_two * scaled_two, axis=0),
        ]
    )
    grad_shifts = jnp.stack([jnp.sum(grad_normed_one, axis=0), jnp.sum(grad_normed_two, axis=0)])
    share_gains, share_shifts, share_qkv, share_out, share_up, share_down = (
        lax.psum_scatter(grad_gains, ("dp", "mem"), scatter_dimension=1, tiled=True),
        lax.psum_scatter(grad_shifts, ("dp", "mem"), scatter_dimension=1, tiled=True),
        lax.psum_scatter(grad_wqkv, ("dp", "mem"), scatter_dimension=0, tiled=True),
        lax.psum_scatter(grad_wout, ("dp", "mem"), scatter_dimension=0, tiled=True),
        lax.psum_scatter(grad_up, ("dp", "mem"), scatter_dimension=0, tiled=True),
        lax.psum_scatter(grad_down, ("dp", "mem"), scatter_dimension=0, tiled=True),
    )
    table_total, gate_total = lax.psum((grad_table, grad_gate), ("dp", "mem"))
    return (
        output.astype(jnp.bfloat16),
        grad_tokens,
        share_gains,
        share_shifts,
        share_qkv,
        share_out,
        share_up,
        share_down,
        table_total,
        gate_total,
    )


def solution(mesh):
    placed = (
        P(("dp", "mem"), None),
        P(None, ("dp", "mem")),
        P(None, ("dp", "mem")),
        P(("dp", "mem"), None),
        P(("dp", "mem"), None),
        P(("dp", "mem"), None),
        P(("dp", "mem"), None),
        P(),
        P(),
        P(("dp", "mem"), None),
        P(("dp", "mem"), None, None),
        P("dp", None, "mem"),
        P(("dp", "mem")),
        P(("dp", "mem"), None),
    )
    return jax.shard_map(
        local,
        mesh=mesh,
        in_specs=placed,
        out_specs=(
            P(("dp", "mem"), None),
            P(("dp", "mem"), None),
            P(None, ("dp", "mem")),
            P(None, ("dp", "mem")),
            P(("dp", "mem"), None),
            P(("dp", "mem"), None),
            P(("dp", "mem"), None),
            P(("dp", "mem"), None),
            P(),
            P(),
        ),
        check_vma=False,
    )
```

profile of v0, /device:TPU:0, one launch (start us, length us, event | category | flops | bytes accessed | tf_op | source)
XLA Modules:
  0.0 3160.5 jit_solution(3184881897743547905)
XLA Ops:
  139.7 552.5 %while.4 = (s32[]{:T(128)}, f32[4,512,8,1,128]{4,1,2,3,0:T(8,128)}, f32[4,512,8,1]{1,2,3,0:T(8,128)}, s32[4,512,8,1,8]{1,2,4,3,0:T(8,128)S(1)}, bf16[4,512,8,128...) while((s32[]{:T(128)}, f32[4,512,8,1,128]{4,1,2,3,0:T(8,128)}, ...), condition=%wide.region_5.6_spmd, body=%wide.region_2.5_spmd.sunk | while | flops 5041610752 | bytes 113311840 | solution.py:233
  183.5 49.3 %multiply_reduce_fusion.12 = f32[512,8]{0,1:T(8,128)S(1)} fusion(f32[8,512,2048]{2,1,0:T(8,128)S(1)} %get-tuple-element.484, f32[512,8]{0,1:T(8,128)S(1)} %is-finite_select_fusion.7, s32[512,8]{0,1:T(8,128)S(1)} %get-tuple-element.476, s32[512,8]{0,1:T(8,128)S(1)} %get-tuple-element.477, s32[512,8]{0,1:T(8,128)S(1)} %get-tuple-element.478, ...), kind=kLoop, calls=%fused_computation.2.clone.1 | loop fusion | flops 260042752 | bytes 33718272 | tf_op jit(solution)/shard_map/while/body/eval_jaxpr/reduce_sum | solution.py:103
  321.4 49.3 %multiply_reduce_fusion.12 = f32[512,8]{0,1:T(8,128)S(1)} fusion(f32[8,512,2048]{2,1,0:T(8,128)S(1)} %get-tuple-element.484, f32[512,8]{0,1:T(8,128)S(1)} %is-finite_select_fusion.7, s32[512,8]{0,1:T(8,128)S(1)} %get-tuple-element.476, s32[512,8]{0,1:T(8,128)S(1)} %get-tuple-element.477, s32[512,8]{0,1:T(8,128)S(1)} %get-tuple-element.478, ...), kind=kLoop, calls=%fused_computation.2.clone.1 | loop fusion | flops 260042752 | bytes 33718272 | tf_op jit(solution)/shard_map/while/body/eval_jaxpr/reduce_sum | solution.py:103
  459.3 49.3 %multiply_reduce_fusion.12 = f32[512,8]{0,1:T(8,128)S(1)} fusion(f32[8,512,2048]{2,1,0:T(8,128)S(1)} %get-tuple-element.484, f32[512,8]{0,1:T(8,128)S(1)} %is-finite_select_fusion.7, s32[512,8]{0,1:T(8,128)S(1)} %get-tuple-element.476, s32[512,8]{0,1:T(8,128)S(1)} %get-tuple-element.477, s32[512,8]{0,1:T(8,128)S(1)} %get-tuple-element.478, ...), kind=kLoop, calls=%fused_computation.2.clone.1 | loop fusion | flops 260042752 | bytes 33718272 | tf_op jit(solution)/shard_map/while/body/eval_jaxpr/reduce_sum | solution.py:103
  597.3 49.3 %multiply_reduce_fusion.12 = f32[512,8]{0,1:T(8,128)S(1)} fusion(f32[8,512,2048]{2,1,0:T(8,128)S(1)} %get-tuple-element.484, f32[512,8]{0,1:T(8,128)S(1)} %is-finite_select_fusion.7, s32[512,8]{0,1:T(8,128)S(1)} %get-tuple-element.476, s32[512,8]{0,1:T(8,128)S(1)} %get-tuple-element.477, s32[512,8]{0,1:T(8,128)S(1)} %get-tuple-element.478, ...), kind=kLoop, calls=%fused_computation.2.clone.1 | loop fusion | flops 260042752 | bytes 33718272 | tf_op jit(solution)/shard_map/while/body/eval_jaxpr/reduce_sum | solution.py:103
  749.1 69.4 %fusion.115 = (f32[8,512]{1,0:T(8,128)S(1)}, f32[8,512,1024]{2,1,0:T(8,128)}) fusion(f32[8]{0:T(128)S(1)} %get-tuple-element.290, pred[512,1024]{1,0:T(8,128)(4,1)} %copy.211, f32[8]{0:T(128)S(1)} %get-tuple-element.291, pred[512,1024]{1,0:T(8,128)(4,1)} %copy.212, f32[8]{0:T(128)S(1)} %copy-done.104, pred[512,1024]{1,0:T(8,128)(4,1)} %copy.213, ...), kind=kOutput, calls=%fused_computation.282 | convolution fusion | flops 1358950400 | bytes 37241856 | tf_op jit(solution)/shard_map/while/body/eval_jaxpr/ihd,chd->hic/dot_general | solution.py:52
  972.4 1117.8 %while.5 = (s32[]{:T(128)}, f32[4,512,8,128]{3,1,2,0:T(8,128)}, s32[4,512,8,1,8]{1,2,4,3,0:T(8,128)}, bf16[4,512,8,128]{3,1,2,0:T(8,128)(2,1)}, bf16[1,2048,8,25...) while((s32[]{:T(128)}, f32[4,512,8,128]{3,1,2,0:T(8,128)}, ...), condition=%wide.region_22.23_spmd, body=%wide.region_17.22_spmd.sunk | while | flops 31333052416 | bytes 420430048 | solution.py:292
  1017.2 49.3 %multiply_reduce_fusion.13 = f32[512,8]{0,1:T(8,128)S(1)} fusion(f32[8,512,2048]{2,1,0:T(8,128)S(1)} %get-tuple-element.503, f32[512,8]{0,1:T(8,128)S(1)} %is-finite_select_fusion.8, s32[512,8]{0,1:T(8,128)S(1)} %get-tuple-element.494, s32[512,8]{0,1:T(8,128)S(1)} %get-tuple-element.495, s32[512,8]{0,1:T(8,128)S(1)} %get-tuple-element.496, ...), kind=kLoop, calls=%fused_computation.53.clone.1 | loop fusion | flops 260042752 | bytes 33718272 | tf_op jit(solution)/shard_map/while/body/eval_jaxpr/reduce_sum | solution.py:103
  1075.8 60.5 %fusion.175 = (f32[512,8]{0,1:T(8,128)S(1)}, f32[8,512,2048]{2,1,0:T(8,128)}) fusion(f32[512,8]{0,1:T(8,128)S(1)} %get-tuple-element.504, f32[8,512,2048]{2,1,0:T(8,128)} %copy-done, s32[512,8]{0,1:T(8,128)S(1)} %get-tuple-element.494, s32[512,8]{0,1:T(8,128)S(1)} %get-tuple-element.495, s32[512,8]{0,1:T(8,128)S(1)} %get-tuple-element.496, ...), kind=kOutput, calls=%fused_computation.46.clone.2 | convolution fusion | flops 13136556032 | bytes 73564160 | tf_op jit(solution)/shard_map/while/body/eval_jaxpr/bhd,shd->bhs/dot_general | solution.py:131
  1185.2 66.9 %bitcast_dynamic-update-slice_fusion.5 = f32[4,512,8,128]{3,1,2,0:T(8,128)} fusion(f32[4,512,8,128]{3,1,2,0:T(8,128)} %get-tuple-element.539, s32[]{:T(128)S(6)} %copy.206, f32[8,512,2048]{2,1,0:T(8,128)} %get-tuple-element.505, f32[512,8]{0,1:T(8,128)S(1)} %bitcast_subtract_fusion.5, f32[512,8]{0,1:T(8,128)S(1)} %get-tuple-element.506, ...), kind=kOutput, calls=%fused_computation.80.clone.3 | convolution fusion | flops 13153861632 | bytes 73596928 | tf_op jit(solution)/shard_map/while/body/eval_jaxpr/bhs,shd->bhd/dot_general | solution.py:139
  1296.5 49.3 %multiply_reduce_fusion.13 = f32[512,8]{0,1:T(8,128)S(1)} fusion(f32[8,512,2048]{2,1,0:T(8,128)S(1)} %get-tuple-element.503, f32[512,8]{0,1:T(8,128)S(1)} %is-finite_select_fusion.8, s32[512,8]{0,1:T(8,128)S(1)} %get-tuple-element.494, s32[512,8]{0,1:T(8,128)S(1)} %get-tuple-element.495, s32[512,8]{0,1:T(8,128)S(1)} %get-tuple-element.496, ...), kind=kLoop, calls=%fused_computation.53.clone.1 | loop fusion | flops 260042752 | bytes 33718272 | tf_op jit(solution)/shard_map/while/body/eval_jaxpr/reduce_sum | solution.py:103
  1355.1 60.5 %fusion.175 = (f32[512,8]{0,1:T(8,128)S(1)}, f32[8,512,2048]{2,1,0:T(8,128)}) fusion(f32[512,8]{0,1:T(8,128)S(1)} %get-tuple-element.504, f32[8,512,2048]{2,1,0:T(8,128)} %copy-done, s32[512,8]{0,1:T(8,128)S(1)} %get-tuple-element.494, s32[512,8]{0,1:T(8,128)S(1)} %get-tuple-element.495, s32[512,8]{0,1:T(8,128)S(1)} %get-tuple-element.496, ...), kind=kOutput, calls=%fused_computation.46.clone.2 | convolution fusion | flops 13136556032 | bytes 73564160 | tf_op jit(solution)/shard_map/while/body/eval_jaxpr/bhd,shd->bhs/dot_general | solution.py:131
  1464.5 66.9 %bitcast_dynamic-update-slice_fusion.5 = f32[4,512,8,128]{3,1,2,0:T(8,128)} fusion(f32[4,512,8,128]{3,1,2,0:T(8,128)} %get-tuple-element.539, s32[]{:T(128)S(6)} %copy.206, f32[8,512,2048]{2,1,0:T(8,128)} %get-tuple-element.505, f32[512,8]{0,1:T(8,128)S(1)} %bitcast_subtract_fusion.5, f32[512,8]{0,1:T(8,128)S(1)} %get-tuple-element.506, ...), kind=kOutput, calls=%fused_computation.80.clone.3 | convolution fusion | flops 13153861632 | bytes 73596928 | tf_op jit(solution)/shard_map/while/body/eval_jaxpr/bhs,shd->bhd/dot_general | solution.py:139
  1575.9 49.3 %multiply_reduce_fusion.13 = f32[512,8]{0,1:T(8,128)S(1)} fusion(f32[8,512,2048]{2,1,0:T(8,128)S(1)} %get-tuple-element.503, f32[512,8]{0,1:T(8,128)S(1)} %is-finite_select_fusion.8, s32[512,8]{0,1:T(8,128)S(1)} %get-tuple-element.494, s32[512,8]{0,1:T(8,128)S(1)} %get-tuple-element.495, s32[512,8]{0,1:T(8,128)S(1)} %get-tuple-element.496, ...), kind=kLoop, calls=%fused_computation.53.clone.1 | loop fusion | flops 260042752 | bytes 33718272 | tf_op jit(solution)/shard_map/while/body/eval_jaxpr/reduce_sum | solution.py:103
  1634.4 60.5 %fusion.175 = (f32[512,8]{0,1:T(8,128)S(1)}, f32[8,512,2048]{2,1,0:T(8,128)}) fusion(f32[512,8]{0,1:T(8,128)S(1)} %get-tuple-element.504, f32[8,512,2048]{2,1,0:T(8,128)} %copy-done, s32[512,8]{0,1:T(8,128)S(1)} %get-tuple-element.494, s32[512,8]{0,1:T(8,128)S(1)} %get-tuple-element.495, s32[512,8]{0,1:T(8,128)S(1)} %get-tuple-element.496, ...), kind=kOutput, calls=%fused_computation.46.clone.2 | convolution fusion | flops 13136556032 | bytes 73564160 | tf_op jit(solution)/shard_map/while/body/eval_jaxpr/bhd,shd->bhs/dot_general | solution.py:131
  1743.8 66.9 %bitcast_dynamic-update-slice_fusion.5 = f32[4,512,8,128]{3,1,2,0:T(8,128)} fusion(f32[4,512,8,128]{3,1,2,0:T(8,128)} %get-tuple-element.539, s32[]{:T(128)S(6)} %copy.206, f32[8,512,2048]{2,1,0:T(8,128)} %get-tuple-element.505, f32[512,8]{0,1:T(8,128)S(1)} %bitcast_subtract_fusion.5, f32[512,8]{0,1:T(8,128)S(1)} %get-tuple-element.506, ...), kind=kOutput, calls=%fused_computation.80.clone.3 | convolution fusion | flops 13153861632 | bytes 73596928 | tf_op jit(solution)/shard_map/while/body/eval_jaxpr/bhs,shd->bhd/dot_general | solution.py:139
  1855.2 49.3 %multiply_reduce_fusion.13 = f32[512,8]{0,1:T(8,128)S(1)} fusion(f32[8,512,2048]{2,1,0:T(8,128)S(1)} %get-tuple-element.503, f32[512,8]{0,1:T(8,128)S(1)} %is-finite_select_fusion.8, s32[512,8]{0,1:T(8,128)S(1)} %get-tuple-element.494, s32[512,8]{0,1:T(8,128)S(1)} %get-tuple-element.495, s32[512,8]{0,1:T(8,128)S(1)} %get-tuple-element.496, ...), kind=kLoop, calls=%fused_computation.53.clone.1 | loop fusion | flops 260042752 | bytes 33718272 | tf_op jit(solution)/shard_map/while/body/eval_jaxpr/reduce_sum | solution.py:103
  1913.7 60.5 %fusion.175 = (f32[512,8]{0,1:T(8,128)S(1)}, f32[8,512,2048]{2,1,0:T(8,128)}) fusion(f32[512,8]{0,1:T(8,128)S(1)} %get-tuple-element.504, f32[8,512,2048]{2,1,0:T(8,128)} %copy-done, s32[512,8]{0,1:T(8,128)S(1)} %get-tuple-element.494, s32[512,8]{0,1:T(8,128)S(1)} %get-tuple-element.495, s32[512,8]{0,1:T(8,128)S(1)} %get-tuple-element.496, ...), kind=kOutput, calls=%fused_computation.46.clone.2 | convolution fusion | flops 13136556032 | bytes 73564160 | tf_op jit(solution)/shard_map/while/body/eval_jaxpr/bhd,shd->bhs/dot_general | solution.py:131
  2023.1 66.9 %bitcast_dynamic-update-slice_fusion.5 = f32[4,512,8,128]{3,1,2,0:T(8,128)} fusion(f32[4,512,8,128]{3,1,2,0:T(8,128)} %get-tuple-element.539, s32[]{:T(128)S(6)} %copy.206, f32[8,512,2048]{2,1,0:T(8,128)} %get-tuple-element.505, f32[512,8]{0,1:T(8,128)S(1)} %bitcast_subtract_fusion.5, f32[512,8]{0,1:T(8,128)S(1)} %get-tuple-element.506, ...), kind=kOutput, calls=%fused_computation.80.clone.3 | convolution fusion | flops 13153861632 | bytes 73596928 | tf_op jit(solution)/shard_map/while/body/eval_jaxpr/bhs,shd->bhd/dot_general | solution.py:139
  2349.7 130.9 %reduce-scatter.21.cloned.1.call-done = f32[32,2]{1,0:T(8,128)} async-done(((f32[1024,2]{1,0:T(8,128)}), f32[32,2]{1,0:T(8,128)}) %reduce-scatter.21.cloned.1.call-update) | async-done | bytes 272
  2481.9 138.4 %reduce-scatter.13.cloned.1.call-done = f32[32,1024]{1,0:T(8,128)} async-done(((f32[1024,1024]{1,0:T(8,128)}), f32[32,1024]{1,0:T(8,128)}) %reduce-scatter.13.cloned.1.call-update) | async-done | bytes 131088 | tf_op jit(solution)/shard_map/reduce_scatter | solution.py:359
  2620.3 181.6 %reduce-scatter.15.cloned.1.call-done = f32[32,4096]{1,0:T(8,128)} async-done(((f32[1024,4096]{1,0:T(8,128)}), f32[32,4096]{1,0:T(8,128)}) %reduce-scatter.15.cloned.1.call-update) | async-done | bytes 524304 | tf_op jit(solution)/shard_map/reduce_scatter | solution.py:360
  2801.9 187.4 %reduce-scatter.17.cloned.1.call-done = f32[128,1024]{1,0:T(8,128)} async-done(((f32[4096,1024]{1,0:T(8,128)}), f32[128,1024]{1,0:T(8,128)}) %reduce-scatter.17.cloned.1.call-update) | async-done | bytes 524304 | tf_op jit(solution)/shard_map/reduce_scatter | solution.py:361
  2989.3 163.9 %reduce-scatter.11.cloned.1.call-done = f32[32,3072]{1,0:T(8,128)} async-done(((f32[1024,3072]{1,0:T(8,128)}), f32[32,3072]{1,0:T(8,128)}) %reduce-scatter.11.cloned.1.call-update) | async-done | bytes 393232 | tf_op jit(solution)/shard_map/reduce_scatter | solution.py:358
  (531 shorter events, 1366.2 us)
Async XLA Ops:
  7.2 85.3 %all-gather.9.cloned.1.call-start = ((), (), s32[]{:S(2)}) async-start(), calls=%async_computation.9 | async-start | bytes 6488064 | tf_op jit(solution)/shard_map/all_gather | solution.py:173
  7.9 126.6 %all-gather.11.cloned.1.call-start = ((), (), s32[]{:S(2)}) async-start(), calls=%async_computation.10 | async-start | bytes 5242880 | tf_op jit(solution)/shard_map/all_gather | solution.py:221
  102.3 732.6 %all-gather.17.cloned.1.call-start = ((), (), s32[]{:S(2)}) async-start(), calls=%async_computation.13 | async-start | bytes 8650752 | tf_op jit(solution)/shard_map/all_gather | solution.py:176
  103.0 760.2 %all-gather.13.cloned.1.call-start = ((), (), s32[]{:S(2)}) async-start(), calls=%async_computation.11 | async-start | bytes 2162688 | tf_op jit(solution)/shard_map/all_gather | solution.py:174
  103.6 764.6 %all-gather.15.cloned.1.call-start = ((), (), s32[]{:S(2)}) async-start(), calls=%async_computation.12 | async-start | bytes 8650752 | tf_op jit(solution)/shard_map/all_gather | solution.py:175
  139.7 556.0 %copy-start.21 = (f32[32,8]{0,1:T(8,128)S(1)}, f32[32,8]{0,1:T(8,128)}, u32[]{:S(2)}) copy-start(f32[32,8]{0,1:T(8,128)} %param.26) | copy-start | bytes 3076
  139.7 567.0 %copy-start.73 = (pred[512,1024]{1,0:T(32,128)(4,1)S(1)}, pred[512,1024]{1,0:T(32,128)(4,1)}, u32[]{:S(2)}) copy-start(pred[512,1024]{1,0:T(32,128)(4,1)} %constant.247) | copy-start | bytes 1572868
  139.7 568.0 %copy-start.72 = (pred[512,1024]{1,0:T(32,128)(4,1)S(1)}, pred[512,1024]{1,0:T(32,128)(4,1)}, u32[]{:S(2)}) copy-start(pred[512,1024]{1,0:T(32,128)(4,1)} %constant.246) | copy-start | bytes 1572868
  692.3 50.1 %all-to-all-start = ((f32[4,512,8]{1,2,0:T(8,128)}), f32[4,512,8]{1,2,0:T(8,128)S(1)}, u32[]{:S(2)}, u32[]{:S(2)}) async-start(f32[4,512,8]{1,2,0:T(8,128)} %bitcast.48), calls=%async_computation | async-start | bytes 131072 | tf_op jit(solution)/shard_map/all_to_all | solution.py:238
  743.1 102.1 %all-to-all-start.1 = ((f32[4,512,8,128]{3,1,2,0:T(8,128)}), f32[4,512,8,128]{3,1,2,0:T(8,128)}, u32[]{:S(2)}, u32[]{:S(2)}) async-start(f32[4,512,8,128]{3,1,2,0:T(8,128)} %bitcast.413), calls=%async_computation.1 | async-start | bytes 16777216 | tf_op jit(solution)/shard_map/all_to_all | solution.py:237
  748.9 212.8 %all-gather.19.cloned.1.call-start = ((), (), s32[]{:S(2)}) async-start(), calls=%async_computation.14 | async-start | bytes 10485760 | tf_op jit(solution)/shard_map/all_gather | solution.py:288
  749.1 69.4 %copy-start.22 = (bf16[512,1024]{1,0:T(8,128)(2,1)S(1)}, bf16[512,1024]{1,0:T(8,128)(2,1)}, u32[]{:S(2)}) copy-start(bf16[512,1024]{1,0:T(8,128)(2,1)} %get-tuple-element.351) | copy-start | bytes 3145732
  830.5 82.4 %copy-start.77 = (f32[8,512]{1,0:T(8,128)}, f32[8,512]{1,0:T(8,128)S(1)}, u32[]{:S(2)}) copy-start(f32[8,512]{1,0:T(8,128)S(1)} %log_add_fusion) | copy-start | bytes 49156
  972.8 93.8 %copy-start.75 = (f32[4,512,8]{1,2,0:T(8,128)}, f32[4,512,8]{1,2,0:T(8,128)S(1)}, u32[]{:S(2)}) copy-start(f32[4,512,8]{1,2,0:T(8,128)S(1)} %get-tuple-element.552) | copy-start | bytes 196612 | tf_op jit(solution)/shard_map/while
  1252.1 93.8 %copy-start.75 = (f32[4,512,8]{1,2,0:T(8,128)}, f32[4,512,8]{1,2,0:T(8,128)S(1)}, u32[]{:S(2)}) copy-start(f32[4,512,8]{1,2,0:T(8,128)S(1)} %get-tuple-element.552) | copy-start | bytes 196612 | tf_op jit(solution)/shard_map/while
  1531.4 93.8 %copy-start.75 = (f32[4,512,8]{1,2,0:T(8,128)}, f32[4,512,8]{1,2,0:T(8,128)S(1)}, u32[]{:S(2)}) copy-start(f32[4,512,8]{1,2,0:T(8,128)S(1)} %get-tuple-element.552) | copy-start | bytes 196612 | tf_op jit(solution)/shard_map/while
  1810.7 93.8 %copy-start.75 = (f32[4,512,8]{1,2,0:T(8,128)}, f32[4,512,8]{1,2,0:T(8,128)S(1)}, u32[]{:S(2)}) copy-start(f32[4,512,8]{1,2,0:T(8,128)S(1)} %get-tuple-element.552) | copy-start | bytes 196612 | tf_op jit(solution)/shard_map/while
  2090.3 99.1 %all-to-all-start.2 = ((f32[4,512,8,128]{3,1,2,0:T(8,128)}), f32[4,512,8,128]{3,1,2,0:T(8,128)}, u32[]{:S(2)}, u32[]{:S(2)}) async-start(f32[4,512,8,128]{3,1,2,0:T(8,128)} %get-tuple-element.147), calls=%async_computation.2 | async-start | bytes 16777216 | tf_op jit(solution)/shard_map/all_to_all | solution.py:302
  2096.2 252.1 %reduce-scatter.19.cloned.1.call-start = ((), (), s32[]{:S(2)}) async-start(), calls=%async_computation.19 | async-start | bytes 540672
  2214.0 266.6 %reduce-scatter.21.cloned.1.call-start = ((), (), s32[]{:S(2)}) async-start(), calls=%async_computation.20 | async-start | bytes 540672
  2215.1 405.2 %reduce-scatter.13.cloned.1.call-start = ((), (), s32[]{:S(2)}) async-start(), calls=%async_computation.16 | async-start | bytes 4325376 | tf_op jit(solution)/shard_map/reduce_scatter | solution.py:359
  2220.3 581.6 %reduce-scatter.15.cloned.1.call-start = ((), (), s32[]{:S(2)}) async-start(), calls=%async_computation.17 | async-start | bytes 17301504 | tf_op jit(solution)/shard_map/reduce_scatter | solution.py:360
  2230.9 758.4 %reduce-scatter.17.cloned.1.call-start = ((), (), s32[]{:S(2)}) async-start(), calls=%async_computation.18 | async-start | bytes 17301504 | tf_op jit(solution)/shard_map/reduce_scatter | solution.py:361
  2246.4 906.8 %reduce-scatter.11.cloned.1.call-start = ((), (), s32[]{:S(2)}) async-start(), calls=%async_computation.15 | async-start | bytes 12976128 | tf_op jit(solution)/shard_map/reduce_scatter | solution.py:358
  (128 other events, 2313.8 us)
Sparse Core Ops, SparseCore 0:
  10.9 72.2 all-gather.8
  102.4 32.0 all-gather.10
  137.4 77.5 all-gather.16
  217.7 55.0 all-gather.12
  275.5 76.2 all-gather.14
  901.8 59.7 all-gather.18
  2214.1 134.2 reduce-scatter.18
  2350.6 129.8 reduce-scatter.20
  2483.4 136.8 reduce-scatter.12
  2623.0 178.8 reduce-scatter.14
  2804.7 184.4 reduce-scatter.16
  2995.7 157.4 reduce-scatter.10
where the time goes:
time: 3170 us; the launch traced here: 3160 us
  matrix products  1430 us (45%)
  waiting for transfers between devices  894 us (28%)
  other arithmetic  518 us (16%)
  local copies, waits for them, and re-layouts  153 us (5%)
  blocking collectives  131 us (4%)
    reduce_sum x8, other arithmetic, part_scores(): part_lse = jax.nn.logsumexp(scores, axis=-1, b=counts)  395 us
    dot_general x8, matrix products, part_scores(): jnp.einsum('bhd,shd->bhs', query_heads, keys_part, preferred_element_type...  347 us
    dot_general x4, matrix products, recall_grad(): jnp.einsum('bhs,shd->bhd', grad_scores, keys_part.astype(jnp.float32), pr...  268 us
    dot_general x4, matrix products, recall_grad(): jnp.einsum('bhd,shd->bhs', grad_recalled, values_part.astype(jnp.float32)...  242 us
    reduce_scatter x1, waiting for transfers between devices, local(): lax.psum_scatter(grad_down, ('dp', 'mem'), scatter_dimension=0, tiled=True)  187 us
    dot_general x4, matrix products, recall_grad(): jnp.einsum('bhs,shd->bhd', probs.astype(jnp.bfloat16), values_part, prefe...  183 us
    reduce_scatter x1, waiting for transfers between devices, local(): lax.psum_scatter(grad_up, ('dp', 'mem'), scatter_dimension=0, tiled=True)  182 us
    dot_general x4, matrix products, recall_parts(): jnp.einsum('bhs,shd->bhd', probs.astype(jnp.bfloat16), table_parts[0, :,...  178 us
  transfers between devices with their start and end apart: 15, of which 9 were waited for; matrix products, arithmetic and copies ran while one was open for 28% of the time, Pallas kernels for 0%

commit v1 on v0

v1 whole, which is shorter than its diff:
```python
import functools

import jax
import jax.numpy as jnp
import numpy as np
from jax import lax
from jax.experimental import pallas as pl
from jax.experimental.pallas import tpu as pltpu
from jax.sharding import PartitionSpec as P

H = 8
HD = 128
W = 512
BUCKETS = 32
NEAR = 128
EPSILON = 1e-05
NEGATIVE = -1e30
SCALE = HD ** (-0.5)
AXES = ("dp", "mem")
MESH = pl.DeviceIdType.MESH
HIGHEST = lax.Precision.HIGHEST
BF = jnp.bfloat16
F32 = jnp.float32
NT = (((1,), (1,)), ((), ()))
NN = (((1,), (0,)), ((), ()))


def dot(left, right, dims=NN):
    return lax.dot_general(left, right, dims, preferred_element_type=F32)


def gather_kernel(n_hi, orders, *refs):
    n = len(orders)
    ins, outs = refs[:n], refs[n : 2 * n]
    send_sem, recv_sem, local_sem = refs[2 * n :]
    dp, mem = lax.axis_index("dp"), lax.axis_index("mem")
    hi, lo = dp // 2, dp % 2
    x_at, core_at = mem // 2, mem % 2
    sizes = (n_hi, 2, 2, 2)
    own, along_y, along_x, along_core = (0, 0, 0, 0), (0, 1, 0, 0), (0, 0, 1, 0), (0, 0, 0, 1)

    def device(step):
        z = lax.rem(hi + step[0], n_hi)
        return (z * 2 + (lo + step[1]) % 2, (x_at + step[2]) % 2 * 2 + (core_at + step[3]) % 2)

    def plus(left, right):
        return tuple((a + b) % k for a, b, k in zip(left, right, sizes))

    def minus(left, right):
        return tuple((a - b) % k for a, b, k in zip(left, right, sizes))

    def number(step):
        return ((step[0] * 2 + step[1]) * 2 + step[2]) * 2 + step[3]

    partners = [(z, 0, 0, 0) for z in range(1, n_hi)] + [along_y, along_x, along_core]
    barrier = pltpu.get_barrier_semaphore()
    for partner in partners:
        pl.semaphore_signal(barrier, inc=1, device_id=device(partner), device_id_type=MESH)
    pl.semaphore_wait(barrier, len(partners))

    def place(a, source):
        d, m = device(source)
        rows = ins[a].shape[0]
        return outs[a].at[pl.ds(pl.multiple_of((d * 4 + m) * rows, rows), rows)]

    started = []
    counts = [0] * n

    def send(a, source, to):
        copy = pltpu.make_async_remote_copy(
            src_ref=ins[a] if source == own else place(a, source),
            dst_ref=place(a, source),
            send_sem=send_sem.at[a, counts[a]],
            recv_sem=recv_sem.at[a, number(minus(source, to))],
            device_id=device(to),
            device_id_type=MESH,
        )
        counts[a] += 1
        copy.start()
        started.append(copy)

    def arrived(a, source):
        ref = place(a, source)
        pltpu.make_async_remote_copy(
            src_ref=ref,
            dst_ref=ref,
            send_sem=send_sem.at[a, 0],
            recv_sem=recv_sem.at[a, number(source)],
            device_id=device(along_core),
            device_id_type=MESH,
        ).wait_recv()

    first = [along_y if order == "zyx" else along_x for order in orders]
    second = [along_x if order == "zyx" else along_y for order in orders]
    for a in range(n):
        for z in range(1, n_hi):
            send(a, own, (z, 0, 0, 0))
        send(a, own, along_y)
        send(a, own, along_x)
    kept = []
    for a in range(n):
        send(a, own, along_core)
        copy = pltpu.make_async_copy(ins[a], place(a, own), local_sem.at[a])
        copy.start()
        kept.append(copy)
    near_first = [0]
    for z in range(1, n_hi // 2 + 1):
        near_first += [k for k in dict.fromkeys((z, n_hi - z)) if k < n_hi]
    for z in near_first:
        at = (z, 0, 0, 0)
        if z:
            for a in range(n):
                arrived(a, at)
                for to in (first[a], second[a], along_core):
                    send(a, at, to)
        for a in range(n):
            source = plus(at, first[a])
            arrived(a, source)
            for to in (second[a], along_core):
                send(a, source, to)
    for z in near_first:
        for a in range(n):
            for source in (second[a], plus(first[a], second[a])):
                source = plus((z, 0, 0, 0), source)
                arrived(a, source)
                send(a, source, along_core)
    for z in near_first:
        for y in range(2):
            for x in range(2):
                for a in range(n):
                    arrived(a, (z, y, x, 1))
    for copy in started:
        copy.wait_send()
    for copy in kept:
        copy.wait()


def gather_rows(arrays, orders, collective_id):
    n = len(arrays)
    n_hi = lax.axis_size("dp") // 2
    total = n_hi * 8
    sends = (n_hi - 1) + 3 + (n_hi - 1) * 3 + n_hi * 2 + n_hi * 2
    anywhere = pl.BlockSpec(memory_space=pl.ANY)
    return pl.pallas_call(
        functools.partial(gather_kernel, n_hi, orders),
        out_shape=[
            jax.ShapeDtypeStruct((a.shape[0] * total,) + a.shape[1:], a.dtype) for a in arrays
        ],
        in_specs=[anywhere] * n,
        out_specs=[anywhere] * n,
        scratch_shapes=[
            pltpu.SemaphoreType.DMA((n, sends)),
            pltpu.SemaphoreType.DMA((n, total)),
            pltpu.SemaphoreType.DMA((n,)),
        ],
        compiler_params=pltpu.CompilerParams(collective_id=collective_id, has_side_effects=True),
    )(*arrays)


def recall_kernel(qa_ref, qb_ref, mem_ref, slot_ref, outa_ref, outb_ref, lse_ref, p_ref):
    slots, tokens = p_ref.shape[1], p_ref.shape[2]
    half = tokens // 2
    chosen = slot_ref[0]
    low, high = chosen & 7, chosen >> 3
    queries = jnp.concatenate([qa_ref[...], qb_ref[...]], axis=0)
    step = 256
    picked = jnp.zeros((8, tokens), F32)
    for at in range(0, slots, step):
        scores = dot(mem_ref[0, pl.ds(at, step), pl.ds(0, HD)], queries, NT)
        for row in range(0, step, 8):
            got = jnp.take_along_axis(scores[row : row + 8], low, axis=0)
            picked = jnp.where(high == (at + row) // 8, got, picked)
    scores = picked * SCALE
    top = jnp.max(scores, axis=0, keepdims=True)
    weights = jnp.exp(scores - top)
    total = jnp.sum(weights, axis=0, keepdims=True)
    lse_ref[0] = top + jnp.log(total)
    times = jnp.ones_like(weights)
    for turn in range(1, 8):
        times = times + jnp.where(pltpu.roll(chosen, turn, 0) == chosen, 1.0, 0.0)
    probs = (weights / total * times).astype(BF)
    rows = lax.broadcasted_iota(jnp.int32, (step, tokens), 0).astype(F32).astype(BF)
    out = jnp.zeros((HD, tokens), F32)
    values_t = mem_ref[0, :, pl.ds(HD, HD)].T
    for at in range(0, slots, step):
        mine = jnp.where(chosen // step == at // step, chosen % step, -1).astype(F32).astype(BF)
        dense = jnp.zeros((step, tokens), BF)
        for j in range(8):
            dense = jnp.where(rows == mine[j : j + 1], probs[j : j + 1], dense)
        p_ref[0, pl.ds(at, step), :] = dense
        out = out + dot(values_t[:, at : at + step], dense)
    out = out.T.astype(BF)
    outa_ref[...] = out[:half]
    outb_ref[...] = out[half:]


def recall_grad_kernel(ga_ref, gb_ref, mem_ref, p_ref, delta_ref, share_ref, outa_ref, outb_ref):
    slots, tokens = p_ref.shape[1], p_ref.shape[2]
    half = tokens // 2
    grads = jnp.concatenate([ga_ref[...], gb_ref[...]], axis=0)
    delta = delta_ref[0]
    keys_t = mem_ref[0, :, pl.ds(0, HD)].T
    step = 512
    out = jnp.zeros((HD, tokens), F32)
    for at in range(0, slots, step):
        along = dot(mem_ref[0, pl.ds(at, step), pl.ds(HD, HD)], grads, NT)
        scores = (along - delta).astype(BF) * p_ref[0, pl.ds(at, step), :]
        out = out + dot(keys_t[:, at : at + step], scores)
    out = (out * (share_ref[0] * SCALE)).T.astype(BF)
    outa_ref[...] = out[:half]
    outb_ref[...] = out[half:]


def head_columns(rows, first=0):
    return pl.BlockSpec((rows, HD), lambda h: (0, first + h))


def per_head(*shape):
    return pl.BlockSpec((1,) + shape, lambda h: (h,) + (0,) * len(shape))


def recall(query_a, query_b, table, chosen):
    rows, slots = query_a.shape[0], table.shape[1]
    return pl.pallas_call(
        recall_kernel,
        grid=(H,),
        in_specs=[
            head_columns(rows),
            head_columns(rows),
            per_head(slots, 2 * HD),
            per_head(8, 2 * rows),
        ],
        out_specs=[
            head_columns(rows),
            head_columns(rows),
            per_head(1, 2 * rows),
            per_head(slots, 2 * rows),
        ],
        out_shape=[
            jax.ShapeDtypeStruct(query_a.shape, BF),
            jax.ShapeDtypeStruct(query_a.shape, BF),
            jax.ShapeDtypeStruct((H, 1, 2 * rows), F32),
            jax.ShapeDtypeStruct((H, slots, 2 * rows), BF),
        ],
        compiler_params=pltpu.CompilerParams(vmem_limit_bytes=48 << 20),
        cost_estimate=pl.CostEstimate(
            flops=8 * rows * slots * HD * H, bytes_accessed=64 << 20, transcendentals=0
        ),
    )(query_a, query_b, table, chosen)


def recall_grad(grad_a, grad_b, table, probs, delta, share):
    rows, slots = grad_a.shape[0], table.shape[1]
    return pl.pallas_call(
        recall_grad_kernel,
        grid=(H,),
        in_specs=[
            head_columns(rows),
            head_columns(rows),
            per_head(slots, 2 * HD),
            per_head(slots, 2 * rows),
            per_head(1, 2 * rows),
            per_head(1, 2 * rows),
        ],
        out_specs=[head_columns(rows), head_columns(rows)],
        out_shape=[jax.ShapeDtypeStruct(grad_a.shape, BF)] * 2,
        compiler_params=pltpu.CompilerParams(vmem_limit_bytes=48 << 20),
        cost_estimate=pl.CostEstimate(
            flops=8 * rows * slots * HD * H, bytes_accessed=64 << 20, transcendentals=0
        ),
    )(grad_a, grad_b, table, probs, delta, share)


def near_buckets():
    distance = np.arange(NEAR)
    exact = BUCKETS // 2
    far = exact + np.floor(
        np.log(np.maximum(distance, 1) / exact) / np.log(128.0 / exact) * exact
    )
    return np.where(distance < exact, distance, np.minimum(far, BUCKETS - 1)).astype(np.int32)


def near_hot():
    return near_buckets()[:, None] == np.arange(BUCKETS)[None, :]


def near_bias(rel_table):
    above = (rel_table - rel_table[-1:])[None]
    rows = jnp.sum(jnp.where(jnp.asarray(near_hot())[:, :, None], above, 0.0), axis=1)
    return jnp.pad(rows.T, ((0, 0), (0, NEAR)))[:, None, :]


def table_gradient(diagonals, totals):
    near = diagonals[:, 0, NEAR - 1 : 2 * NEAR - 1]
    sums = jnp.dot(near, jnp.asarray(near_hot(), F32), precision=HIGHEST)
    far = jnp.sum(totals, axis=(1, 2)) - jnp.sum(near, axis=1)
    return (sums + far[:, None] * (np.arange(BUCKETS) == BUCKETS - 1)).T


def segment_kernel(len_ref, near_ref, q_ref, kc_ref, kn_ref, vc_ref, vn_ref, out_ref, p_ref):
    length = len_ref[0]
    band = pltpu.roll(
        jnp.broadcast_to(near_ref[0], (NEAR, 2 * NEAR)), 0, 1, stride=1, stride_axis=0
    )
    key_ids = lax.broadcasted_iota(jnp.int32, (NEAR, NEAR), 0)
    query_ids = lax.broadcasted_iota(jnp.int32, (NEAR, NEAR), 1)
    on_diagonal = jnp.where(query_ids >= key_ids, band[:, :NEAR], NEGATIVE)
    beside = band[:, NEAR:]
    masked = jnp.full((NEAR, NEAR), NEGATIVE, F32)
    zero = jnp.zeros((NEAR, NEAR), F32)
    cache_t, values_t = vc_ref[...].T, vn_ref[...].T
    step = 2 * NEAR
    for at in range(W // step):
        count = 2 * (at + 1)
        queries = q_ref[pl.ds(step * at, step), :]
        cached = dot(kc_ref[...], queries, NT) * SCALE
        if at == 0:
            last = cached[W - NEAR :] + jnp.concatenate([beside, zero], axis=1)
            cached = jnp.concatenate([cached[: W - NEAR], last], axis=0)
        fresh = dot(kn_ref[pl.ds(0, NEAR * count), :], queries, NT) * SCALE
        rows = [cached]
        for k in range(count):
            block = fresh[NEAR * k : NEAR * (k + 1)]
            tiles = [
                masked if q < k else on_diagonal if q == k else beside if q == k + 1 else zero
                for q in (2 * at, 2 * at + 1)
            ]
            if any(tile is not zero for tile in tiles):
                block = block + jnp.concatenate(tiles, axis=1)
            ids = lax.broadcasted_iota(jnp.int32, (NEAR, step), 0) + NEAR * k
            rows.append(jnp.where(ids < length, block, NEGATIVE))
        scores = jnp.concatenate(rows, axis=0)
        weights = jnp.exp(scores - jnp.max(scores, axis=0, keepdims=True))
        probs = (weights * (1.0 / jnp.sum(weights, axis=0, keepdims=True))).astype(BF)
        p_ref[0, pl.ds(0, W + NEAR * count), pl.ds(step * at, step)] = probs
        out = dot(cache_t, probs[:W]) + dot(values_t[:, : NEAR * count], probs[W:])
        out_ref[pl.ds(step * at, step), :] = out.T


def segment_grad_kernel(
    open_ref, g_ref, q_ref, kc_ref, kn_ref, vc_ref, vn_ref, p_ref, gq_ref, gk_ref, gv_ref, diag_ref, tot_ref
):
    closed = 1.0 - open_ref[pl.program_id(0)]
    cache_t, keys_t = kc_ref[...].T, kn_ref[...].T
    on_diagonal = jnp.zeros((NEAR, NEAR), F32)
    beside = jnp.zeros((NEAR, NEAR), F32)
    step = 2 * NEAR
    total = jnp.zeros((8, step), F32)
    grad_keys, grad_values = [], []
    for at in range(W // step):
        count = 2 * (at + 1)
        grads = (closed * g_ref[pl.ds(step * at, step), :]).astype(BF)
        queries = q_ref[pl.ds(step * at, step), :]
        grad_probs = jnp.concatenate(
            [dot(vc_ref[...], grads, NT), dot(vn_ref[pl.ds(0, NEAR * count), :], grads, NT)], axis=0
        )
        probs = p_ref[0, pl.ds(0, W + NEAR * count), pl.ds(step * at, step)]
        wide = probs.astype(F32)
        product = wide * grad_probs
        grad_scores = product - wide * jnp.sum(product, axis=0, keepdims=True)
        low = grad_scores.astype(BF)
        grad_q = dot(cache_t, low[:W]) + dot(keys_t[:, : NEAR * count], low[W:])
        gq_ref[pl.ds(step * at, step), :] = (grad_q * SCALE).T
        grad_keys.append(dot(low[W:], queries) * SCALE)
        grad_values.append(dot(probs[W:], grads))
        if at == 0:
            beside = beside + grad_scores[W - NEAR : W, :NEAR]
        for k in range(count):
            for side, q in enumerate((2 * at, 2 * at + 1)):
                tile = grad_scores[W + NEAR * k : W + NEAR * (k + 1), NEAR * side : NEAR * (side + 1)]
                if q == k:
                    on_diagonal = on_diagonal + tile
                elif q == k + 1:
                    beside = beside + tile
        total = total + jnp.sum(grad_scores.reshape(-1, 8, step), axis=0)
    for ref, (early, late) in ((gk_ref, grad_keys), (gv_ref, grad_values)):
        ref[...] = jnp.concatenate([late[:step] + early, late[step:]], axis=0).astype(BF)
    down = lax.broadcasted_iota(jnp.int32, (NEAR, NEAR), 0)
    across = lax.broadcasted_iota(jnp.int32, (NEAR, NEAR), 1)
    turned = lax.dot_general(
        (down + across == NEAR - 1).astype(F32),
        jnp.concatenate([on_diagonal, beside], axis=1),
        NN,
        precision=HIGHEST,
        preferred_element_type=F32,
    )
    diagonals = pltpu.roll(turned, 0, 1, stride=1, stride_axis=0)
    diag_ref[0] = jnp.sum(diagonals, axis=0, keepdims=True)
    tot_ref[0] = total


SCALARS = pl.BlockSpec(memory_space=pltpu.SMEM)


def segment_forward(queries, keys_values, cache, near, length):
    return pl.pallas_call(
        segment_kernel,
        grid=(H,),
        in_specs=[
            SCALARS,
            per_head(1, 2 * NEAR),
            head_columns(W),
            head_columns(W),
            head_columns(W),
            head_columns(W, H),
            head_columns(W, H),
        ],
        out_specs=[head_columns(W), per_head(2 * W, W)],
        out_shape=[
            jax.ShapeDtypeStruct((W, H * HD), F32),
            jax.ShapeDtypeStruct((H, 2 * W, W), BF),
        ],
        compiler_params=pltpu.CompilerParams(vmem_limit_bytes=32 << 20),
        cost_estimate=pl.CostEstimate(
            flops=8 * W * W * HD * H, bytes_accessed=20 << 20, transcendentals=0
        ),
    )(length, near, queries, cache, keys_values, cache, keys_values)


def segment_backward(gate_open, grad_mixed, queries, keys_values, cache, probs):
    return pl.pallas_call(
        segment_grad_kernel,
        grid=(H,),
        in_specs=[
            SCALARS,
            head_columns(W),
            head_columns(W),
            head_columns(W),
            head_columns(W),
            head_columns(W, H),
            head_columns(W, H),
            per_head(2 * W, W),
        ],
        out_specs=[
            head_columns(W),
            head_columns(W),
            head_columns(W),
            per_head(1, 2 * NEAR),
            per_head(8, 2 * NEAR),
        ],
        out_shape=[
            jax.ShapeDtypeStruct((W, H * HD), F32),
            jax.ShapeDtypeStruct((W, H * HD), BF),
            jax.ShapeDtypeStruct((W, H * HD), BF),
            jax.ShapeDtypeStruct((H, 1, 2 * NEAR), F32),
            jax.ShapeDtypeStruct((H, 8, 2 * NEAR), F32),
        ],
        compiler_params=pltpu.CompilerParams(vmem_limit_bytes=32 << 20),
        cost_estimate=pl.CostEstimate(
            flops=16 * W * W * HD * H, bytes_accessed=20 << 20, transcendentals=0
        ),
    )(gate_open, grad_mixed, queries, cache, keys_values, cache, keys_values, probs)


def norm_forward(values, gain_row, shift_row):
    center = values - jnp.mean(values, axis=-1, keepdims=True)
    inverse = lax.rsqrt(jnp.mean(center * center, axis=-1, keepdims=True) + EPSILON)
    scaled = center * inverse
    return (scaled * gain_row + shift_row, scaled, inverse)


def norm_backward(grad_normed, scaled, inverse, gain_row):
    grad_scaled = grad_normed * gain_row
    mean_grad = jnp.mean(grad_scaled, axis=-1, keepdims=True)
    mean_cross = jnp.mean(grad_scaled * scaled, axis=-1, keepdims=True)
    return inverse * (grad_scaled - mean_grad - scaled * mean_cross)


def swap(value, turn):
    return jax.tree.map(
        lambda v: lax.ppermute(v, "mem", [(i, i ^ turn) for i in range(lax.axis_size("mem"))]), value
    )


def combine(outs, lses):
    total = jax.nn.logsumexp(jnp.stack(lses), axis=0)
    rows = outs[0].shape[0]
    result = 0.0
    for out, lse in zip(outs, lses):
        share = jnp.exp(lse - total).T[:, :, None]
        result = result + share * out.reshape(rows, H, HD).astype(F32)
    return result.reshape(rows, H * HD), total


def local(
    tokens,
    norm_gains,
    norm_shifts,
    w_qkv,
    w_out,
    w_up,
    w_down,
    rel_table,
    gate_bias,
    xl_cache,
    memory,
    slot_index,
    seg_len,
    cotangent,
):
    width = tokens.shape[1]
    count = tokens.shape[0]
    slot_count = memory.shape[0]
    groups = lax.axis_size("mem")
    me = lax.axis_index("mem")

    norms = jnp.pad(
        jnp.concatenate([norm_gains, norm_shifts], axis=0),
        ((0, 12), (0, 128 - norm_gains.shape[1])),
    )
    full_q, full_norms = gather_rows([w_qkv[:, :width], norms], ("zyx", "zxy"), 0)
    full_kv, full_out, full_up, full_down = gather_rows(
        [w_qkv[:, width:], w_out, w_up, w_down], ("zxy", "zyx", "zyx", "zxy"), 1
    )
    rows = full_norms.reshape(-1, 16, 128)[:, :4, : norm_gains.shape[1]].astype(F32)
    rows = rows.transpose(1, 0, 2).reshape(4, width)
    gain_rows, shift_rows = rows[:2], rows[2:]

    inputs = tokens.astype(F32)
    normed_one, scaled_one, inverse_one = norm_forward(inputs, gain_rows[0], shift_rows[0])
    normed_one = normed_one.astype(BF)
    queries = dot(normed_one, full_q).astype(BF)
    query_core, query_x = swap(queries, 1), swap(queries, 2)
    query_cross = swap(query_x, 1)

    table = memory.transpose(1, 0, 2)
    slot_rows = (slot_index - me * slot_count).reshape(groups, count, H, -1).transpose(0, 2, 3, 1)
    picks = [
        lax.dynamic_index_in_dim(slot_rows, me ^ turn, 0, keepdims=False) for turn in range(groups)
    ]
    out_own, out_core, lse_chip, probs_chip = recall(
        queries, query_core, table, jnp.concatenate(picks[:2], axis=-1)
    )
    out_x, out_cross, lse_far, probs_far = recall(
        query_x, query_cross, table, jnp.concatenate(picks[2:], axis=-1)
    )
    lse_chip, lse_far = lse_chip[:, 0], lse_far[:, 0]
    keys_values = dot(normed_one, full_kv).astype(BF)
    local_out, probs_local = segment_forward(
        queries, keys_values, xl_cache, near_bias(rel_table), seg_len
    )

    own_lse, own_out = lse_chip[:, :count], out_own
    core_out, core_lse = swap((out_core, lse_chip[:, count:]), 1)
    other_out, other_lse = swap((out_cross, lse_far[:, count:]), 1)
    pair_out, pair_lse = combine((out_x, other_out), (lse_far[:, :count], other_lse))
    far_out, far_lse = swap((pair_out.astype(BF), pair_lse), 2)
    recalled, total_lse = combine((own_out, core_out, far_out), (own_lse, core_lse, far_lse))

    gate_open = jax.nn.sigmoid(gate_bias)
    gate_row = jnp.repeat(gate_open, HD)[None]
    mixed_low = (gate_row * recalled + (1.0 - gate_row) * local_out).astype(BF)
    attended = inputs + dot(mixed_low, full_out)
    normed_two, scaled_two, inverse_two = norm_forward(attended, gain_rows[1], shift_rows[1])
    normed_two = normed_two.astype(BF)
    up_pre = dot(normed_two, full_up)
    hidden = jax.nn.gelu(up_pre).astype(BF)
    output = attended + dot(hidden, full_down)

    grad_output = cotangent.astype(F32)
    grad_down = jnp.einsum("tf,td->fd", hidden, cotangent, preferred_element_type=F32)
    grad_hidden = dot(cotangent, full_down, NT)
    grad_up_pre = jax.vjp(jax.nn.gelu, up_pre)[1](grad_hidden)[0].astype(BF)
    grad_up = jnp.einsum("td,tf->df", normed_two, grad_up_pre, preferred_element_type=F32)
    grad_normed_two = dot(grad_up_pre, full_up, NT)
    grad_attended = grad_output + norm_backward(
        grad_normed_two, scaled_two, inverse_two, gain_rows[1]
    )
    attended_low = grad_attended.astype(BF)
    grad_wout = jnp.einsum("td,te->de", mixed_low, attended_low, preferred_element_type=F32)
    grad_mixed = dot(attended_low, full_out, NT)
    grad_gate = (
        jnp.sum((grad_mixed * (recalled - local_out)).reshape(count, H, HD), axis=(0, 2))
        * gate_open
        * (1.0 - gate_open)
    )
    grad_recalled = (gate_row * grad_mixed).astype(BF)
    delta = jnp.sum(
        (grad_recalled.astype(F32) * recalled).reshape(count, H, HD), axis=-1
    ).T
    sent = (grad_recalled, jnp.concatenate([delta, total_lse], axis=0))
    sent_core, sent_x = swap(sent, 1), swap(sent, 2)
    sent_cross = swap(sent_x, 1)

    grad_query_local, grad_keys, grad_values, diagonals, totals = segment_backward(
        gate_open, grad_mixed, queries, keys_values, xl_cache, probs_local
    )
    grad_table = table_gradient(diagonals, totals)

    def recall_back(left, right, lse, probs):
        delta_rows = jnp.concatenate([left[1][:H], right[1][:H]], axis=1)
        total_rows = jnp.concatenate([left[1][H:], right[1][H:]], axis=1)
        return recall_grad(
            left[0],
            right[0],
            table,
            probs,
            delta_rows[:, None],
            jnp.exp(lse - total_rows)[:, None],
        )

    back_x, back_cross = recall_back(sent_x, sent_cross, lse_far, probs_far)
    back_own, back_core = recall_back(sent, sent_core, lse_chip, probs_chip)
    pair_back = (back_x.astype(F32) + swap(back_cross, 1).astype(F32)).astype(BF)
    grad_query = (
        grad_query_local
        + back_own.astype(F32)
        + swap(back_core, 1).astype(F32)
        + swap(pair_back, 2).astype(F32)
    )
    grad_qkv_low = jnp.concatenate([grad_query.astype(BF), grad_keys, grad_values], axis=1)
    grad_wqkv = jnp.einsum("td,te->de", normed_one, grad_qkv_low, preferred_element_type=F32)
    grad_normed_one = dot(grad_qkv_low[:, :width], full_q, NT) + dot(
        grad_qkv_low[:, width:], full_kv, NT
    )
    grad_tokens = grad_attended + norm_backward(
        grad_normed_one, scaled_one, inverse_one, gain_rows[0]
    )
    grad_norms = jnp.stack(
        [
            jnp.sum(grad_normed_one * scaled_one, axis=0),
            jnp.sum(grad_normed_two * scaled_two, axis=0),
            jnp.sum(grad_normed_one, axis=0),
            jnp.sum(grad_normed_two, axis=0),
        ]
    )
    share_qkv, share_out, share_up, share_down = [
        lax.psum_scatter(g.astype(BF), AXES, scatter_dimension=0, tiled=True).astype(F32)
        for g in (grad_wqkv, grad_wout, grad_up, grad_down)
    ]
    share_norms = lax.psum_scatter(grad_norms, AXES, scatter_dimension=1, tiled=True)
    table_total, gate_total = lax.psum((grad_table, grad_gate), AXES)
    return (
        output.astype(BF),
        grad_tokens,
        share_norms[:2],
        share_norms[2:],
        share_qkv,
        share_out,
        share_up,
        share_down,
        table_total,
        gate_total,
    )


def solution(mesh):
    shard = P(AXES, None)
    placed = (
        shard,
        P(None, AXES),
        P(None, AXES),
        shard,
        shard,
        shard,
        shard,
        P(),
        P(),
        shard,
        P(AXES, None, None),
        P("dp", None, "mem"),
        P(AXES),
        shard,
    )
    return jax.shard_map(
        local,
        mesh=mesh,
        in_specs=placed,
        out_specs=(
            shard,
            shard,
            P(None, AXES),
            P(None, AXES),
            shard,
            shard,
            shard,
            shard,
            P(),
            P(),
        ),
        check_vma=False,
    )
```

time: 3170 us -> 1090 us (0.34)
  matrix products: 1430 us -> 99.2 us
  other arithmetic: 518 us -> 33 us
  waiting for transfers between devices: 894 us -> 531 us
  Pallas kernels: 0 us -> 300 us
  local copies, waits for them, and re-layouts: 153 us -> 38.8 us
  blocking collectives: 131 us -> 54.2 us
    dot_general x41 -> x14, matrix products: 1420 us -> 91.5 us  [the longest x10 64.8 us: dot(): return lax.dot_general(left, right, dims, preferred_element_type=F32)]
    reduce_sum x15 -> x7, other arithmetic: 500 us -> 2.81 us  [the longest x1 2.21 us: local(): jnp.sum((grad_recalled.astype(F32) * recalled).reshape(count, H, HD), axi...]
    pallas_call x0 -> x8, Pallas kernels: none -> 300 us  [the longest x2 150 us: gather_rows(): pl.pallas_call(functools.partial(gather_kernel, n_hi, orders), out_shape=...]
    reduce_scatter x4, waiting for transfers between devices: 671 us -> 407 us  [local(): lax.psum_scatter(g.astype(BF), AXES, scatter_dimension=0, tiled=True)]
    all_gather x4 -> x0, blocking collectives: 91.1 us -> none  [the longest x1 43.2 us: local(): lax.all_gather(norm_shifts, ('dp', 'mem'), axis=1, tiled=True)]
    unnamed x14 -> x6, waiting for transfers between devices: 168 us -> 91.8 us
    all_gather x6 -> x0, waiting for transfers between devices: 50.8 us -> none  [the longest x1 35.2 us: local(): lax.all_gather(grad_recalled, 'mem', axis=0, tiled=True)]
    unnamed x282 -> x119, local copies, waits for them, and re-layouts: 66.2 us -> 27.5 us
  transfers between devices with their start and end apart: 15 -> 23, of which waited for: 9 -> 8; matrix products, arithmetic and copies ran while one was open for 28% -> 10% of each run, Pallas kernels for 0% -> 25%
where the time goes in v1:
time: 1090 us; the launch traced here: 1080 us
  waiting for transfers between devices  531 us (49%)
  Pallas kernels  300 us (28%)
  matrix products  99.2 us (9%)
  blocking collectives  54.2 us (5%)
  local copies, waits for them, and re-layouts  38.8 us (4%)
  other arithmetic  33 us (3%)
  between operations  15.7 us (1%)
    reduce_scatter x4, waiting for transfers between devices, local(): lax.psum_scatter(g.astype(BF), AXES, scatter_dimension=0, tiled=True)  407 us
    pallas_call x2, Pallas kernels, gather_rows(): pl.pallas_call(functools.partial(gather_kernel, n_hi, orders), out_shape=...  150 us
    unnamed x6, waiting for transfers between devices  91.8 us
    pallas_call x2, Pallas kernels, recall(): pl.pallas_call(recall_kernel, grid=(H,), in_specs=[head_columns(rows), he...  76.3 us
    dot_general x10, matrix products, dot(): return lax.dot_general(left, right, dims, preferred_element_type=F32)  64.8 us
    psum x1, blocking collectives, local(): table_total, gate_total = lax.psum((grad_table, grad_gate), AXES)  54.2 us
    pallas_call x2, Pallas kernels, recall_grad(): pl.pallas_call(recall_grad_kernel, grid=(H,), in_specs=[head_columns(rows...  43.6 us
    ppermute x18, waiting for transfers between devices, swap(): lax.ppermute(v, 'mem', [(i, i ^ turn) for i in range(lax.axis_size('mem'))])  31.5 us
  transfers between devices with their start and end apart: 23, of which 8 were waited for; matrix products, arithmetic and copies ran while one was open for 10% of the time, Pallas kernels for 25%

profile of v1, /device:TPU:0, one launch (start us, length us, event | category | flops | bytes accessed | tf_op | source)
XLA Modules:
  0.0 1080.6 jit_solution(11658928863537919852)
XLA Ops:
  10.1 29.0 %shard_map.240 = (bf16[1024,1024]{1,0:T(8,128)(2,1)}, bf16[512,128]{1,0:T(8,128)(2,1)}) custom-call(bf16[32,1024]{1,0:T(8,128)(2,1)} %slice.79.refs_0_, bf16[16,128]{1,0:T(8,128)(2,1)} %fusion.51.refs_1_), custom_call_target="tpu_custom_call" | custom-call | tf_op jit(solution)/shard_map/pallas_call | solution.py:144
  48.4 121.0 %shard_map.243 = (bf16[1024,2048]{1,0:T(8,128)(2,1)}, bf16[1024,1024]{1,0:T(8,128)(2,1)}, bf16[1024,4096]{1,0:T(8,128)(2,1)}, bf16[4096,1024]{1,0:T(8,128)(2,1)}) custom-call(bf16[32,2048]{1,0:T(8,128)(2,1)} %slice.88.refs_0_, bf16[32,1024]{1,0:T(8,128)(2,1)} %refs_1_.1, bf16[32,4096]{1,0:T(8,128)(2,1)} %refs_2_.1, bf16[128,1024]{1,0:T(8,128)(2,1)} %refs_3_.1), custom_call_target="tpu_custom_call" | custom-call | tf_op jit(solution)/shard_map/pallas_call | solution.py:144
  169.4 11.6 %fusion.62 = f32[4096,512]{0,1:T(8,128)} fusion(bf16[4096,1024]{1,0:T(8,128)(2,1)} %get-tuple-element.47, bf16[512,1024]{1,0:T(8,128)(2,1)} %param.30), kind=kOutput, calls=%fused_computation.153 | convolution fusion | flops 4294967296 | bytes 17825792 | tf_op jit(solution)/shard_map/dot_general | solution.py:29
  185.6 8.6 copy.126
  194.2 38.0 %shard_map.242 = (bf16[512,1024]{1,0:T(8,128)(2,1)S(1)}, bf16[512,1024]{1,0:T(8,128)(2,1)}, f32[8,1,1024]{2,1,0:T(1,128)S(1)}, bf16[8,2048,1024]{2,1,0:T(8,128)(2,1)}) custom-call(bf16[512,1024]{1,0:T(8,128)(2,1)} %collective-permute-done.2.qa_ref, bf16[512,1024]{1,0:T(8,128)(2,1)} %collective-permute-done.3.qb_ref, bf16[8,2048,256]{2,1,0:T(8,128)(2,1)} %bitcast.140, ...), custom_call_target="tpu_custom_call" | custom-call | flops 8589934592 | bytes 67108864 | tf_op jit(solution)/shard_map/pallas_call | solution.py:224
  232.8 38.3 %shard_map.241 = (bf16[512,1024]{1,0:T(8,128)(2,1)S(1)}, bf16[512,1024]{1,0:T(8,128)(2,1)}, f32[8,1,1024]{2,1,0:T(1,128)S(1)}, bf16[8,2048,1024]{2,1,0:T(8,128)(2,1)}) custom-call(bf16[512,1024]{1,0:T(8,128)(2,1)S(1)} %convolution_convert_fusion.5.qa_ref.q_ref, bf16[512,1024]{1,0:T(8,128)(2,1)S(1)} %collective-permute-done.qb_ref, ...), custom_call_target="tpu_custom_call" | custom-call | flops 8589934592 | bytes 67108864 | tf_op jit(solution)/shard_map/pallas_call | solution.py:224
  280.8 14.1 %shard_map.244 = (f32[512,1024]{1,0:T(8,128)S(1)}, bf16[8,1024,512]{2,1,0:T(8,128)(2,1)S(1)}) custom-call(s32[1]{0:T(128)S(6)} %copy.129.len_ref, f32[8,1,256]{2,1,0:T(1,128)S(1)} %broadcast_in_dim.32.near_ref, bf16[512,1024]{1,0:T(8,128)(2,1)S(1)} %convolution_convert_fusion.5.qa_ref.q_ref, bf16[512,2048]{1,0:T(8,128)(2,1)S(1)} %copy-done, ...), custom_call_target="tpu_custom_call" | custom-call | flops 2147483648 | bytes 20971520 | tf_op jit(solution)/shard_map/pallas_call | solution.py:396
  316.9 15.1 %fusion.6 = (bf16[512,4096]{1,0:T(8,128)(2,1)}, f32[512,4096]{1,0:T(8,128)}) fusion(f32[4096,512]{0,1:T(8,128)} %fusion.62, bf16[1024,4096]{1,0:T(8,128)(2,1)S(1)} %bitcast.173, f32[512,1024]{1,0:T(8,128)S(1)} %get-tuple-element.104, f32[1024]{0:T(1024)S(1)} %copy-done.43, f32[1024]{0:T(1024)S(1)} %copy-done.36, f32[512]{0:T(512)S(1)} %add_rsqrt_fusion, ...), kind=kOutput, calls=%fused_computation.8 | convolution fusion | flops 4339531776 | bytes 31469568 | tf_op jit(solution)/shard_map/dot_general | solution.py:29
  332.0 9.2 multiply_reduce_fusion.1
  352.6 19.1 %collective-permute-done.12.ga_ref = bf16[512,1024]{1,0:T(8,128)(2,1)} collective-permute-done((bf16[512,1024]{1,0:T(8,128)(2,1)}, bf16[512,1024]{1,0:T(8,128)(2,1)}, u32[]{:S(2)}, u32[]{:S(2)}) %collective-permute-start.12) | collective-permute-done | bytes 1048608 | tf_op jit(solution)/shard_map/ppermute | solution.py:471
  371.7 4.5 convolution_convert_fusion.4
  377.9 21.8 %shard_map.247 = (bf16[512,1024]{1,0:T(8,128)(2,1)S(1)}, bf16[512,1024]{1,0:T(8,128)(2,1)}) custom-call(bf16[512,1024]{1,0:T(8,128)(2,1)} %collective-permute-done.12.ga_ref, bf16[512,1024]{1,0:T(8,128)(2,1)} %collective-permute-done.13.gb_ref, bf16[8,2048,256]{2,1,0:T(8,128)(2,1)} %bitcast.142, bf16[8,2048,1024]{2,1,0:T(8,128)(2,1)} %get-tuple-element.53.p_ref, ...), custom_call_target="tpu_custom_call" | custom-call | flops 8589934592 | bytes 67108864 | tf_op jit(solution)/shard_map/pallas_call | solution.py:254
  401.1 21.8 %shard_map.246 = (bf16[512,1024]{1,0:T(8,128)(2,1)S(1)}, bf16[512,1024]{1,0:T(8,128)(2,1)S(1)}) custom-call(bf16[512,1024]{1,0:T(8,128)(2,1)} %get-tuple-element.75.ga_ref, bf16[512,1024]{1,0:T(8,128)(2,1)} %collective-permute-done.9.gb_ref, bf16[8,2048,256]{2,1,0:T(8,128)(2,1)} %bitcast.143, bf16[8,2048,1024]{2,1,0:T(8,128)(2,1)} %get-tuple-element.50.p_ref, ...), custom_call_target="tpu_custom_call" | custom-call | flops 8589934592 | bytes 67108864 | tf_op jit(solution)/shard_map/pallas_call | solution.py:254
  429.7 15.8 %shard_map.245 = (f32[512,1024]{1,0:T(8,128)S(1)}, bf16[512,1024]{1,0:T(8,128)(2,1)S(1)}, bf16[512,1024]{1,0:T(8,128)(2,1)S(1)}, f32[8,1,256]{2,1,0:T(1,128)S(1)}, f32[8,8,256]{2,1,0:T(8,128)S(1)}) custom-call(f32[8]{0:T(128)S(1)} %add_divide_fusion.open_ref, f32[512,1024]{1,0:T(8,128)S(1)} %copy-done.7, ...), custom_call_target="tpu_custom_call" | custom-call | flops 4294967296 | bytes 20971520 | tf_op jit(solution)/shard_map/pallas_call | solution.py:421
  447.9 8.5 collective-permute-done.17
  462.9 7.7 convolution_convert_fusion.2
  472.2 9.2 convolution_convert_fusion.1
  481.5 12.9 %convolution_convert_fusion = bf16[4096,1024]{1,0:T(8,128)(2,1)} fusion(bf16[512,1024]{1,0:T(8,128)(2,1)} %param.30, f32[512,4096]{1,0:T(8,128)} %get-tuple-element.106), kind=kOutput, calls=%fused_computation.16 | convolution fusion | flops 4318035968 | bytes 17825792 | tf_op jit(solution)/shard_map/tf,td->fd/dot_general | solution.py:561
  495.3 54.2 %all-reduce.2 = (f32[32,8]{0,1:T(8,128)}, f32[8]{0:T(128)}) all-reduce(f32[32,8]{0,1:T(8,128)S(1)} %convolution_add_fusion.1, f32[8]{0:T(128)S(1)} %subtract_multiply_fusion.1), channel_id=1, replica_groups=mesh['dp'=8,'mem'=4] {'dp','mem'}, use_global_device_ids=true, to_apply=%region_23.24 | all-reduce | flops 264 | bytes 2112 | tf_op jit(solution)/shard_map/psum | solution.py:632
  549.5 11.9 %add_convert_fusion.2 = bf16[512,1024]{1,0:T(8,128)(2,1)} fusion(f32[512,1024]{1,0:T(8,128)S(1)} %copy-done.25, bf16[4096,1024]{1,0:T(8,128)(2,1)} %get-tuple-element.47, f32[512,4096]{1,0:T(8,128)} %get-tuple-element.106), kind=kOutput, calls=%fused_computation.63 | convolution fusion | flops 4314890240 | bytes 19922944 | tf_op jit(solution)/shard_map/dot_general | solution.py:29
  567.2 91.7 %reduce-scatter.16.cloned.1.call-done = f32[32,4]{1,0:T(8,128)} async-done(((f32[1024,4]{1,0:T(8,128)}), f32[32,4]{1,0:T(8,128)}) %reduce-scatter.16.cloned.1.call-update) | async-done | bytes 528
  661.1 114.1 %reduce-scatter.8.cloned.1.call-done = bf16[32,3072]{1,0:T(8,128)(2,1)} async-done(((bf16[1024,3072]{1,0:T(8,128)(2,1)}), bf16[32,3072]{1,0:T(8,128)(2,1)}) %reduce-scatter.8.cloned.1.call-update) | async-done | bytes 196624 | tf_op jit(solution)/shard_map/reduce_scatter | solution.py:628
  776.8 148.3 %reduce-scatter.12.cloned.1.call-done = bf16[32,4096]{1,0:T(8,128)(2,1)} async-done(((bf16[1024,4096]{1,0:T(8,128)(2,1)}), bf16[32,4096]{1,0:T(8,128)(2,1)}) %reduce-scatter.12.cloned.1.call-update) | async-done | bytes 262160 | tf_op jit(solution)/shard_map/reduce_scatter | solution.py:628
  927.0 144.9 %reduce-scatter.14.cloned.1.call-done = bf16[128,1024]{1,0:T(8,128)(2,1)} async-done(((bf16[4096,1024]{1,0:T(8,128)(2,1)}), bf16[128,1024]{1,0:T(8,128)(2,1)}) %reduce-scatter.14.cloned.1.call-update) | async-done | bytes 262160 | tf_op jit(solution)/shard_map/reduce_scatter | solution.py:628
  (261 shorter events, 93.8 us)
Async XLA Ops:
  7.2 554.2 %reduce-scatter.10.cloned.1.call-start = ((), (), s32[]{:S(2)}) async-start(), calls=%async_computation.6 | async-start | bytes 2162688 | tf_op jit(solution)/shard_map/reduce_scatter | solution.py:628
  40.1 141.5 %copy-start.41 = (f32[1024]{0:T(1024)}, f32[1024]{0:T(1024)S(1)}, u32[]{:S(2)}) copy-start(f32[1024]{0:T(1024)S(1)} %add.133) | copy-start | bytes 12292
  45.2 135.9 %collective-permute-start.2 = (bf16[512,1024]{1,0:T(8,128)(2,1)S(1)}, bf16[512,1024]{1,0:T(8,128)(2,1)}, u32[]{:S(2)}, u32[]{:S(2)}) collective-permute-start(bf16[512,1024]{1,0:T(8,128)(2,1)S(1)} %convolution_convert_fusion.5.qa_ref.q_ref), channel_id=1, source_target_pairs={{0,2},{1,3},{2,0},{3,1},{4,6},{5,7},{6,4},{7,5},{8,10},{9,11},{10,... | collective-permute-start | bytes 3145736 | tf_op jit(solution)/shard_map/ppermute | solution.py:471
  45.4 187.4 %collective-permute-start = (bf16[512,1024]{1,0:T(8,128)(2,1)S(1)}, bf16[512,1024]{1,0:T(8,128)(2,1)S(1)}, u32[]{:S(2)}, u32[]{:S(2)}) collective-permute-start(bf16[512,1024]{1,0:T(8,128)(2,1)S(1)} %convolution_convert_fusion.5.qa_ref.q_ref), channel_id=1, source_target_pairs={{0,1},{1,0},{2,3},{3,2},{4,5},{5,4},{6,7},{7,6},{8,9},{9,8},{10,11... | collective-permute-start | bytes 3145736 | tf_op jit(solution)/shard_map/ppermute | solution.py:471
  181.1 13.2 %collective-permute-start.3 = (bf16[512,1024]{1,0:T(8,128)(2,1)}, bf16[512,1024]{1,0:T(8,128)(2,1)}, u32[]{:S(2)}, u32[]{:S(2)}) collective-permute-start(bf16[512,1024]{1,0:T(8,128)(2,1)} %collective-permute-done.2.qa_ref), channel_id=1, source_target_pairs={{0,1},{1,0},{2,3},{3,2},{4,5},{5,4},{6,7},{7,6},{8,9},{9,8},{10,11... | collective-permute-start | bytes 3145736 | tf_op jit(solution)/shard_map/ppermute | solution.py:471
  232.3 39.9 %collective-permute-start.4 = (f32[8,512]{1,0:T(8,128)S(1)}, f32[8,512]{1,0:T(8,128)S(1)}, u32[]{:S(2)}, u32[]{:S(2)}) collective-permute-start(f32[8,512]{1,0:T(8,128)S(1)} %slice.106), channel_id=1, source_target_pairs={{0,1},{1,0},{2,3},{3,2},{4,5},{5,4},{6,7},{7,6},{8,9},{9,8},{10,11... | collective-permute-start | bytes 49160 | tf_op jit(solution)/shard_map/ppermute | solution.py:471
  232.3 40.2 %collective-permute-start.7 = (bf16[512,1024]{1,0:T(8,128)(2,1)}, bf16[512,1024]{1,0:T(8,128)(2,1)S(1)}, u32[]{:S(2)}, u32[]{:S(2)}) collective-permute-start(bf16[512,1024]{1,0:T(8,128)(2,1)} %get-tuple-element.42), channel_id=1, source_target_pairs={{0,1},{1,0},{2,3},{3,2},{4,5},{5,4},{6,7},{7,6},{8,9},{9,8},{10,11... | collective-permute-start | bytes 3145736 | tf_op jit(solution)/shard_map/ppermute | solution.py:471
  272.1 33.6 %collective-permute-start.6 = (bf16[512,1024]{1,0:T(8,128)(2,1)}, bf16[512,1024]{1,0:T(8,128)(2,1)}, u32[]{:S(2)}, u32[]{:S(2)}) collective-permute-start(bf16[512,1024]{1,0:T(8,128)(2,1)} %get-tuple-element.40), channel_id=1, source_target_pairs={{0,1},{1,0},{2,3},{3,2},{4,5},{5,4},{6,7},{7,6},{8,9},{9,8},{10,11... | collective-permute-start | bytes 3145736 | tf_op jit(solution)/shard_map/ppermute | solution.py:471
  277.7 28.0 %collective-permute-start.8 = (bf16[512,1024]{1,0:T(8,128)(2,1)}, bf16[512,1024]{1,0:T(8,128)(2,1)}, u32[]{:S(2)}, u32[]{:S(2)}) collective-permute-start(bf16[512,1024]{1,0:T(8,128)(2,1)} %fusion.30), channel_id=1, source_target_pairs={{0,2},{1,3},{2,0},{3,1},{4,6},{5,7},{6,4},{7,5},{8,10},{9,11},{10,... | collective-permute-start | bytes 3145736 | tf_op jit(solution)/shard_map/ppermute | solution.py:471
  280.1 20.7 %collective-permute-start.1 = (f32[8,512]{1,0:T(8,128)S(1)}, f32[8,512]{1,0:T(8,128)S(1)}, u32[]{:S(2)}, u32[]{:S(2)}) collective-permute-start(f32[8,512]{1,0:T(8,128)S(1)} %slice.104), channel_id=1, source_target_pairs={{0,1},{1,0},{2,3},{3,2},{4,5},{5,4},{6,7},{7,6},{8,9},{9,8},{10,11... | collective-permute-start | bytes 49160 | tf_op jit(solution)/shard_map/ppermute | solution.py:471
  280.3 23.5 %collective-permute-start.5 = (f32[8,512]{1,0:T(8,128)S(1)}, f32[8,512]{1,0:T(8,128)S(1)}, u32[]{:S(2)}, u32[]{:S(2)}) collective-permute-start(f32[8,512]{1,0:T(8,128)S(1)} %get-tuple-element.79), channel_id=1, source_target_pairs={{0,2},{1,3},{2,0},{3,1},{4,6},{5,7},{6,4},{7,5},{8,10},{9,11},{10,... | collective-permute-start | bytes 49160 | tf_op jit(solution)/shard_map/ppermute | solution.py:471
  346.2 25.5 %collective-permute-start.12 = (bf16[512,1024]{1,0:T(8,128)(2,1)}, bf16[512,1024]{1,0:T(8,128)(2,1)}, u32[]{:S(2)}, u32[]{:S(2)}) collective-permute-start(bf16[512,1024]{1,0:T(8,128)(2,1)} %get-tuple-element.75.ga_ref), channel_id=1, source_target_pairs={{0,2},{1,3},{2,0},{3,1},{4,6},{5,7},{6,4},{7,5},{8,10},{9,11},{10,... | collective-permute-start | bytes 3145736 | tf_op jit(solution)/shard_map/ppermute | solution.py:471
  347.7 53.4 %collective-permute-start.9 = (bf16[512,1024]{1,0:T(8,128)(2,1)}, bf16[512,1024]{1,0:T(8,128)(2,1)}, u32[]{:S(2)}, u32[]{:S(2)}) collective-permute-start(bf16[512,1024]{1,0:T(8,128)(2,1)} %get-tuple-element.75.ga_ref), channel_id=1, source_target_pairs={{0,1},{1,0},{2,3},{3,2},{4,5},{5,4},{6,7},{7,6},{8,9},{9,8},{10,11... | collective-permute-start | bytes 3145736 | tf_op jit(solution)/shard_map/ppermute | solution.py:471
  351.8 24.4 %collective-permute-start.14 = (f32[16,512]{1,0:T(8,128)S(1)}, f32[16,512]{1,0:T(8,128)S(1)}, u32[]{:S(2)}, u32[]{:S(2)}) collective-permute-start(f32[16,512]{1,0:T(8,128)S(1)} %pad_maximum_fusion), channel_id=1, source_target_pairs={{0,2},{1,3},{2,0},{3,1},{4,6},{5,7},{6,4},{7,5},{8,10},{9,11},{10,... | collective-permute-start | bytes 98312 | tf_op jit(solution)/shard_map/ppermute | solution.py:471
  352.4 24.5 %collective-permute-start.10 = (f32[16,512]{1,0:T(8,128)S(1)}, f32[16,512]{1,0:T(8,128)S(1)}, u32[]{:S(2)}, u32[]{:S(2)}) collective-permute-start(f32[16,512]{1,0:T(8,128)S(1)} %pad_maximum_fusion), channel_id=1, source_target_pairs={{0,1},{1,0},{2,3},{3,2},{4,5},{5,4},{6,7},{7,6},{8,9},{9,8},{10,11... | collective-permute-start | bytes 98312 | tf_op jit(solution)/shard_map/ppermute | solution.py:471
  371.7 6.2 collective-permute-start.13
  376.2 282.7 %reduce-scatter.16.cloned.1.call-start = ((), (), s32[]{:S(2)}) async-start(), calls=%async_computation.9 | async-start | bytes 540672
  376.3 1.4 collective-permute-start.15
  400.6 23.4 %collective-permute-start.16 = (bf16[512,1024]{1,0:T(8,128)(2,1)}, bf16[512,1024]{1,0:T(8,128)(2,1)}, u32[]{:S(2)}, u32[]{:S(2)}) collective-permute-start(bf16[512,1024]{1,0:T(8,128)(2,1)} %get-tuple-element.55), channel_id=1, source_target_pairs={{0,1},{1,0},{2,3},{3,2},{4,5},{5,4},{6,7},{7,6},{8,9},{9,8},{10,11... | collective-permute-start | bytes 3145736 | tf_op jit(solution)/shard_map/ppermute | solution.py:471
  423.9 24.0 %collective-permute-start.11 = (bf16[512,1024]{1,0:T(8,128)(2,1)}, bf16[512,1024]{1,0:T(8,128)(2,1)S(1)}, u32[]{:S(2)}, u32[]{:S(2)}) collective-permute-start(bf16[512,1024]{1,0:T(8,128)(2,1)} %copy-done.19), channel_id=1, source_target_pairs={{0,1},{1,0},{2,3},{3,2},{4,5},{5,4},{6,7},{7,6},{8,9},{9,8},{10,11... | collective-permute-start | bytes 3145736 | tf_op jit(solution)/shard_map/ppermute | solution.py:471
  426.5 30.0 %collective-permute-start.17 = (bf16[512,1024]{1,0:T(8,128)(2,1)S(1)}, bf16[512,1024]{1,0:T(8,128)(2,1)S(1)}, u32[]{:S(2)}, u32[]{:S(2)}) collective-permute-start(bf16[512,1024]{1,0:T(8,128)(2,1)S(1)} %add_convert_fusion.1), channel_id=1, source_target_pairs={{0,2},{1,3},{2,0},{3,1},{4,6},{5,7},{6,4},{7,5},{8,10},{9,11},{10,... | collective-permute-start | bytes 3145736 | tf_op jit(solution)/shard_map/ppermute | solution.py:471
  462.6 312.5 %reduce-scatter.8.cloned.1.call-start = ((), (), s32[]{:S(2)}) async-start(), calls=%async_computation.5 | async-start | bytes 6488064 | tf_op jit(solution)/shard_map/reduce_scatter | solution.py:628
  470.6 454.6 %reduce-scatter.12.cloned.1.call-start = ((), (), s32[]{:S(2)}) async-start(), calls=%async_computation.7 | async-start | bytes 8650752 | tf_op jit(solution)/shard_map/reduce_scatter | solution.py:628
  481.4 590.4 %reduce-scatter.14.cloned.1.call-start = ((), (), s32[]{:S(2)}) async-start(), calls=%async_computation.8 | async-start | bytes 8650752 | tf_op jit(solution)/shard_map/reduce_scatter | solution.py:628
  (55 other events, 478.1 us)
Sparse Core Ops, SparseCore 0:
  376.3 149.5 reduce-scatter.9
  528.8 130.0 reduce-scatter.15
  664.6 110.5 reduce-scatter.7
  777.4 147.7 reduce-scatter.11
  927.4 144.3 reduce-scatter.13

commit v2 on v1

--- a/solution.py
+++ b/solution.py
@@ -29,132 +29,396 @@
     return lax.dot_general(left, right, dims, preferred_element_type=F32)
 
 
-def gather_kernel(n_hi, orders, *refs):
-    n = len(orders)
-    ins, outs = refs[:n], refs[n : 2 * n]
-    send_sem, recv_sem, local_sem = refs[2 * n :]
-    dp, mem = lax.axis_index("dp"), lax.axis_index("mem")
-    hi, lo = dp // 2, dp % 2
-    x_at, core_at = mem // 2, mem % 2
-    sizes = (n_hi, 2, 2, 2)
-    own, along_y, along_x, along_core = (0, 0, 0, 0), (0, 1, 0, 0), (0, 0, 1, 0), (0, 0, 0, 1)
-
-    def device(step):
-        z = lax.rem(hi + step[0], n_hi)
-        return (z * 2 + (lo + step[1]) % 2, (x_at + step[2]) % 2 * 2 + (core_at + step[3]) % 2)
-
-    def plus(left, right):
-        return tuple((a + b) % k for a, b, k in zip(left, right, sizes))
-
-    def minus(left, right):
-        return tuple((a - b) % k for a, b, k in zip(left, right, sizes))
-
-    def number(step):
-        return ((step[0] * 2 + step[1]) * 2 + step[2]) * 2 + step[3]
-
-    partners = [(z, 0, 0, 0) for z in range(1, n_hi)] + [along_y, along_x, along_core]
-    barrier = pltpu.get_barrier_semaphore()
-    for partner in partners:
-        pl.semaphore_signal(barrier, inc=1, device_id=device(partner), device_id_type=MESH)
-    pl.semaphore_wait(barrier, len(partners))
-
-    def place(a, source):
-        d, m = device(source)
-        rows = ins[a].shape[0]
-        return outs[a].at[pl.ds(pl.multiple_of((d * 4 + m) * rows, rows), rows)]
-
-    started = []
-    counts = [0] * n
-
-    def send(a, source, to):
+OWN, ALONG_Y, ALONG_X, ALONG_CORE = (0, 0, 0, 0), (0, 1, 0, 0), (0, 0, 1, 0), (0, 0, 0, 1)
+ANYWHERE = pl.BlockSpec(memory_space=pl.ANY)
+IN_VMEM = pl.BlockSpec(memory_space=pltpu.VMEM)
+SCALARS = pl.BlockSpec(memory_space=pltpu.SMEM)
+
+
+class Place:
+    def __init__(self, n_hi):
+        self.sizes = (n_hi, 2, 2, 2)
+        dp, mem = lax.axis_index("dp"), lax.axis_index("mem")
+        self.at = (dp // 2, dp % 2, mem // 2, mem % 2)
+
+    def device(self, step):
+        z, y, x, core = [(a + s) % n for a, s, n in zip(self.at, step, self.sizes)]
+        return (z * 2 + y, x * 2 + core)
+
+    def number(self, step):
+        dp, mem = self.device(step)
+        return dp * 4 + mem
+
+    def plus(self, left, right):
+        return tuple((a + b) % n for a, b, n in zip(left, right, self.sizes))
+
+    def minus(self, left, right):
+        return tuple((a - b) % n for a, b, n in zip(left, right, self.sizes))
+
+    def partners(self):
+        return [(z, 0, 0, 0) for z in range(1, self.sizes[0])] + [ALONG_Y, ALONG_X, ALONG_CORE]
+
+    def greet(self):
+        barrier = pltpu.get_barrier_semaphore()
+        for partner in self.partners():
+            pl.semaphore_signal(
+                barrier, inc=1, device_id=self.device(partner), device_id_type=MESH
+            )
+        pl.semaphore_wait(barrier, len(self.partners()))
+
+    def copy(self, src, dst, send, recv, device):
         copy = pltpu.make_async_remote_copy(
-            src_ref=ins[a] if source == own else place(a, source),
-            dst_ref=place(a, source),
-            send_sem=send_sem.at[a, counts[a]],
-            recv_sem=recv_sem.at[a, number(minus(source, to))],
-            device_id=device(to),
+            src_ref=src,
+            dst_ref=dst,
+            send_sem=send,
+            recv_sem=recv,
+            device_id=device,
             device_id_type=MESH,
         )
-        counts[a] += 1
         copy.start()
-        started.append(copy)
-
-    def arrived(a, source):
-        ref = place(a, source)
+        return copy
+
+    def arrived(self, ref, recv):
         pltpu.make_async_remote_copy(
             src_ref=ref,
             dst_ref=ref,
-            send_sem=send_sem.at[a, 0],
-            recv_sem=recv_sem.at[a, number(source)],
-            device_id=device(along_core),
+            send_sem=recv,
+            recv_sem=recv,
+            device_id=self.device(ALONG_CORE),
             device_id_type=MESH,
         ).wait_recv()
 
-    first = [along_y if order == "zyx" else along_x for order in orders]
-    second = [along_x if order == "zyx" else along_y for order in orders]
-    for a in range(n):
-        for z in range(1, n_hi):
-            send(a, own, (z, 0, 0, 0))
-        send(a, own, along_y)
-        send(a, own, along_x)
-    kept = []
-    for a in range(n):
-        send(a, own, along_core)
-        copy = pltpu.make_async_copy(ins[a], place(a, own), local_sem.at[a])
-        copy.start()
-        kept.append(copy)
-    near_first = [0]
+
+def near_first(n_hi):
+    order = [0]
     for z in range(1, n_hi // 2 + 1):
-        near_first += [k for k in dict.fromkeys((z, n_hi - z)) if k < n_hi]
-    for z in near_first:
+        order += [k for k in dict.fromkeys((z, n_hi - z)) if k < n_hi]
+    return order
+
+
+class Gather:
+    def __init__(self, place, orders, ins, outs, sems):
+        self.place, self.ins, self.outs = place, ins, outs
+        self.send_sem, self.recv_sem, self.own_sem = sems
+        self.n = len(orders)
+        self.first = [ALONG_Y if order == "zyx" else ALONG_X for order in orders]
+        self.second = [ALONG_X if order == "zyx" else ALONG_Y for order in orders]
+        self.started = []
+        self.counts = [0] * self.n
+
+    def spot(self, a, source):
+        return self.outs[a].at[self.place.number(source)]
+
+    def index(self, step):
+        return ((step[0] * 2 + step[1]) * 2 + step[2]) * 2 + step[3]
+
+    def send(self, a, source, to):
+        place = self.place
+        self.started.append(
+            place.copy(
+                self.ins[a] if source == OWN else self.spot(a, source),
+                self.spot(a, source),
+                self.send_sem.at[a, self.counts[a]],
+                self.recv_sem.at[a, self.index(place.minus(source, to))],
+                place.device(to),
+            )
+        )
+        self.counts[a] += 1
+
+    def arrived(self, a, source):
+        self.place.arrived(self.spot(a, source), self.recv_sem.at[a, self.index(source)])
+
+    def begin(self):
+        for a in range(self.n):
+            for to in self.place.partners()[:-1]:
+                self.send(a, OWN, to)
+        self.kept = []
+        for a in range(self.n):
+            self.send(a, OWN, ALONG_CORE)
+            copy = pltpu.make_async_copy(self.ins[a], self.spot(a, OWN), self.own_sem.at[a])
+            copy.start()
+            self.kept.append(copy)
+
+    def middle(self, z):
         at = (z, 0, 0, 0)
         if z:
-            for a in range(n):
-                arrived(a, at)
-                for to in (first[a], second[a], along_core):
-                    send(a, at, to)
-        for a in range(n):
-            source = plus(at, first[a])
-            arrived(a, source)
-            for to in (second[a], along_core):
-                send(a, source, to)
-    for z in near_first:
-        for a in range(n):
-            for source in (second[a], plus(first[a], second[a])):
-                source = plus((z, 0, 0, 0), source)
-                arrived(a, source)
-                send(a, source, along_core)
-    for z in near_first:
-        for y in range(2):
-            for x in range(2):
-                for a in range(n):
-                    arrived(a, (z, y, x, 1))
-    for copy in started:
-        copy.wait_send()
-    for copy in kept:
-        copy.wait()
+            for a in range(self.n):
+                self.arrived(a, at)
+                for to in (self.first[a], self.second[a], ALONG_CORE):
+                    self.send(a, at, to)
+        for a in range(self.n):
+            source = self.place.plus(at, self.first[a])
+            self.arrived(a, source)
+            for to in (self.second[a], ALONG_CORE):
+                self.send(a, source, to)
+
+    def late(self, z):
+        for a in range(self.n):
+            for step in (self.second[a], self.place.plus(self.first[a], self.second[a])):
+                source = self.place.plus((z, 0, 0, 0), step)
+                self.arrived(a, source)
+                self.send(a, source, ALONG_CORE)
+
+    def finish(self):
+        for z in near_first(self.place.sizes[0]):
+            for y in range(2):
+                for x in range(2):
+                    for a in range(self.n):
+                        self.arrived(a, (z, y, x, 1))
+        for copy in self.started:
+            copy.wait_send()
+        for copy in self.kept:
+            copy.wait()
+
+
+def gather_scratch(n, n_hi):
+    sends = (n_hi - 1) + 3 + (n_hi - 1) * 3 + n_hi * 2 + n_hi * 2
+    dma = pltpu.SemaphoreType.DMA
+    return [dma((n, sends)), dma((n, n_hi * 8)), dma((n,))]
+
+
+def gather_kernel(n_hi, orders, *refs):
+    n = len(orders)
+    place = Place(n_hi)
+    place.greet()
+    gather = Gather(place, orders, refs[:n], refs[n : 2 * n], refs[2 * n :])
+    gather.begin()
+    for z in near_first(n_hi):
+        gather.middle(z)
+    for z in near_first(n_hi):
+        gather.late(z)
+    gather.finish()
 
 
 def gather_rows(arrays, orders, collective_id):
     n = len(arrays)
     n_hi = lax.axis_size("dp") // 2
-    total = n_hi * 8
-    sends = (n_hi - 1) + 3 + (n_hi - 1) * 3 + n_hi * 2 + n_hi * 2
-    anywhere = pl.BlockSpec(memory_space=pl.ANY)
     return pl.pallas_call(
         functools.partial(gather_kernel, n_hi, orders),
-        out_shape=[
-            jax.ShapeDtypeStruct((a.shape[0] * total,) + a.shape[1:], a.dtype) for a in arrays
-        ],
-        in_specs=[anywhere] * n,
-        out_specs=[anywhere] * n,
-        scratch_shapes=[
-            pltpu.SemaphoreType.DMA((n, sends)),
-            pltpu.SemaphoreType.DMA((n, total)),
-            pltpu.SemaphoreType.DMA((n,)),
-        ],
+        out_shape=[jax.ShapeDtypeStruct((n_hi * 8,) + a.shape, a.dtype) for a in arrays],
+        in_specs=[ANYWHERE] * n,
+        out_specs=[ANYWHERE] * n,
+        scratch_shapes=gather_scratch(n, n_hi),
         compiler_params=pltpu.CompilerParams(collective_id=collective_id, has_side_effects=True),
     )(*arrays)
+
+
+class Scatter:
+    def __init__(self, place, orders, ins, outs, buffers, sems, small=None):
+        self.place, self.ins, self.outs = place, ins, outs
+        self.accs, self.from_core, self.from_first, self.from_second, self.from_z = buffers
+        (
+            self.load_sem,
+            self.core_send,
+            self.core_recv,
+            self.first_send,
+            self.first_recv,
+            self.second_send,
+            self.second_recv,
+            self.z_send,
+            self.z_recv,
+        ) = sems[:9]
+        self.small = small
+        self.small_sems = sems[9:]
+        self.n = len(orders)
+        self.n_hi = place.sizes[0]
+        self.first = [ALONG_X if order == "xyz" else ALONG_Y for order in orders]
+        self.second = [ALONG_Y if order == "xyz" else ALONG_X for order in orders]
+        self.started = []
+        self.loads = {}
+
+    def step(self, a, z, two, one):
+        y, x = (two, one) if self.second[a] == ALONG_Y else (one, two)
+        return (z, y, x, 0)
+
+    def send(self, src, dst, send, recv, to):
+        self.started.append(self.place.copy(src, dst, send, recv, self.place.device(to)))
+
+    def begin(self, z, a):
+        for two, one in ((1, 1), (0, 1), (1, 0), (0, 0)):
+            s = (z * 2 + two) * 2 + one
+            step = self.step(a, z, two, one)
+            self.send(
+                self.ins[a].at[self.place.number(step[:3] + (1,))],
+                self.from_core[a].at[s],
+                self.core_send.at[a, s],
+                self.core_recv.at[a, s],
+                ALONG_CORE,
+            )
+            load = pltpu.make_async_copy(
+                self.ins[a].at[self.place.number(step)], self.accs[a].at[s], self.load_sem.at[a, s]
+            )
+            load.start()
+            self.loads[a, s] = load
+
+    def add(self, acc, got):
+        width = min(acc.shape[1], 1024)
+
+        def piece(k, carry):
+            at = pl.ds(pl.multiple_of(k * width, width), width)
+            acc[:, at] = (acc[:, at].astype(F32) + got[:, at].astype(F32)).astype(BF)
+            return carry
+
+        lax.fori_loop(0, acc.shape[1] // width, piece, 0)
+
+    def core(self, z, a):
+        for two, one in ((1, 1), (0, 1), (1, 0), (0, 0)):
+            k = z * 2 + two
+            s = k * 2 + one
+            self.loads[a, s].wait()
+            self.place.arrived(self.from_core[a].at[s], self.core_recv.at[a, s])
+            self.add(self.accs[a].at[s], self.from_core[a].at[s])
+            if one:
+                self.send(
+                    self.accs[a].at[s],
+                    self.from_first[a].at[k],
+                    self.first_send.at[a, k],
+                    self.first_recv.at[a, k],
+                    self.first[a],
+                )
+
+    def one(self, z, a):
+        for two in (1, 0):
+            k = z * 2 + two
+            acc = self.accs[a].at[k * 2]
+            self.place.arrived(self.from_first[a].at[k], self.first_recv.at[a, k])
+            self.add(acc, self.from_first[a].at[k])
+            if two:
+                self.send(
+                    acc,
+                    self.from_second[a].at[z],
+                    self.second_send.at[a, z],
+                    self.second_recv.at[a, z],
+                    self.second[a],
+                )
+
+    def two(self, z, a):
+        acc = self.accs[a].at[z * 4]
+        self.place.arrived(self.from_second[a].at[z], self.second_recv.at[a, z])
+        self.add(acc, self.from_second[a].at[z])
+        if z:
+            self.send(
+                acc,
+                self.from_z[a].at[z - 1],
+                self.z_send.at[a, z - 1],
+                self.z_recv.at[a, z - 1],
+                (z, 0, 0, 0),
+            )
+
+    def last(self, a):
+        for z in range(1, self.n_hi):
+            self.place.arrived(self.from_z[a].at[z - 1], self.z_recv.at[a, z - 1])
+        out, acc, got = self.outs[a], self.accs[a].at[0], self.from_z[a]
+        width = min(out.shape[1], 1024)
+
+        def piece(k, carry):
+            at = pl.ds(pl.multiple_of(k * width, width), width)
+            total = acc[:, at].astype(F32)
+            for z in range(1, self.n_hi):
+                total = total + got[z - 1, :, at].astype(F32)
+            out[:, at] = total
+            return carry
+
+        lax.fori_loop(0, out.shape[1] // width, piece, 0)
+
+    def small_steps(self):
+        return [ALONG_CORE, ALONG_X, ALONG_Y] + [1 << k for k in range((self.n_hi - 1).bit_length())]
+
+    def small_begin(self):
+        source, total, _ = self.small
+        total[...] = source[...]
+        self.small_send(0)
+
+    def small_send(self, k):
+        _, total, buffer = self.small
+        step = self.small_steps()[k]
+        z, y, x, core = self.place.at
+        if isinstance(step, int):
+            device = ((z + step - 2 * step * ((z // step) % 2)) * 2 + y, x * 2 + core)
+        else:
+            device = self.place.device(step)
+        buffer[0, k] = total[...]
+        send, recv = self.small_sems
+        self.started.append(
+            self.place.copy(buffer.at[0, k], buffer.at[1, k], send.at[k], recv.at[k], device)
+        )
+
+    def small_next(self, k):
+        _, total, buffer = self.small
+        self.place.arrived(buffer.at[1, k], self.small_sems[1].at[k])
+        total[...] = total[...] + buffer[1, k]
+        if k + 1 < len(self.small_steps()):
+            self.small_send(k + 1)
+
+    def finish(self):
+        for copy in self.started:
+            copy.wait_send()
+
+
+def scatter_buffers(shapes, n_hi):
+    counts = (n_hi * 4, n_hi * 4, n_hi * 2, n_hi, n_hi - 1)
+    return [pltpu.VMEM((count,) + shape, BF) for count in counts for shape in shapes]
+
+
+def scatter_sems(n, n_hi):
+    counts = (n_hi * 4,) * 3 + (n_hi * 2,) * 2 + (n_hi,) * 2 + (n_hi - 1,) * 2
+    return [pltpu.SemaphoreType.DMA((n, count)) for count in counts]
+
+
+def scatter_kernel(n_hi, orders, *refs):
+    n = len(orders)
+    ins, small_in, outs, small_out = refs[:n], refs[n], refs[n + 1 : 2 * n + 1], refs[2 * n + 1]
+    rest = refs[2 * n + 2 :]
+    buffers = [rest[k * n : (k + 1) * n] for k in range(5)]
+    place = Place(n_hi)
+    place.greet()
+    scatter = Scatter(
+        place, orders, ins, outs, buffers, rest[5 * n + 1 :], (small_in, small_out, rest[5 * n])
+    )
+    order = near_first(n_hi)[::-1]
+    rounds = len(scatter.small_steps())
+    for k, z in enumerate(order):
+        for a in range(n):
+            scatter.begin(z, a)
+        if k == 0:
+            scatter.small_begin()
+    for k in range(max(len(order) + 2, rounds)):
+        for a in range(n):
+            if k < len(order):
+                scatter.core(order[k], a)
+        for a in range(n):
+            if 0 <= k - 1 < len(order):
+                scatter.one(order[k - 1], a)
+        for a in range(n):
+            if 0 <= k - 2 < len(order):
+                scatter.two(order[k - 2], a)
+        if k < rounds:
+            scatter.small_next(k)
+    for a in range(n):
+        scatter.last(a)
+    scatter.finish()
+
+
+def scatter_sums(arrays, orders, small, collective_id):
+    n = len(arrays)
+    n_hi = lax.axis_size("dp") // 2
+    shapes = [a.shape[1:] for a in arrays]
+    rounds = 3 + (n_hi - 1).bit_length()
+    dma = pltpu.SemaphoreType.DMA
+    return pl.pallas_call(
+        functools.partial(scatter_kernel, n_hi, orders),
+        out_shape=[jax.ShapeDtypeStruct(shape, F32) for shape in shapes]
+        + [jax.ShapeDtypeStruct(small.shape, F32)],
+        in_specs=[ANYWHERE] * n + [IN_VMEM],
+        out_specs=[IN_VMEM] * (n + 1),
+        scratch_shapes=scatter_buffers(shapes, n_hi)
+        + [pltpu.VMEM((2, rounds) + small.shape, F32)]
+        + scatter_sems(n, n_hi)
+        + [dma((rounds,)), dma((rounds,))],
+        compiler_params=pltpu.CompilerParams(
+            collective_id=collective_id, has_side_effects=True, vmem_limit_bytes=56 << 20
+        ),
+    )(*arrays, small)
 
 
 def recall_kernel(qa_ref, qb_ref, mem_ref, slot_ref, outa_ref, outb_ref, lse_ref, p_ref):
@@ -389,9 +653,6 @@
     tot_ref[0] = total
 
 
-SCALARS = pl.BlockSpec(memory_space=pltpu.SMEM)
-
-
 def segment_forward(queries, keys_values, cache, near, length):
     return pl.pallas_call(
         segment_kernel,
@@ -512,7 +773,10 @@
     full_kv, full_out, full_up, full_down = gather_rows(
         [w_qkv[:, width:], w_out, w_up, w_down], ("zxy", "zyx", "zyx", "zxy"), 1
     )
-    rows = full_norms.reshape(-1, 16, 128)[:, :4, : norm_gains.shape[1]].astype(F32)
+    full_q, full_kv, full_out, full_up, full_down = [
+        full.reshape(-1, full.shape[2]) for full in (full_q, full_kv, full_out, full_up, full_down)
+    ]
+    rows = full_norms[:, :4, : norm_gains.shape[1]].astype(F32)
     rows = rows.transpose(1, 0, 2).reshape(4, width)
     gain_rows, shift_rows = rows[:2], rows[2:]
 
@@ -624,12 +888,23 @@
             jnp.sum(grad_normed_two, axis=0),
         ]
     )
-    share_qkv, share_out, share_up, share_down = [
-        lax.psum_scatter(g.astype(BF), AXES, scatter_dimension=0, tiled=True).astype(F32)
-        for g in (grad_wqkv, grad_wout, grad_up, grad_down)
-    ]
-    share_norms = lax.psum_scatter(grad_norms, AXES, scatter_dimension=1, tiled=True)
-    table_total, gate_total = lax.psum((grad_table, grad_gate), AXES)
+    devices = lax.axis_size("dp") * groups
+    rest = jnp.pad(jnp.concatenate([grad_table.reshape(-1), grad_gate]), (0, 1024 - 264))
+    small = jnp.concatenate([grad_norms.reshape(-1, 128), rest.reshape(-1, 128)], axis=0)
+    share_qkv, share_out, share_up, share_down, small = scatter_sums(
+        [
+            g.astype(BF).reshape(devices, -1, g.shape[1])
+            for g in (grad_wqkv, grad_wout, grad_up, grad_down)
+        ],
+        ("yxz", "xyz", "xyz", "yxz"),
+        small,
+        2,
+    )
+    own = norm_gains.shape[1]
+    at = (lax.axis_index("dp") * groups + me) * own
+    share_norms = lax.dynamic_slice_in_dim(small[:32].reshape(4, width), at, own, axis=1)
+    rest = small[32:].reshape(-1)
+    table_total, gate_total = rest[: BUCKETS * H].reshape(BUCKETS, H), rest[BUCKETS * H :][:H]
     return (
         output.astype(BF),
         grad_tokens,

time: 1090 us -> 649 us (0.60)
  waiting for transfers between devices: 531 us -> 18.5 us
  Pallas kernels: 300 us -> 446 us
  blocking collectives: 54.2 us -> 0 us
  between operations: 15.7 us -> 2.57 us
    reduce_scatter x4 -> x0, waiting for transfers between devices: 407 us -> none  [local(): lax.psum_scatter(g.astype(BF), AXES, scatter_dimension=0, tiled=True)]
    pallas_call x0 -> x1, Pallas kernels: none -> 138 us  [scatter_sums(): pl.pallas_call(functools.partial(scatter_kernel, n_hi, orders), out_shape...]
    unnamed x6 -> x0, waiting for transfers between devices: 91.8 us -> none
    psum x1 -> x0, blocking collectives: 54.2 us -> none  [local(): table_total, gate_total = lax.psum((grad_table, grad_gate), AXES)]
    ppermute x18, waiting for transfers between devices: 31.5 us -> 18.5 us  [swap(): lax.ppermute(v, 'mem', [(i, i ^ turn) for i in range(lax.axis_size('mem'))])]
    unnamed x119 -> x131, local copies, waits for them, and re-layouts: 27.5 us -> 29.5 us
  transfers between devices with their start and end apart: 23 -> 18, of which waited for: 8 -> 2; matrix products, arithmetic and copies ran while one was open for 10% -> 12% of each run, Pallas kernels for 25% -> 44%
where the time goes in v2:
time: 649 us; the launch traced here: 640 us
  Pallas kernels  446 us (69%)
  matrix products  97 us (15%)
  local copies, waits for them, and re-layouts  42.9 us (7%)
  other arithmetic  23.7 us (4%)
  waiting for transfers between devices  18.5 us (3%)
  starting transfers between devices  9.22 us (1%)
    pallas_call x2, Pallas kernels, gather_rows(): pl.pallas_call(functools.partial(gather_kernel, n_hi, orders), out_shape=...  151 us
    pallas_call x1, Pallas kernels, scatter_sums(): pl.pallas_call(functools.partial(scatter_kernel, n_hi, orders), out_shape...  138 us
    pallas_call x2, Pallas kernels, recall(): pl.pallas_call(recall_kernel, grid=(H,), in_specs=[head_columns(rows), he...  76.3 us
    dot_general x10, matrix products, dot(): return lax.dot_general(left, right, dims, preferred_element_type=F32)  65.5 us
    pallas_call x2, Pallas kernels, recall_grad(): pl.pallas_call(recall_grad_kernel, grid=(H,), in_specs=[head_columns(rows...  41.7 us
    unnamed x131, local copies, waits for them, and re-layouts  29.5 us
    pallas_call x1, Pallas kernels, segment_forward(): pl.pallas_call(segment_kernel, grid=(H,), in_specs=[SCALARS, per_head(1,...  23.4 us
    ppermute x18, waiting for transfers between devices, swap(): lax.ppermute(v, 'mem', [(i, i ^ turn) for i in range(lax.axis_size('mem'))])  18.5 us
  transfers between devices with their start and end apart: 18, of which 2 were waited for; matrix products, arithmetic and copies ran while one was open for 12% of the time, Pallas kernels for 44%

profile of v2, /device:TPU:0, one launch (start us, length us, event | category | flops | bytes accessed | tf_op | source)
XLA Modules:
  0.0 640.0 jit_solution(7675549390073533547)
XLA Ops:
  3.5 29.0 %shard_map.240 = (bf16[32,32,1024]{2,1,0:T(8,128)(2,1)}, bf16[32,16,128]{2,1,0:T(8,128)(2,1)}) custom-call(bf16[32,1024]{1,0:T(8,128)(2,1)} %slice.98.refs_0_, bf16[16,128]{1,0:T(8,128)(2,1)} %fusion.51.refs_1_), custom_call_target="tpu_custom_call" | custom-call | tf_op jit(solution)/shard_map/pallas_call | solution.py:196
  41.3 121.6 %shard_map.243 = (bf16[32,32,2048]{2,1,0:T(8,128)(2,1)}, bf16[32,32,1024]{2,1,0:T(8,128)(2,1)}, bf16[32,32,4096]{2,1,0:T(8,128)(2,1)}, bf16[32,128,1024]{2,1,0:T(8,128)(2,1)}) custom-call(bf16[32,2048]{1,0:T(8,128)(2,1)} %slice.107.refs_0_, bf16[32,1024]{1,0:T(8,128)(2,1)} %refs_1_.1, bf16[32,4096]{1,0:T(8,128)(2,1)} %refs_2_.1, bf16[128,1024]{1,0:T(8,128)(2,1)} %refs_3_.1), custom_call_target="tpu_custom_call" | custom-call | tf_op jit(solution)/shard_map/pallas_call | solution.py:196
  162.9 11.6 %fusion.63 = f32[4096,512]{0,1:T(8,128)} fusion(bf16[4096,1024]{1,0:T(8,128)(2,1)} %bitcast.181, bf16[512,1024]{1,0:T(8,128)(2,1)} %param.30), kind=kOutput, calls=%fused_computation.159 | convolution fusion | flops 4294967296 | bytes 17825792 | tf_op jit(solution)/shard_map/dot_general | solution.py:29
  175.1 3.8 convolution_convert_fusion.3.kn_ref.vn_ref
  179.1 8.6 %copy.129 = bf16[2048,8,256]{2,0,1:T(8,128)(2,1)} copy(bf16[2048,8,256]{2,1,0:T(8,128)(2,1)} %param.27) | data formatting | bytes 16777216 | tf_op args[10]
  187.8 38.0 %shard_map.242 = (bf16[512,1024]{1,0:T(8,128)(2,1)S(1)}, bf16[512,1024]{1,0:T(8,128)(2,1)}, f32[8,1,1024]{2,1,0:T(1,128)S(1)}, bf16[8,2048,1024]{2,1,0:T(8,128)(2,1)}) custom-call(bf16[512,1024]{1,0:T(8,128)(2,1)} %collective-permute-done.2.qa_ref, bf16[512,1024]{1,0:T(8,128)(2,1)} %collective-permute-done.3.qb_ref, bf16[8,2048,256]{2,1,0:T(8,128)(2,1)} %bitcast.148, ...), custom_call_target="tpu_custom_call" | custom-call | flops 8589934592 | bytes 67108864 | tf_op jit(solution)/shard_map/pallas_call | solution.py:488
  226.3 38.3 %shard_map.241 = (bf16[512,1024]{1,0:T(8,128)(2,1)S(1)}, bf16[512,1024]{1,0:T(8,128)(2,1)}, f32[8,1,1024]{2,1,0:T(1,128)S(1)}, bf16[8,2048,1024]{2,1,0:T(8,128)(2,1)}) custom-call(bf16[512,1024]{1,0:T(8,128)(2,1)S(1)} %convolution_convert_fusion.5.qa_ref.q_ref, bf16[512,1024]{1,0:T(8,128)(2,1)S(1)} %collective-permute-done.qb_ref, ...), custom_call_target="tpu_custom_call" | custom-call | flops 8589934592 | bytes 67108864 | tf_op jit(solution)/shard_map/pallas_call | solution.py:488
  267.6 3.6 fusion.30
  274.3 23.4 %shard_map.244 = (f32[512,1024]{1,0:T(8,128)S(1)}, bf16[8,1024,512]{2,1,0:T(8,128)(2,1)S(1)}) custom-call(s32[1]{0:T(128)S(6)} %copy.136.len_ref, f32[8,1,256]{2,1,0:T(1,128)S(1)} %broadcast_in_dim.32.near_ref, bf16[512,1024]{1,0:T(8,128)(2,1)S(1)} %convolution_convert_fusion.5.qa_ref.q_ref, bf16[512,2048]{1,0:T(8,128)(2,1)S(1)} %copy-done, ...), custom_call_target="tpu_custom_call" | custom-call | flops 2147483648 | bytes 20971520 | tf_op jit(solution)/shard_map/pallas_call | solution.py:657
  307.8 4.2 add_convert_fusion.4
  316.1 15.1 %fusion.6 = (bf16[512,4096]{1,0:T(8,128)(2,1)}, f32[512,4096]{1,0:T(8,128)}) fusion(f32[4096,512]{0,1:T(8,128)} %fusion.63, bf16[1024,4096]{1,0:T(8,128)(2,1)S(1)} %bitcast.186, f32[512,1024]{1,0:T(8,128)S(1)} %get-tuple-element.152, f32[1024]{0:T(1024)S(1)} %copy-done.49, f32[1024]{0:T(1024)S(1)} %mul.285, f32[512]{0:T(512)S(1)} %add_rsqrt_fusion, ...), kind=kOutput, calls=%fused_computation.8 | convolution fusion | flops 4339531776 | bytes 31469568 | tf_op jit(solution)/shard_map/dot_general | solution.py:29
  331.2 9.3 %multiply_reduce_fusion.1 = (f32[1024]{0:T(1024)S(1)}, f32[512]{0:T(512)S(1)}, f32[512]{0:T(512)S(1)}, f32[1024]{0:T(1024)S(1)}, f32[512,1024]{1,0:T(8,128)S(1)}) fusion(f32[512,1024]{1,0:T(8,128)S(1)} %get-tuple-element.152, f32[512]{0:T(512)S(1)} %add_rsqrt_fusion, f32[512]{0:T(512)S(1)} %broadcast_multiply_fusion.4, f32[1024]{0:T(1024)S(1)} %mul.285, ...), kind=kOutput, calls=%fused_computation.56 | convolution fusion | flops 4299682816 | bytes 16797696 | tf_op jit(solution)/shard_map/dot_general | solution.py:29
  352.0 12.6 %add_convert_fusion.2 = bf16[512,1024]{1,0:T(8,128)(2,1)} fusion(f32[512,1024]{1,0:T(8,128)} %copy-done.23, bf16[4096,1024]{1,0:T(8,128)(2,1)} %bitcast.182, f32[512,4096]{1,0:T(8,128)} %get-tuple-element.154), kind=kOutput, calls=%fused_computation.63 | convolution fusion | flops 4314890240 | bytes 19922944 | tf_op jit(solution)/shard_map/dot_general | solution.py:29
  364.6 13.0 %convolution_convert_fusion = bf16[4096,1024]{1,0:T(8,128)(2,1)} fusion(bf16[512,1024]{1,0:T(8,128)(2,1)S(1)} %copy-done.32, f32[512,4096]{1,0:T(8,128)} %get-tuple-element.154), kind=kOutput, calls=%fused_computation.16 | convolution fusion | flops 4318035968 | bytes 17825792 | tf_op jit(solution)/shard_map/tf,td->fd/dot_general | solution.py:825
  377.6 3.4 copy-done.4
  381.0 15.7 %shard_map.245 = (f32[512,1024]{1,0:T(8,128)S(1)}, bf16[512,1024]{1,0:T(8,128)(2,1)S(1)}, bf16[512,1024]{1,0:T(8,128)(2,1)S(1)}, f32[8,1,256]{2,1,0:T(1,128)S(1)}, f32[8,8,256]{2,1,0:T(8,128)S(1)}) custom-call(f32[8]{0:T(128)S(1)} %add_divide_fusion.open_ref, f32[512,1024]{1,0:T(8,128)S(1)} %copy-done.8, ...), custom_call_target="tpu_custom_call" | custom-call | flops 4294967296 | bytes 20971520 | tf_op jit(solution)/shard_map/pallas_call | solution.py:682
  400.9 4.7 convolution_convert_fusion.4
  410.9 20.6 %shard_map.247 = (bf16[512,1024]{1,0:T(8,128)(2,1)S(1)}, bf16[512,1024]{1,0:T(8,128)(2,1)S(1)}) custom-call(bf16[512,1024]{1,0:T(8,128)(2,1)} %collective-permute-done.12.ga_ref, bf16[512,1024]{1,0:T(8,128)(2,1)S(1)} %collective-permute-done.13.gb_ref, bf16[8,2048,256]{2,1,0:T(8,128)(2,1)} %bitcast.150, bf16[8,2048,1024]{2,1,0:T(8,128)(2,1)} %get-tuple-element.58.p_ref, ...), custom_call_target="tpu_custom_call" | custom-call | flops 8589934592 | bytes 67108864 | tf_op jit(solution)/shard_map/pallas_call | solution.py:518
  432.0 21.0 %shard_map.246 = (bf16[512,1024]{1,0:T(8,128)(2,1)S(1)}, bf16[512,1024]{1,0:T(8,128)(2,1)S(1)}) custom-call(bf16[512,1024]{1,0:T(8,128)(2,1)} %get-tuple-element.123.ga_ref, bf16[512,1024]{1,0:T(8,128)(2,1)} %collective-permute-done.9.gb_ref, bf16[8,2048,256]{2,1,0:T(8,128)(2,1)} %bitcast.151, bf16[8,2048,1024]{2,1,0:T(8,128)(2,1)} %get-tuple-element.55.p_ref, ...), custom_call_target="tpu_custom_call" | custom-call | flops 8589934592 | bytes 67108864 | tf_op jit(solution)/shard_map/pallas_call | solution.py:518
  455.4 7.5 %convolution_convert_fusion.1 = bf16[1024,4096]{1,0:T(8,128)(2,1)} fusion(bf16[512,4096]{1,0:T(8,128)(2,1)S(1)} %copy-done.58, f32[512,1024]{1,0:T(8,128)S(1)} %copy-done.24, f32[1024]{0:T(1024)S(1)} %copy-done.49, f32[1024]{0:T(1024)S(1)} %mul.285, f32[512]{0:T(512)S(1)} %add_rsqrt_fusion, f32[512]{0:T(512)S(1)} %broadcast_multiply_fusion.4), kind=kOutput, calls=%fused_computation.17 | convolution fusion | flops 4301783040 | bytes 14692352 | tf_op jit(solution)/shard_map/td,tf->df/dot_general | solution.py:828
  462.9 16.3 %collective-permute-done.17 = bf16[512,1024]{1,0:T(8,128)(2,1)S(1)} collective-permute-done((bf16[512,1024]{1,0:T(8,128)(2,1)S(1)}, bf16[512,1024]{1,0:T(8,128)(2,1)S(1)}, u32[]{:S(2)}, u32[]{:S(2)}) %collective-permute-start.17) | collective-permute-done | bytes 1048608 | tf_op jit(solution)/shard_map/ppermute | solution.py:732
  480.5 6.2 convolution_convert_fusion.2
  490.5 138.4 %shard_map.248 = (f32[32,3072]{1,0:T(8,128)}, f32[32,1024]{1,0:T(8,128)}, f32[32,4096]{1,0:T(8,128)}, f32[128,1024]{1,0:T(8,128)}, f32[40,128]{1,0:T(8,128)}) custom-call(bf16[32,32,3072]{2,1,0:T(8,128)(2,1)} %bitcast.160, bf16[32,32,1024]{2,1,0:T(8,128)(2,1)} %bitcast.161, bf16[32,32,4096]{2,1,0:T(8,128)(2,1)} %bitcast.153, ...), custom_call_target="tpu_custom_call" | custom-call | tf_op jit(solution)/shard_map/pallas_call | solution.py:408
  632.9 3.7 fusion.26
  (265 shorter events, 67.6 us)
Async XLA Ops:
  33.6 141.5 %copy-start.47 = (f32[1024]{0:T(1024)}, f32[1024]{0:T(1024)S(1)}, u32[]{:S(2)}) copy-start(f32[1024]{0:T(1024)S(1)} %add.127) | copy-start | bytes 12292
  33.6 141.4 %copy-start.42 = (f32[1024]{0:T(1024)}, f32[1024]{0:T(1024)S(1)}, u32[]{:S(2)}) copy-start(f32[1024]{0:T(1024)S(1)} %mul.260) | copy-start | bytes 12292
  35.1 140.0 %copy-start.40 = (f32[512]{0:T(512)}, f32[512]{0:T(512)S(1)}, u32[]{:S(2)}) copy-start(f32[512]{0:T(512)S(1)} %broadcast_multiply_fusion.5) | copy-start | bytes 6148
  35.5 139.6 %copy-start.45 = (f32[512]{0:T(512)}, f32[512]{0:T(512)S(1)}, u32[]{:S(2)}) copy-start(f32[512]{0:T(512)S(1)} %add_rsqrt_fusion.1) | copy-start | bytes 6148
  38.6 135.9 %collective-permute-start.2 = (bf16[512,1024]{1,0:T(8,128)(2,1)S(1)}, bf16[512,1024]{1,0:T(8,128)(2,1)}, u32[]{:S(2)}, u32[]{:S(2)}) collective-permute-start(bf16[512,1024]{1,0:T(8,128)(2,1)S(1)} %convolution_convert_fusion.5.qa_ref.q_ref), channel_id=1, source_target_pairs={{0,2},{1,3},{2,0},{3,1},{4,6},{5,7},{6,4},{7,5},{8,10},{9,11},{10,... | collective-permute-start | bytes 3145736 | tf_op jit(solution)/shard_map/ppermute | solution.py:732
  38.8 187.5 %collective-permute-start = (bf16[512,1024]{1,0:T(8,128)(2,1)S(1)}, bf16[512,1024]{1,0:T(8,128)(2,1)S(1)}, u32[]{:S(2)}, u32[]{:S(2)}) collective-permute-start(bf16[512,1024]{1,0:T(8,128)(2,1)S(1)} %convolution_convert_fusion.5.qa_ref.q_ref), channel_id=1, source_target_pairs={{0,1},{1,0},{2,3},{3,2},{4,5},{5,4},{6,7},{7,6},{8,9},{9,8},{10,11... | collective-permute-start | bytes 3145736 | tf_op jit(solution)/shard_map/ppermute | solution.py:732
  174.5 13.3 %collective-permute-start.3 = (bf16[512,1024]{1,0:T(8,128)(2,1)}, bf16[512,1024]{1,0:T(8,128)(2,1)}, u32[]{:S(2)}, u32[]{:S(2)}) collective-permute-start(bf16[512,1024]{1,0:T(8,128)(2,1)} %collective-permute-done.2.qa_ref), channel_id=1, source_target_pairs={{0,1},{1,0},{2,3},{3,2},{4,5},{5,4},{6,7},{7,6},{8,9},{9,8},{10,11... | collective-permute-start | bytes 3145736 | tf_op jit(solution)/shard_map/ppermute | solution.py:732
  225.7 38.9 %copy-start.13 = (bf16[512,1024]{1,0:T(8,128)(2,1)}, bf16[512,1024]{1,0:T(8,128)(2,1)S(1)}, u32[]{:S(2)}) copy-start(bf16[512,1024]{1,0:T(8,128)(2,1)S(1)} %get-tuple-element.46) | copy-start | bytes 3145732
  225.8 39.9 %collective-permute-start.4 = (f32[8,512]{1,0:T(8,128)S(1)}, f32[8,512]{1,0:T(8,128)S(1)}, u32[]{:S(2)}, u32[]{:S(2)}) collective-permute-start(f32[8,512]{1,0:T(8,128)S(1)} %slice.129), channel_id=1, source_target_pairs={{0,1},{1,0},{2,3},{3,2},{4,5},{5,4},{6,7},{7,6},{8,9},{9,8},{10,11... | collective-permute-start | bytes 49160 | tf_op jit(solution)/shard_map/ppermute | solution.py:732
  225.8 40.2 %collective-permute-start.7 = (bf16[512,1024]{1,0:T(8,128)(2,1)}, bf16[512,1024]{1,0:T(8,128)(2,1)S(1)}, u32[]{:S(2)}, u32[]{:S(2)}) collective-permute-start(bf16[512,1024]{1,0:T(8,128)(2,1)} %get-tuple-element.47), channel_id=1, source_target_pairs={{0,1},{1,0},{2,3},{3,2},{4,5},{5,4},{6,7},{7,6},{8,9},{9,8},{10,11... | collective-permute-start | bytes 3145736 | tf_op jit(solution)/shard_map/ppermute | solution.py:732
  265.6 39.4 %collective-permute-start.6 = (bf16[512,1024]{1,0:T(8,128)(2,1)}, bf16[512,1024]{1,0:T(8,128)(2,1)}, u32[]{:S(2)}, u32[]{:S(2)}) collective-permute-start(bf16[512,1024]{1,0:T(8,128)(2,1)} %get-tuple-element.45), channel_id=1, source_target_pairs={{0,1},{1,0},{2,3},{3,2},{4,5},{5,4},{6,7},{7,6},{8,9},{9,8},{10,11... | collective-permute-start | bytes 3145736 | tf_op jit(solution)/shard_map/ppermute | solution.py:732
  271.2 33.8 %collective-permute-start.8 = (bf16[512,1024]{1,0:T(8,128)(2,1)}, bf16[512,1024]{1,0:T(8,128)(2,1)}, u32[]{:S(2)}, u32[]{:S(2)}) collective-permute-start(bf16[512,1024]{1,0:T(8,128)(2,1)} %fusion.30), channel_id=1, source_target_pairs={{0,2},{1,3},{2,0},{3,1},{4,6},{5,7},{6,4},{7,5},{8,10},{9,11},{10,... | collective-permute-start | bytes 3145736 | tf_op jit(solution)/shard_map/ppermute | solution.py:732
  273.6 29.5 %collective-permute-start.1 = (f32[8,512]{1,0:T(8,128)S(1)}, f32[8,512]{1,0:T(8,128)S(1)}, u32[]{:S(2)}, u32[]{:S(2)}) collective-permute-start(f32[8,512]{1,0:T(8,128)S(1)} %slice.127), channel_id=1, source_target_pairs={{0,1},{1,0},{2,3},{3,2},{4,5},{5,4},{6,7},{7,6},{8,9},{9,8},{10,11... | collective-permute-start | bytes 49160 | tf_op jit(solution)/shard_map/ppermute | solution.py:732
  273.8 29.3 %collective-permute-start.5 = (f32[8,512]{1,0:T(8,128)S(1)}, f32[8,512]{1,0:T(8,128)S(1)}, u32[]{:S(2)}, u32[]{:S(2)}) collective-permute-start(f32[8,512]{1,0:T(8,128)S(1)} %get-tuple-element.127), channel_id=1, source_target_pairs={{0,2},{1,3},{2,0},{3,1},{4,6},{5,7},{6,4},{7,5},{8,10},{9,11},{10,... | collective-permute-start | bytes 49160 | tf_op jit(solution)/shard_map/ppermute | solution.py:732
  345.6 62.4 %collective-permute-start.12 = (bf16[512,1024]{1,0:T(8,128)(2,1)}, bf16[512,1024]{1,0:T(8,128)(2,1)}, u32[]{:S(2)}, u32[]{:S(2)}) collective-permute-start(bf16[512,1024]{1,0:T(8,128)(2,1)} %get-tuple-element.123.ga_ref), channel_id=1, source_target_pairs={{0,2},{1,3},{2,0},{3,1},{4,6},{5,7},{6,4},{7,5},{8,10},{9,11},{10,... | collective-permute-start | bytes 3145736 | tf_op jit(solution)/shard_map/ppermute | solution.py:732
  347.1 84.9 %collective-permute-start.9 = (bf16[512,1024]{1,0:T(8,128)(2,1)}, bf16[512,1024]{1,0:T(8,128)(2,1)}, u32[]{:S(2)}, u32[]{:S(2)}) collective-permute-start(bf16[512,1024]{1,0:T(8,128)(2,1)} %get-tuple-element.123.ga_ref), channel_id=1, source_target_pairs={{0,1},{1,0},{2,3},{3,2},{4,5},{5,4},{6,7},{7,6},{8,9},{9,8},{10,11... | collective-permute-start | bytes 3145736 | tf_op jit(solution)/shard_map/ppermute | solution.py:732
  351.2 57.1 %collective-permute-start.14 = (f32[16,512]{1,0:T(8,128)S(1)}, f32[16,512]{1,0:T(8,128)S(1)}, u32[]{:S(2)}, u32[]{:S(2)}) collective-permute-start(f32[16,512]{1,0:T(8,128)S(1)} %pad_maximum_fusion), channel_id=1, source_target_pairs={{0,2},{1,3},{2,0},{3,1},{4,6},{5,7},{6,4},{7,5},{8,10},{9,11},{10,... | collective-permute-start | bytes 98312 | tf_op jit(solution)/shard_map/ppermute | solution.py:732
  351.8 56.8 %collective-permute-start.10 = (f32[16,512]{1,0:T(8,128)S(1)}, f32[16,512]{1,0:T(8,128)S(1)}, u32[]{:S(2)}, u32[]{:S(2)}) collective-permute-start(f32[16,512]{1,0:T(8,128)S(1)} %pad_maximum_fusion), channel_id=1, source_target_pairs={{0,1},{1,0},{2,3},{3,2},{4,5},{5,4},{6,7},{7,6},{8,9},{9,8},{10,11... | collective-permute-start | bytes 98312 | tf_op jit(solution)/shard_map/ppermute | solution.py:732
  408.0 2.9 collective-permute-start.13
  408.3 2.4 collective-permute-start.15
  431.6 21.8 %collective-permute-start.16 = (bf16[512,1024]{1,0:T(8,128)(2,1)S(1)}, bf16[512,1024]{1,0:T(8,128)(2,1)S(1)}, u32[]{:S(2)}, u32[]{:S(2)}) collective-permute-start(bf16[512,1024]{1,0:T(8,128)(2,1)S(1)} %get-tuple-element.60), channel_id=1, source_target_pairs={{0,1},{1,0},{2,3},{3,2},{4,5},{5,4},{6,7},{7,6},{8,9},{9,8},{10,11... | collective-permute-start | bytes 3145736 | tf_op jit(solution)/shard_map/ppermute | solution.py:732
  453.1 9.8 %collective-permute-start.11 = (bf16[512,1024]{1,0:T(8,128)(2,1)S(1)}, bf16[512,1024]{1,0:T(8,128)(2,1)S(1)}, u32[]{:S(2)}, u32[]{:S(2)}) collective-permute-start(bf16[512,1024]{1,0:T(8,128)(2,1)S(1)} %get-tuple-element.57), channel_id=1, source_target_pairs={{0,1},{1,0},{2,3},{3,2},{4,5},{5,4},{6,7},{7,6},{8,9},{9,8},{10,11... | collective-permute-start | bytes 3145736 | tf_op jit(solution)/shard_map/ppermute | solution.py:732
  453.8 25.4 %collective-permute-start.17 = (bf16[512,1024]{1,0:T(8,128)(2,1)S(1)}, bf16[512,1024]{1,0:T(8,128)(2,1)S(1)}, u32[]{:S(2)}, u32[]{:S(2)}) collective-permute-start(bf16[512,1024]{1,0:T(8,128)(2,1)S(1)} %add_convert_fusion.1), channel_id=1, source_target_pairs={{0,2},{1,3},{2,0},{3,1},{4,6},{5,7},{6,4},{7,5},{8,10},{9,11},{10,... | collective-permute-start | bytes 3145736 | tf_op jit(solution)/shard_map/ppermute | solution.py:732
  490.5 142.4 %copy-start.26 = (f32[512,1024]{1,0:T(8,128)S(1)}, f32[512,1024]{1,0:T(8,128)}, u32[]{:S(2)}) copy-start(f32[512,1024]{1,0:T(8,128)} %copy-done.25) | copy-start | bytes 6291460
  (55 other events, 371.0 us)

commit v3 on v2

--- a/solution.py
+++ b/solution.py
@@ -103,8 +103,7 @@
         self.n = len(orders)
         self.first = [ALONG_Y if order == "zyx" else ALONG_X for order in orders]
         self.second = [ALONG_X if order == "zyx" else ALONG_Y for order in orders]
-        self.started = []
-        self.counts = [0] * self.n
+        self.sent = [[] for _ in orders]
 
     def spot(self, a, source):
         return self.outs[a].at[self.place.number(source)]
@@ -112,95 +111,64 @@
     def index(self, step):
         return ((step[0] * 2 + step[1]) * 2 + step[2]) * 2 + step[3]
 
+    def copy(self, a, k):
+        source, to = self.sent[a][k]
+        place = self.place
+        return pltpu.make_async_remote_copy(
+            src_ref=self.ins[a] if source == OWN else self.spot(a, source),
+            dst_ref=self.spot(a, source),
+            send_sem=self.send_sem.at[a, k],
+            recv_sem=self.recv_sem.at[a, self.index(place.minus(source, to))],
+            device_id=place.device(to),
+            device_id_type=MESH,
+        )
+
     def send(self, a, source, to):
-        place = self.place
-        self.started.append(
-            place.copy(
-                self.ins[a] if source == OWN else self.spot(a, source),
-                self.spot(a, source),
-                self.send_sem.at[a, self.counts[a]],
-                self.recv_sem.at[a, self.index(place.minus(source, to))],
-                place.device(to),
-            )
-        )
-        self.counts[a] += 1
+        self.sent[a].append((source, to))
+        self.copy(a, len(self.sent[a]) - 1).start()
+
+    def own(self, a):
+        return pltpu.make_async_copy(self.ins[a], self.spot(a, OWN), self.own_sem.at[a])
 
     def arrived(self, a, source):
         self.place.arrived(self.spot(a, source), self.recv_sem.at[a, self.index(source)])
 
-    def begin(self):
-        for a in range(self.n):
-            for to in self.place.partners()[:-1]:
-                self.send(a, OWN, to)
-        self.kept = []
-        for a in range(self.n):
-            self.send(a, OWN, ALONG_CORE)
-            copy = pltpu.make_async_copy(self.ins[a], self.spot(a, OWN), self.own_sem.at[a])
-            copy.start()
-            self.kept.append(copy)
-
-    def middle(self, z):
+    def begin(self, a):
+        for to in self.place.partners():
+            self.send(a, OWN, to)
+        self.own(a).start()
+
+    def middle(self, a, z):
         at = (z, 0, 0, 0)
         if z:
-            for a in range(self.n):
-                self.arrived(a, at)
-                for to in (self.first[a], self.second[a], ALONG_CORE):
-                    self.send(a, at, to)
-        for a in range(self.n):
-            source = self.place.plus(at, self.first[a])
+            self.arrived(a, at)
+            for to in (self.first[a], self.second[a], ALONG_CORE):
+                self.send(a, at, to)
+        source = self.place.plus(at, self.first[a])
+        self.arrived(a, source)
+        for to in (self.second[a], ALONG_CORE):
+            self.send(a, source, to)
+
+    def late(self, a, z):
+        for step in (self.second[a], self.place.plus(self.first[a], self.second[a])):
+            source = self.place.plus((z, 0, 0, 0), step)
             self.arrived(a, source)
-            for to in (self.second[a], ALONG_CORE):
-                self.send(a, source, to)
-
-    def late(self, z):
-        for a in range(self.n):
-            for step in (self.second[a], self.place.plus(self.first[a], self.second[a])):
-                source = self.place.plus((z, 0, 0, 0), step)
-                self.arrived(a, source)
-                self.send(a, source, ALONG_CORE)
-
-    def finish(self):
+            self.send(a, source, ALONG_CORE)
+
+    def finish(self, a):
         for z in near_first(self.place.sizes[0]):
             for y in range(2):
                 for x in range(2):
-                    for a in range(self.n):
-                        self.arrived(a, (z, y, x, 1))
-        for copy in self.started:
-            copy.wait_send()
-        for copy in self.kept:
-            copy.wait()
-
-
-def gather_scratch(n, n_hi):
+                    self.arrived(a, (z, y, x, 1))
+        for k in range(len(self.sent[a])):
+            self.copy(a, k).wait_send()
+        self.own(a).wait()
+
+
+def gather_sems(n, n_hi):
     sends = (n_hi - 1) + 3 + (n_hi - 1) * 3 + n_hi * 2 + n_hi * 2
     dma = pltpu.SemaphoreType.DMA
     return [dma((n, sends)), dma((n, n_hi * 8)), dma((n,))]
-
-
-def gather_kernel(n_hi, orders, *refs):
-    n = len(orders)
-    place = Place(n_hi)
-    place.greet()
-    gather = Gather(place, orders, refs[:n], refs[n : 2 * n], refs[2 * n :])
-    gather.begin()
-    for z in near_first(n_hi):
-        gather.middle(z)
-    for z in near_first(n_hi):
-        gather.late(z)
-    gather.finish()
-
-
-def gather_rows(arrays, orders, collective_id):
-    n = len(arrays)
-    n_hi = lax.axis_size("dp") // 2
-    return pl.pallas_call(
-        functools.partial(gather_kernel, n_hi, orders),
-        out_shape=[jax.ShapeDtypeStruct((n_hi * 8,) + a.shape, a.dtype) for a in arrays],
-        in_specs=[ANYWHERE] * n,
-        out_specs=[ANYWHERE] * n,
-        scratch_shapes=gather_scratch(n, n_hi),
-        compiler_params=pltpu.CompilerParams(collective_id=collective_id, has_side_effects=True),
-    )(*arrays)
 
 
 class Scatter:
@@ -421,20 +389,20 @@
     )(*arrays, small)
 
 
-def recall_kernel(qa_ref, qb_ref, mem_ref, slot_ref, outa_ref, outb_ref, lse_ref, p_ref):
-    slots, tokens = p_ref.shape[1], p_ref.shape[2]
-    half = tokens // 2
-    chosen = slot_ref[0]
+def pick_scores(queries, table_ref, chosen):
+    slots, step = table_ref.shape[1], 256
     low, high = chosen & 7, chosen >> 3
-    queries = jnp.concatenate([qa_ref[...], qb_ref[...]], axis=0)
-    step = 256
-    picked = jnp.zeros((8, tokens), F32)
+    picked = jnp.zeros(chosen.shape, F32)
     for at in range(0, slots, step):
-        scores = dot(mem_ref[0, pl.ds(at, step), pl.ds(0, HD)], queries, NT)
+        scores = dot(table_ref[0, pl.ds(at, step), pl.ds(0, HD)], queries, NT)
         for row in range(0, step, 8):
             got = jnp.take_along_axis(scores[row : row + 8], low, axis=0)
             picked = jnp.where(high == (at + row) // 8, got, picked)
-    scores = picked * SCALE
+    return picked * SCALE
+
+
+def recall_values(scores, table_ref, chosen, lse_ref, p_ref):
+    slots, tokens, step = table_ref.shape[1], chosen.shape[1], 256
     top = jnp.max(scores, axis=0, keepdims=True)
     weights = jnp.exp(scores - top)
     total = jnp.sum(weights, axis=0, keepdims=True)
@@ -445,7 +413,7 @@
     probs = (weights / total * times).astype(BF)
     rows = lax.broadcasted_iota(jnp.int32, (step, tokens), 0).astype(F32).astype(BF)
     out = jnp.zeros((HD, tokens), F32)
-    values_t = mem_ref[0, :, pl.ds(HD, HD)].T
+    values_t = table_ref[0, :, pl.ds(HD, HD)].T
     for at in range(0, slots, step):
         mine = jnp.where(chosen // step == at // step, chosen % step, -1).astype(F32).astype(BF)
         dense = jnp.zeros((step, tokens), BF)
@@ -453,9 +421,181 @@
             dense = jnp.where(rows == mine[j : j + 1], probs[j : j + 1], dense)
         p_ref[0, pl.ds(at, step), :] = dense
         out = out + dot(values_t[:, at : at + step], dense)
-    out = out.T.astype(BF)
-    outa_ref[...] = out[:half]
-    outb_ref[...] = out[half:]
+    return out.T.astype(BF)
+
+
+def attend_kernel(n_hi, orders, *refs):
+    n = len(orders) - 2
+    x_ref, table_ref, slot_ref = refs[:3]
+    early_in, late_in = refs[3:5], refs[5 : 5 + n]
+    normed_ref, q_ref, norms_ref, out_ref, lse_ref, p_ref, full_q = refs[5 + n : 12 + n]
+    late_out = refs[12 + n : 12 + 2 * n]
+    wq, norms, asked, keep_sem, q_send, q_recv = refs[12 + 2 * n : 18 + 2 * n]
+    sems = refs[18 + 2 * n :]
+    phase, head = pl.program_id(0), pl.program_id(1)
+    tick = phase * H + head
+    place = Place(n_hi)
+    early = Gather(place, orders[:2], early_in, (wq, norms), sems[:3])
+    late = Gather(place, orders[2:], late_in, late_out, sems[3:])
+    zs = near_first(n_hi)
+    rows = x_ref.shape[0]
+
+    def ask(src, slot, to):
+        return pltpu.make_async_remote_copy(
+            src_ref=src,
+            dst_ref=asked.at[slot],
+            send_sem=q_send.at[slot],
+            recv_sem=q_recv.at[slot],
+            device_id=place.device(to),
+            device_id_type=MESH,
+        )
+
+    def keep():
+        return pltpu.make_async_copy(wq, full_q, keep_sem)
+
+    @pl.when(tick == 0)
+    def _():
+        place.greet()
+        for a in range(2):
+            early.begin(a)
+        x = x_ref[...].astype(F32)
+        center = x - jnp.mean(x, axis=-1, keepdims=True)
+        scaled = center * lax.rsqrt(jnp.mean(center * center, axis=-1, keepdims=True) + EPSILON)
+        for z in zs:
+            for a in range(2):
+                early.middle(a, z)
+        for z in zs:
+            for a in range(2):
+                early.late(a, z)
+        for a in range(2):
+            early.finish(a)
+        keep().start()
+        share = norms.shape[0] // H
+        lanes = [
+            functools.reduce(jnp.add, [norms[g * share + k].astype(F32) for k in range(share)])
+            for g in range(H)
+        ]
+        norm_rows = jnp.concatenate(lanes, axis=1)
+        norms_ref[...] = norm_rows
+        normed = (scaled * norm_rows[0:1] + norm_rows[2:3]).astype(BF)
+        normed_ref[...] = normed
+        for at in range(0, wq.shape[2], 256):
+            weights = wq[:, :, pl.ds(at, 256)]
+            if weights.shape[1] % 16:
+                weights = weights.astype(F32)
+            weights = weights.reshape(-1, 256).astype(BF)
+            q_ref[:, pl.ds(at, 256)] = dot(normed, weights).astype(BF)
+        ask(q_ref, 1, ALONG_CORE).start()
+        ask(q_ref, 2, ALONG_X).start()
+        for a in range(n):
+            late.begin(a)
+        asked[0] = q_ref[...]
+        place.arrived(asked.at[1], q_recv.at[1])
+
+    events = []
+    for a in range(n + 1):
+        for z in zs:
+            if a < n:
+                events.append(functools.partial(late.middle, a, z))
+            if a > 0:
+                events.append(functools.partial(late.late, a - 1, z))
+    ticks = 2 * H
+
+    def slot(at):
+        count = 2 * ticks - 2
+        mine = events[len(events) * (at - 2) // count : len(events) * (at - 1) // count]
+        if at >= 2 and mine:
+
+            @pl.when(tick == at // 2)
+            def _():
+                for event in mine:
+                    event()
+
+    for at in range(0, 2 * ticks, 2):
+        slot(at)
+
+    @pl.when(tick == H)
+    def _():
+        place.arrived(asked.at[3], q_recv.at[3])
+
+    queries = asked[pl.ds(phase * 2, 2), :, pl.ds(pl.multiple_of(head * HD, HD), HD)]
+    chosen = slot_ref[0]
+    scores = pick_scores(queries.reshape(2 * rows, HD), table_ref, chosen)
+
+    @pl.when(tick == H - 2)
+    def _():
+        place.arrived(asked.at[2], q_recv.at[2])
+        ask(asked.at[2], 3, ALONG_CORE).start()
+
+    for at in range(1, 2 * ticks, 2):
+        slot(at)
+    out_ref[...] = recall_values(scores, table_ref, chosen, lse_ref, p_ref)
+
+    @pl.when(tick == ticks - 1)
+    def _():
+        for a in range(n):
+            late.finish(a)
+        ask(q_ref, 1, ALONG_CORE).wait_send()
+        ask(q_ref, 2, ALONG_X).wait_send()
+        ask(asked.at[2], 3, ALONG_CORE).wait_send()
+        keep().wait()
+
+
+def attend(x, table, chosen, early, late, orders, collective_id):
+    n, n_hi = len(late), lax.axis_size("dp") // 2
+    devices = n_hi * 8
+    (rows, width), slots = x.shape, table.shape[1]
+    whole = pl.BlockSpec((rows, width), lambda p, h: (0, 0))
+    dma = pltpu.SemaphoreType.DMA
+
+    def gathered(a):
+        return jax.ShapeDtypeStruct((devices,) + a.shape, a.dtype)
+
+    return pl.pallas_call(
+        functools.partial(attend_kernel, n_hi, orders),
+        grid=(2, H),
+        in_specs=[
+            whole,
+            pl.BlockSpec((1, slots, 2 * HD), lambda p, h: (h, 0, 0)),
+            pl.BlockSpec((1, 8, 2 * rows), lambda p, h: (h, 0, p)),
+        ]
+        + [ANYWHERE] * (2 + n),
+        out_specs=[
+            whole,
+            whole,
+            pl.BlockSpec((16, width), lambda p, h: (0, 0)),
+            pl.BlockSpec((2 * rows, HD), lambda p, h: (p, h)),
+            pl.BlockSpec((1, 1, 2 * rows), lambda p, h: (h, 0, p)),
+            pl.BlockSpec((1, slots, 2 * rows), lambda p, h: (p * H + h, 0, 0)),
+        ]
+        + [ANYWHERE] * (1 + n),
+        out_shape=[
+            jax.ShapeDtypeStruct(x.shape, BF),
+            jax.ShapeDtypeStruct(x.shape, BF),
+            jax.ShapeDtypeStruct((16, width), F32),
+            jax.ShapeDtypeStruct((4 * rows, width), BF),
+            jax.ShapeDtypeStruct((H, 1, 4 * rows), F32),
+            jax.ShapeDtypeStruct((2 * H, slots, 2 * rows), BF),
+            gathered(early[0]),
+        ]
+        + [gathered(a) for a in late],
+        scratch_shapes=[
+            pltpu.VMEM((devices,) + early[0].shape, BF),
+            pltpu.VMEM((devices,) + early[1].shape, BF),
+            pltpu.VMEM((4, rows, width), BF),
+            dma(()),
+            dma((4,)),
+            dma((4,)),
+        ]
+        + gather_sems(2, n_hi)
+        + gather_sems(n, n_hi),
+        compiler_params=pltpu.CompilerParams(
+            collective_id=collective_id, has_side_effects=True, vmem_limit_bytes=52 << 20
+        ),
+        cost_estimate=pl.CostEstimate(
+            flops=16 * rows * slots * HD * H, bytes_accessed=128 << 20, transcendentals=0
+        ),
+    )(x, table, chosen, *early, *late)
 
 
 def recall_grad_kernel(ga_ref, gb_ref, mem_ref, p_ref, delta_ref, share_ref, outa_ref, outb_ref):
@@ -483,37 +623,7 @@
     return pl.BlockSpec((1,) + shape, lambda h: (h,) + (0,) * len(shape))
 
 
-def recall(query_a, query_b, table, chosen):
-    rows, slots = query_a.shape[0], table.shape[1]
-    return pl.pallas_call(
-        recall_kernel,
-        grid=(H,),
-        in_specs=[
-            head_columns(rows),
-            head_columns(rows),
-            per_head(slots, 2 * HD),
-            per_head(8, 2 * rows),
-        ],
-        out_specs=[
-            head_columns(rows),
-            head_columns(rows),
-            per_head(1, 2 * rows),
-            per_head(slots, 2 * rows),
-        ],
-        out_shape=[
-            jax.ShapeDtypeStruct(query_a.shape, BF),
-            jax.ShapeDtypeStruct(query_a.shape, BF),
-            jax.ShapeDtypeStruct((H, 1, 2 * rows), F32),
-            jax.ShapeDtypeStruct((H, slots, 2 * rows), BF),
-        ],
-        compiler_params=pltpu.CompilerParams(vmem_limit_bytes=48 << 20),
-        cost_estimate=pl.CostEstimate(
-            flops=8 * rows * slots * HD * H, bytes_accessed=64 << 20, transcendentals=0
-        ),
-    )(query_a, query_b, table, chosen)
-
-
-def recall_grad(grad_a, grad_b, table, probs, delta, share):
+def recall_grad(grad_a, grad_b, table, probs, first, delta, share):
     rows, slots = grad_a.shape[0], table.shape[1]
     return pl.pallas_call(
         recall_grad_kernel,
@@ -522,7 +632,7 @@
             head_columns(rows),
             head_columns(rows),
             per_head(slots, 2 * HD),
-            per_head(slots, 2 * rows),
+            pl.BlockSpec((1, slots, 2 * rows), lambda h: (first + h, 0, 0)),
             per_head(1, 2 * rows),
             per_head(1, 2 * rows),
         ],
@@ -765,40 +875,35 @@
     groups = lax.axis_size("mem")
     me = lax.axis_index("mem")
 
+    devices = lax.axis_size("dp") * groups
+    number = lax.axis_index("dp") * groups + me
+    own = norm_gains.shape[1]
     norms = jnp.pad(
-        jnp.concatenate([norm_gains, norm_shifts], axis=0),
-        ((0, 12), (0, 128 - norm_gains.shape[1])),
-    )
-    full_q, full_norms = gather_rows([w_qkv[:, :width], norms], ("zyx", "zxy"), 0)
-    full_kv, full_out, full_up, full_down = gather_rows(
-        [w_qkv[:, width:], w_out, w_up, w_down], ("zxy", "zyx", "zyx", "zxy"), 1
-    )
-    full_q, full_kv, full_out, full_up, full_down = [
-        full.reshape(-1, full.shape[2]) for full in (full_q, full_kv, full_out, full_up, full_down)
-    ]
-    rows = full_norms[:, :4, : norm_gains.shape[1]].astype(F32)
-    rows = rows.transpose(1, 0, 2).reshape(4, width)
-    gain_rows, shift_rows = rows[:2], rows[2:]
-
-    inputs = tokens.astype(F32)
-    normed_one, scaled_one, inverse_one = norm_forward(inputs, gain_rows[0], shift_rows[0])
-    normed_one = normed_one.astype(BF)
-    queries = dot(normed_one, full_q).astype(BF)
-    query_core, query_x = swap(queries, 1), swap(queries, 2)
-    query_cross = swap(query_x, 1)
-
+        jnp.concatenate([norm_gains, norm_shifts], axis=0), ((0, 12), (0, 128 - own))
+    )
+    norms = jnp.roll(norms, number % (128 // own) * own, axis=1)
     table = memory.transpose(1, 0, 2)
-    slot_rows = (slot_index - me * slot_count).reshape(groups, count, H, -1).transpose(0, 2, 3, 1)
+    slot_rows = (slot_index - me * slot_count).reshape(groups, count, H, -1)
     picks = [
         lax.dynamic_index_in_dim(slot_rows, me ^ turn, 0, keepdims=False) for turn in range(groups)
     ]
-    out_own, out_core, lse_chip, probs_chip = recall(
-        queries, query_core, table, jnp.concatenate(picks[:2], axis=-1)
-    )
-    out_x, out_cross, lse_far, probs_far = recall(
-        query_x, query_cross, table, jnp.concatenate(picks[2:], axis=-1)
-    )
-    lse_chip, lse_far = lse_chip[:, 0], lse_far[:, 0]
+    chosen = jnp.stack(picks).transpose(2, 3, 0, 1).reshape(H, -1, groups * count)
+    normed_one, queries, norm_rows, out_all, lse_all, probs_all, *full = attend(
+        tokens,
+        table,
+        chosen,
+        (w_qkv[:, :width], norms),
+        (w_qkv[:, width:], w_out, w_up, w_down),
+        ("zyx", "zxy", "zxy", "zyx", "zyx", "zxy"),
+        0,
+    )
+    full_q, full_kv, full_out, full_up, full_down = [f.reshape(-1, f.shape[2]) for f in full]
+    gain_rows, shift_rows = norm_rows[:2], norm_rows[2:4]
+    out_own, out_core, out_x, out_cross = jnp.split(out_all, groups)
+    lse_chip, lse_far = lse_all[:, 0, : 2 * count], lse_all[:, 0, 2 * count :]
+
+    inputs = tokens.astype(F32)
+    _, scaled_one, inverse_one = norm_forward(inputs, gain_rows[0], shift_rows[0])
     keys_values = dot(normed_one, full_kv).astype(BF)
     local_out, probs_local = segment_forward(
         queries, keys_values, xl_cache, near_bias(rel_table), seg_len
@@ -851,20 +956,21 @@
     )
     grad_table = table_gradient(diagonals, totals)
 
-    def recall_back(left, right, lse, probs):
+    def recall_back(left, right, lse, first):
         delta_rows = jnp.concatenate([left[1][:H], right[1][:H]], axis=1)
         total_rows = jnp.concatenate([left[1][H:], right[1][H:]], axis=1)
         return recall_grad(
             left[0],
             right[0],
             table,
-            probs,
+            probs_all,
+            first,
             delta_rows[:, None],
             jnp.exp(lse - total_rows)[:, None],
         )
 
-    back_x, back_cross = recall_back(sent_x, sent_cross, lse_far, probs_far)
-    back_own, back_core = recall_back(sent, sent_core, lse_chip, probs_chip)
+    back_x, back_cross = recall_back(sent_x, sent_cross, lse_far, H)
+    back_own, back_core = recall_back(sent, sent_core, lse_chip, 0)
     pair_back = (back_x.astype(F32) + swap(back_cross, 1).astype(F32)).astype(BF)
     grad_query = (
         grad_query_local
@@ -888,7 +994,6 @@
             jnp.sum(grad_normed_two, axis=0),
         ]
     )
-    devices = lax.axis_size("dp") * groups
     rest = jnp.pad(jnp.concatenate([grad_table.reshape(-1), grad_gate]), (0, 1024 - 264))
     small = jnp.concatenate([grad_norms.reshape(-1, 128), rest.reshape(-1, 128)], axis=0)
     share_qkv, share_out, share_up, share_down, small = scatter_sums(
@@ -900,9 +1005,9 @@
         small,
         2,
     )
-    own = norm_gains.shape[1]
-    at = (lax.axis_index("dp") * groups + me) * own
-    share_norms = lax.dynamic_slice_in_dim(small[:32].reshape(4, width), at, own, axis=1)
+    share_norms = lax.dynamic_slice_in_dim(
+        small[:32].reshape(4, width), number * own, own, axis=1
+    )
     rest = small[32:].reshape(-1)
     table_total, gate_total = rest[: BUCKETS * H].reshape(BUCKETS, H), rest[BUCKETS * H :][:H]
     return (

time: 649 us -> 610 us (0.940)
  Pallas kernels: 446 us -> 408 us
    pallas_call x4 -> x1, Pallas kernels: 227 us -> 211 us  [attend(): pl.pallas_call(functools.partial(attend_kernel, n_hi, orders), grid=(2, H...]
    pallas_call x1, Pallas kernels: 138 us -> 125 us  [scatter_sums(): pl.pallas_call(functools.partial(scatter_kernel, n_hi, orders), out_shape...]
    pallas_call x1, Pallas kernels: 23.4 us -> 13.9 us  [segment_forward(): pl.pallas_call(segment_kernel, grid=(H,), in_specs=[SCALARS, per_head(1,...]
    ppermute x18 -> x15, waiting for transfers between devices: 18.5 us -> 23.8 us  [swap(): lax.ppermute(v, 'mem', [(i, i ^ turn) for i in range(lax.axis_size('mem'))])]
    dot_general x10 -> x9, matrix products: 65.5 us -> 61.7 us  [dot(): return lax.dot_general(left, right, dims, preferred_element_type=F32)]
    unnamed x131 -> x135, local copies, waits for them, and re-layouts: 29.5 us -> 30.3 us
  transfers between devices with their start and end apart: 18 -> 15, of which waited for: 2 -> 4; matrix products, arithmetic and copies ran while one was open for 12% -> 12% of each run, Pallas kernels for 44% -> 12%
where the time goes in v3:
time: 610 us; the launch traced here: 600 us
  Pallas kernels  408 us (67%)
  matrix products  93.2 us (15%)
  local copies, waits for them, and re-layouts  45.1 us (7%)
  waiting for transfers between devices  23.8 us (4%)
  other arithmetic  20.6 us (3%)
  starting transfers between devices  6.94 us (1%)
    pallas_call x1, Pallas kernels, attend(): pl.pallas_call(functools.partial(attend_kernel, n_hi, orders), grid=(2, H...  211 us
    pallas_call x1, Pallas kernels, scatter_sums(): pl.pallas_call(functools.partial(scatter_kernel, n_hi, orders), out_shape...  125 us
    dot_general x9, matrix products, dot(): return lax.dot_general(left, right, dims, preferred_element_type=F32)  61.7 us
    pallas_call x2, Pallas kernels, recall_grad(): pl.pallas_call(recall_grad_kernel, grid=(H,), in_specs=[head_columns(rows...  42.2 us
    unnamed x135, local copies, waits for them, and re-layouts  30.3 us
    ppermute x15, waiting for transfers between devices, swap(): lax.ppermute(v, 'mem', [(i, i ^ turn) for i in range(lax.axis_size('mem'))])  23.8 us
    pallas_call x1, Pallas kernels, segment_backward(): pl.pallas_call(segment_grad_kernel, grid=(H,), in_specs=[SCALARS, head_co...  15.7 us
    pallas_call x1, Pallas kernels, segment_forward(): pl.pallas_call(segment_kernel, grid=(H,), in_specs=[SCALARS, per_head(1,...  13.9 us
  transfers between devices with their start and end apart: 15, of which 4 were waited for; matrix products, arithmetic and copies ran while one was open for 12% of the time, Pallas kernels for 12%

profile of v3, /device:TPU:0, one launch (start us, length us, event | category | flops | bytes accessed | tf_op | source)
XLA Modules:
  0.0 600.0 jit_solution(1796151826036106970)
XLA Ops:
  2.5 8.5 %copy.129 = bf16[2048,8,256]{2,0,1:T(8,128)(2,1)} copy(bf16[2048,8,256]{2,1,0:T(8,128)(2,1)} %param.27) | data formatting | bytes 16777216 | tf_op args[10]
  12.0 211.1 %shard_map.240 = (bf16[512,1024]{1,0:T(8,128)(2,1)}, bf16[512,1024]{1,0:T(8,128)(2,1)}, f32[16,1024]{1,0:T(8,128)S(1)}, bf16[2048,1024]{1,0:T(8,128)(2,1)}, f32[...) custom-call(bf16[512,1024]{1,0:T(8,128)(2,1)} %refs_0_.1, ...), custom_call_target="tpu_custom_call" | custom-call | flops 17179869184 | bytes 134217728 | tf_op jit(solution)/shard_map/pallas_call | solution.py:554
  228.8 6.0 %convolution_convert_fusion.3.kn_ref.vn_ref = bf16[512,2048]{1,0:T(8,128)(2,1)} fusion(bf16[512,1024]{1,0:T(8,128)(2,1)S(1)} %copy-done.57, bf16[1024,2048]{1,0:T(8,128)(2,1)} %bitcast.178), kind=kOutput, calls=%fused_computation.27 | convolution fusion | flops 2148532224 | bytes 7340032 | tf_op jit(solution)/shard_map/dot_general | solution.py:29
  234.8 7.0 %fusion.58 = f32[4096,512]{0,1:T(8,128)} fusion(bf16[4096,1024]{1,0:T(8,128)(2,1)S(1)} %bitcast.173, bf16[512,1024]{1,0:T(8,128)(2,1)S(1)} %copy-done.32), kind=kOutput, calls=%fused_computation.150 | convolution fusion | flops 4294967296 | bytes 17825792 | tf_op jit(solution)/shard_map/dot_general | solution.py:29
  244.5 4.0 fusion.27
  251.4 13.9 %shard_map.241 = (f32[512,1024]{1,0:T(8,128)S(1)}, bf16[8,1024,512]{2,1,0:T(8,128)(2,1)S(1)}) custom-call(s32[1]{0:T(128)S(6)} %copy.134.len_ref, f32[8,1,256]{2,1,0:T(1,128)S(1)} %broadcast_in_dim.32.near_ref, bf16[512,1024]{1,0:T(8,128)(2,1)S(1)} %copy-done.9, bf16[512,2048]{1,0:T(8,128)(2,1)S(1)} %copy-done, bf16[512,2048]{1,0:T(8,128)(2,1)S(1)} %copy-done.1, ...), custom_call_target="tpu_custom_call" | custom-call | flops 2147483648 | bytes 20971520 | tf_op jit(solution)/shard_map/pallas_call | solution.py:767
  269.9 4.2 collective-permute-done.2
  278.6 4.4 add_convert_fusion.4
  283.0 3.3 fusion.57
  287.1 15.6 %fusion.6 = (bf16[512,4096]{1,0:T(8,128)(2,1)}, f32[512,4096]{1,0:T(8,128)}) fusion(f32[4096,512]{0,1:T(8,128)} %fusion.58, bf16[1024,4096]{1,0:T(8,128)(2,1)S(1)} %bitcast.177, f32[512,1024]{1,0:T(8,128)S(1)} %get-tuple-element.161, f32[1024]{0:T(1024)S(1)} %bitcast.163, f32[1024]{0:T(1024)S(1)} %bitcast.157, f32[512]{0:T(512)S(1)} %add_rsqrt_fusion.1, ...), kind=kOutput, calls=%fused_computation.8 | convolution fusion | flops 4339531776 | bytes 31469568 | tf_op jit(solution)/shard_map/dot_general | solution.py:29
  302.6 9.1 %multiply_reduce_fusion.1 = (f32[1024]{0:T(1024)S(1)}, f32[512]{0:T(512)S(1)}, f32[512]{0:T(512)S(1)}, f32[1024]{0:T(1024)S(1)}, f32[512,1024]{1,0:T(8,128)S(1)}) fusion(f32[512,1024]{1,0:T(8,128)S(1)} %get-tuple-element.161, f32[512]{0:T(512)S(1)} %add_rsqrt_fusion.1, f32[512]{0:T(512)S(1)} %broadcast_multiply_fusion.5, f32[1024]{0:T(1024)S(1)} %bitcast.158, ...), kind=kOutput, calls=%fused_computation.53 | convolution fusion | flops 4299682816 | bytes 16797696 | tf_op jit(solution)/shard_map/dot_general | solution.py:29
  322.9 12.6 %add_convert_fusion.2 = bf16[512,1024]{1,0:T(8,128)(2,1)} fusion(f32[512,1024]{1,0:T(8,128)} %copy-done.24, bf16[4096,1024]{1,0:T(8,128)(2,1)} %bitcast.170, f32[512,4096]{1,0:T(8,128)} %get-tuple-element.163), kind=kOutput, calls=%fused_computation.60 | convolution fusion | flops 4314890240 | bytes 19922944 | tf_op jit(solution)/shard_map/dot_general | solution.py:29
  335.5 13.2 %convolution_convert_fusion = bf16[4096,1024]{1,0:T(8,128)(2,1)} fusion(bf16[512,1024]{1,0:T(8,128)(2,1)S(1)} %copy-done.34, f32[512,4096]{1,0:T(8,128)} %get-tuple-element.163), kind=kOutput, calls=%fused_computation.16 | convolution fusion | flops 4318035968 | bytes 17825792 | tf_op jit(solution)/shard_map/tf,td->fd/dot_general | solution.py:930
  348.7 3.4 copy-done.4
  352.1 15.7 %shard_map.242 = (f32[512,1024]{1,0:T(8,128)S(1)}, bf16[512,1024]{1,0:T(8,128)(2,1)S(1)}, bf16[512,1024]{1,0:T(8,128)(2,1)S(1)}, f32[8,1,256]{2,1,0:T(1,128)S(1)}, f32[8,8,256]{2,1,0:T(8,128)S(1)}) custom-call(f32[8]{0:T(128)S(1)} %add_divide_fusion.open_ref, f32[512,1024]{1,0:T(8,128)S(1)} %copy-done.8, bf16[512,1024]{1,0:T(8,128)(2,1)S(1)} %copy-done.10, ...), custom_call_target="tpu_custom_call" | custom-call | flops 4294967296 | bytes 20971520 | tf_op jit(solution)/shard_map/pallas_call | solution.py:792
  371.7 4.7 convolution_convert_fusion.4
  376.5 3.7 fusion.30
  383.5 21.3 %shard_map.244 = (bf16[512,1024]{1,0:T(8,128)(2,1)S(1)}, bf16[512,1024]{1,0:T(8,128)(2,1)}) custom-call(bf16[512,1024]{1,0:T(8,128)(2,1)} %collective-permute-done.9.ga_ref, bf16[512,1024]{1,0:T(8,128)(2,1)S(1)} %collective-permute-done.10.gb_ref, bf16[8,2048,256]{2,1,0:T(8,128)(2,1)} %bitcast.136, bf16[16,2048,1024]{2,1,0:T(8,128)(2,1)} %get-tuple-element.49.p_ref, ...), custom_call_target="tpu_custom_call" | custom-call | flops 8589934592 | bytes 67108864 | tf_op jit(solution)/shard_map/pallas_call | solution.py:628
  405.4 20.9 %shard_map.243 = (bf16[512,1024]{1,0:T(8,128)(2,1)S(1)}, bf16[512,1024]{1,0:T(8,128)(2,1)S(1)}) custom-call(bf16[512,1024]{1,0:T(8,128)(2,1)S(1)} %get-tuple-element.123.ga_ref, bf16[512,1024]{1,0:T(8,128)(2,1)} %collective-permute-done.6.gb_ref, bf16[8,2048,256]{2,1,0:T(8,128)(2,1)} %bitcast.137, bf16[16,2048,1024]{2,1,0:T(8,128)(2,1)} %get-tuple-element.49.p_ref, ...), custom_call_target="tpu_custom_call" | custom-call | flops 8589934592 | bytes 67108864 | tf_op jit(solution)/shard_map/pallas_call | solution.py:628
  427.9 7.6 %convolution_convert_fusion.1 = bf16[1024,4096]{1,0:T(8,128)(2,1)} fusion(bf16[512,4096]{1,0:T(8,128)(2,1)S(1)} %copy-done.59, f32[512,1024]{1,0:T(8,128)S(1)} %copy-done.25, f32[1024]{0:T(1024)S(1)} %bitcast.164, f32[1024]{0:T(1024)S(1)} %bitcast.160, f32[512]{0:T(512)S(1)} %add_rsqrt_fusion.1, f32[512]{0:T(512)S(1)} %broadcast_multiply_fusion.5), kind=kOutput, calls=%fused_computation.17 | convolution fusion | flops 4301783040 | bytes 14692352 | tf_op jit(solution)/shard_map/td,tf->df/dot_general | solution.py:933
  435.4 17.0 %collective-permute-done.14 = bf16[512,1024]{1,0:T(8,128)(2,1)S(1)} collective-permute-done((bf16[512,1024]{1,0:T(8,128)(2,1)S(1)}, bf16[512,1024]{1,0:T(8,128)(2,1)S(1)}, u32[]{:S(2)}, u32[]{:S(2)}) %collective-permute-start.14) | collective-permute-done | bytes 1048608 | tf_op jit(solution)/shard_map/ppermute | solution.py:842
  454.3 5.9 convolution_convert_fusion.2
  464.0 125.1 %shard_map.245 = (f32[32,3072]{1,0:T(8,128)}, f32[32,1024]{1,0:T(8,128)}, f32[32,4096]{1,0:T(8,128)}, f32[128,1024]{1,0:T(8,128)}, f32[40,128]{1,0:T(8,128)}) custom-call(bf16[32,32,3072]{2,1,0:T(8,128)(2,1)} %bitcast.146, bf16[32,32,1024]{2,1,0:T(8,128)(2,1)} %bitcast.147, bf16[32,32,4096]{2,1,0:T(8,128)(2,1)} %bitcast.139, ...), custom_call_target="tpu_custom_call" | custom-call | tf_op jit(solution)/shard_map/pallas_call | solution.py:376
  593.2 3.7 fusion.23
  (252 shorter events, 55.8 us)
Async XLA Ops:
  223.2 19.7 %collective-permute-start.1 = (f32[8,512]{1,0:T(8,128)S(1)}, f32[8,512]{1,0:T(8,128)S(1)}, u32[]{:S(2)}, u32[]{:S(2)}) collective-permute-start(f32[8,512]{1,0:T(8,128)S(1)} %slice.121), channel_id=1, source_target_pairs={{0,1},{1,0},{2,3},{3,2},{4,5},{5,4},{6,7},{7,6},{8,9},{9,8},{10,11... | collective-permute-start | bytes 49160 | tf_op jit(solution)/shard_map/ppermute | solution.py:842
  226.5 16.7 %collective-permute-start.4 = (bf16[512,1024]{1,0:T(8,128)(2,1)}, bf16[512,1024]{1,0:T(8,128)(2,1)S(1)}, u32[]{:S(2)}, u32[]{:S(2)}) collective-permute-start(bf16[512,1024]{1,0:T(8,128)(2,1)} %get-tuple-element.132), channel_id=1, source_target_pairs={{0,1},{1,0},{2,3},{3,2},{4,5},{5,4},{6,7},{7,6},{8,9},{9,8},{10,11... | collective-permute-start | bytes 3145736 | tf_op jit(solution)/shard_map/ppermute | solution.py:842
  227.0 42.9 %collective-permute-start = (f32[8,512]{1,0:T(8,128)S(1)}, f32[8,512]{1,0:T(8,128)S(1)}, u32[]{:S(2)}, u32[]{:S(2)}) collective-permute-start(f32[8,512]{1,0:T(8,128)S(1)} %slice.118), channel_id=1, source_target_pairs={{0,1},{1,0},{2,3},{3,2},{4,5},{5,4},{6,7},{7,6},{8,9},{9,8},{10,11... | collective-permute-start | bytes 49160 | tf_op jit(solution)/shard_map/ppermute | solution.py:842
  227.0 49.0 %collective-permute-start.3 = (bf16[512,1024]{1,0:T(8,128)(2,1)}, bf16[512,1024]{1,0:T(8,128)(2,1)}, u32[]{:S(2)}, u32[]{:S(2)}) collective-permute-start(bf16[512,1024]{1,0:T(8,128)(2,1)} %get-tuple-element.131), channel_id=1, source_target_pairs={{0,1},{1,0},{2,3},{3,2},{4,5},{5,4},{6,7},{7,6},{8,9},{9,8},{10,11... | collective-permute-start | bytes 3145736 | tf_op jit(solution)/shard_map/ppermute | solution.py:842
  248.5 27.6 %collective-permute-start.5 = (bf16[512,1024]{1,0:T(8,128)(2,1)}, bf16[512,1024]{1,0:T(8,128)(2,1)}, u32[]{:S(2)}, u32[]{:S(2)}) collective-permute-start(bf16[512,1024]{1,0:T(8,128)(2,1)} %fusion.27), channel_id=1, source_target_pairs={{0,2},{1,3},{2,0},{3,1},{4,6},{5,7},{6,4},{7,5},{8,10},{9,11},{10,... | collective-permute-start | bytes 3145736 | tf_op jit(solution)/shard_map/ppermute | solution.py:842
  249.3 24.9 %collective-permute-start.2 = (f32[8,512]{1,0:T(8,128)S(1)}, f32[8,512]{1,0:T(8,128)S(1)}, u32[]{:S(2)}, u32[]{:S(2)}) collective-permute-start(f32[8,512]{1,0:T(8,128)S(1)} %get-tuple-element.127), channel_id=1, source_target_pairs={{0,2},{1,3},{2,0},{3,1},{4,6},{5,7},{6,4},{7,5},{8,10},{9,11},{10,... | collective-permute-start | bytes 49160 | tf_op jit(solution)/shard_map/ppermute | solution.py:842
  286.3 25.4 %copy-start.24 = (f32[512,1024]{1,0:T(8,128)}, f32[512,1024]{1,0:T(8,128)S(1)}, u32[]{:S(2)}) copy-start(f32[512,1024]{1,0:T(8,128)S(1)} %get-tuple-element.161) | copy-start | bytes 6291460
  320.6 59.7 %collective-permute-start.11 = (f32[16,512]{1,0:T(8,128)S(1)}, f32[16,512]{1,0:T(8,128)S(1)}, u32[]{:S(2)}, u32[]{:S(2)}) collective-permute-start(f32[16,512]{1,0:T(8,128)S(1)} %pad_maximum_fusion), channel_id=1, source_target_pairs={{0,2},{1,3},{2,0},{3,1},{4,6},{5,7},{6,4},{7,5},{8,10},{9,11},{10,... | collective-permute-start | bytes 98312 | tf_op jit(solution)/shard_map/ppermute | solution.py:842
  320.9 59.9 %collective-permute-start.7 = (f32[16,512]{1,0:T(8,128)S(1)}, f32[16,512]{1,0:T(8,128)S(1)}, u32[]{:S(2)}, u32[]{:S(2)}) collective-permute-start(f32[16,512]{1,0:T(8,128)S(1)} %pad_maximum_fusion), channel_id=1, source_target_pairs={{0,1},{1,0},{2,3},{3,2},{4,5},{5,4},{6,7},{7,6},{8,9},{9,8},{10,11... | collective-permute-start | bytes 98312 | tf_op jit(solution)/shard_map/ppermute | solution.py:842
  320.9 59.7 %collective-permute-start.9 = (bf16[512,1024]{1,0:T(8,128)(2,1)S(1)}, bf16[512,1024]{1,0:T(8,128)(2,1)}, u32[]{:S(2)}, u32[]{:S(2)}) collective-permute-start(bf16[512,1024]{1,0:T(8,128)(2,1)S(1)} %get-tuple-element.123.ga_ref), channel_id=1, source_target_pairs={{0,2},{1,3},{2,0},{3,1},{4,6},{5,7},{6,4},{7,5},{8,10},{9,11},{10,... | collective-permute-start | bytes 3145736 | tf_op jit(solution)/shard_map/ppermute | solution.py:842
  322.7 82.7 %collective-permute-start.6 = (bf16[512,1024]{1,0:T(8,128)(2,1)S(1)}, bf16[512,1024]{1,0:T(8,128)(2,1)}, u32[]{:S(2)}, u32[]{:S(2)}) collective-permute-start(bf16[512,1024]{1,0:T(8,128)(2,1)S(1)} %get-tuple-element.123.ga_ref), channel_id=1, source_target_pairs={{0,1},{1,0},{2,3},{3,2},{4,5},{5,4},{6,7},{7,6},{8,9},{9,8},{10,11... | collective-permute-start | bytes 3145736 | tf_op jit(solution)/shard_map/ppermute | solution.py:842
  335.5 13.2 %copy-start.8 = (f32[512,1024]{1,0:T(8,128)S(1)}, f32[512,1024]{1,0:T(8,128)}, u32[]{:S(2)}) copy-start(f32[512,1024]{1,0:T(8,128)} %copy-done.7) | copy-start | bytes 6291460
  335.5 13.3 %copy-start.10 = (bf16[512,1024]{1,0:T(8,128)(2,1)S(1)}, bf16[512,1024]{1,0:T(8,128)(2,1)}, u32[]{:S(2)}) copy-start(bf16[512,1024]{1,0:T(8,128)(2,1)} %get-tuple-element.39.q_ref) | copy-start | bytes 3145732
  352.1 19.4 %copy-start.40 = (f32[128,32]{1,0:T(8,128)S(1)}, f32[128,32]{1,0:T(8,128)}, u32[]{:S(2)}) copy-start(f32[128,32]{1,0:T(8,128)} %constant.106.clone) | copy-start | bytes 49156
  352.1 19.4 %copy-start.48 = (f32[32]{0:T(128)S(1)}, f32[32]{0:T(128)}, u32[]{:S(2)}) copy-start(f32[32]{0:T(128)} %constant.115) | copy-start | bytes 388
  380.3 1.3 collective-permute-start.12
  380.6 2.9 collective-permute-start.10
  383.5 21.6 %copy-start.52 = (f32[8]{0:T(128)S(1)}, f32[8]{0:T(128)}, u32[]{:S(2)}) copy-start(f32[8]{0:T(128)} %param.25) | copy-start | bytes 100
  404.8 21.8 %collective-permute-start.13 = (bf16[512,1024]{1,0:T(8,128)(2,1)}, bf16[512,1024]{1,0:T(8,128)(2,1)S(1)}, u32[]{:S(2)}, u32[]{:S(2)}) collective-permute-start(bf16[512,1024]{1,0:T(8,128)(2,1)} %get-tuple-element.53), channel_id=1, source_target_pairs={{0,1},{1,0},{2,3},{3,2},{4,5},{5,4},{6,7},{7,6},{8,9},{9,8},{10,11... | collective-permute-start | bytes 3145736 | tf_op jit(solution)/shard_map/ppermute | solution.py:842
  405.4 22.1 %copy-start.59 = (bf16[512,4096]{1,0:T(8,128)(2,1)S(1)}, bf16[512,4096]{1,0:T(8,128)(2,1)}, u32[]{:S(2)}) copy-start(bf16[512,4096]{1,0:T(8,128)(2,1)} %get-tuple-element.162) | copy-start | bytes 12582916
  426.3 9.1 %collective-permute-start.8 = (bf16[512,1024]{1,0:T(8,128)(2,1)S(1)}, bf16[512,1024]{1,0:T(8,128)(2,1)S(1)}, u32[]{:S(2)}, u32[]{:S(2)}) collective-permute-start(bf16[512,1024]{1,0:T(8,128)(2,1)S(1)} %get-tuple-element.51), channel_id=1, source_target_pairs={{0,1},{1,0},{2,3},{3,2},{4,5},{5,4},{6,7},{7,6},{8,9},{9,8},{10,11... | collective-permute-start | bytes 3145736 | tf_op jit(solution)/shard_map/ppermute | solution.py:842
  427.1 25.4 %copy-start.12 = (f32[512,1024]{1,0:T(8,128)S(1)}, f32[512,1024]{1,0:T(8,128)}, u32[]{:S(2)}) copy-start(f32[512,1024]{1,0:T(8,128)} %copy-done.11) | copy-start | bytes 6291460
  427.1 25.4 %collective-permute-start.14 = (bf16[512,1024]{1,0:T(8,128)(2,1)S(1)}, bf16[512,1024]{1,0:T(8,128)(2,1)S(1)}, u32[]{:S(2)}, u32[]{:S(2)}) collective-permute-start(bf16[512,1024]{1,0:T(8,128)(2,1)S(1)} %add_convert_fusion.1), channel_id=1, source_target_pairs={{0,2},{1,3},{2,0},{3,1},{4,6},{5,7},{6,4},{7,5},{8,10},{9,11},{10,... | collective-permute-start | bytes 3145736 | tf_op jit(solution)/shard_map/ppermute | solution.py:842
  464.0 129.1 %copy-start.27 = (f32[512,1024]{1,0:T(8,128)S(1)}, f32[512,1024]{1,0:T(8,128)}, u32[]{:S(2)}) copy-start(f32[512,1024]{1,0:T(8,128)} %copy-done.26) | copy-start | bytes 6291460
  (55 other events, 257.7 us)

commit v4 on v3

--- a/solution.py
+++ b/solution.py
@@ -66,18 +66,6 @@
             )
         pl.semaphore_wait(barrier, len(self.partners()))
 
-    def copy(self, src, dst, send, recv, device):
-        copy = pltpu.make_async_remote_copy(
-            src_ref=src,
-            dst_ref=dst,
-            send_sem=send,
-            recv_sem=recv,
-            device_id=device,
-            device_id_type=MESH,
-        )
-        copy.start()
-        return copy
-
     def arrived(self, ref, recv):
         pltpu.make_async_remote_copy(
             src_ref=ref,
@@ -97,78 +85,125 @@
 
 
 class Gather:
+    LEFT, RIGHT, Y, X, CORE = "left", "right", ALONG_Y, ALONG_X, ALONG_CORE
+
     def __init__(self, place, orders, ins, outs, sems):
         self.place, self.ins, self.outs = place, ins, outs
         self.send_sem, self.recv_sem, self.own_sem = sems
         self.n = len(orders)
-        self.first = [ALONG_Y if order == "zyx" else ALONG_X for order in orders]
-        self.second = [ALONG_X if order == "zyx" else ALONG_Y for order in orders]
+        self.orders = [["zyx".index(axis) for axis in order] for order in orders]
         self.sent = [[] for _ in orders]
 
+    def exists(self, steps):
+        z, n = self.place.at[0], self.place.sizes[0]
+        return z + steps >= 0 if steps < 0 else z + steps < n
+
+    def device(self, to):
+        z, y, x, core = self.place.at
+        if to in (self.LEFT, self.RIGHT):
+            return ((z + (1 if to == self.RIGHT else -1)) * 2 + y, x * 2 + core)
+        return self.place.device(to)
+
     def spot(self, a, source):
-        return self.outs[a].at[self.place.number(source)]
-
-    def index(self, step):
-        return ((step[0] * 2 + step[1]) * 2 + step[2]) * 2 + step[3]
+        z, y, x, core = self.place.at
+        dp = (z + source[0]) * 2 + (y + source[1]) % 2
+        return self.outs[a].at[dp * 4 + (x + source[2]) % 2 * 2 + (core + source[3]) % 2]
+
+    def recv(self, a, source, to=None):
+        z = self.place.at[0] + source[0]
+        rest = list(source[1:])
+        if to is not None and to not in (self.LEFT, self.RIGHT):
+            rest = [(have - step) % 2 for have, step in zip(rest, to[1:])]
+        return self.recv_sem.at[a, ((z * 2 + rest[0]) * 2 + rest[1]) * 2 + rest[2]]
 
     def copy(self, a, k):
         source, to = self.sent[a][k]
-        place = self.place
         return pltpu.make_async_remote_copy(
             src_ref=self.ins[a] if source == OWN else self.spot(a, source),
             dst_ref=self.spot(a, source),
             send_sem=self.send_sem.at[a, k],
-            recv_sem=self.recv_sem.at[a, self.index(place.minus(source, to))],
-            device_id=place.device(to),
+            recv_sem=self.recv(a, source, to),
+            device_id=self.device(to),
             device_id_type=MESH,
         )
 
+    def when(self, conditions, run):
+        conditions = [c for c in conditions if c is not None]
+        if conditions:
+            pl.when(functools.reduce(jnp.logical_and, conditions))(run)
+        else:
+            run()
+
+    def limits(self, source, to):
+        ends = {self.LEFT: -1, self.RIGHT: 1}
+        return [
+            self.exists(source[0]) if source[0] else None,
+            self.exists(ends[to]) if to in ends else None,
+        ]
+
     def send(self, a, source, to):
         self.sent[a].append((source, to))
-        self.copy(a, len(self.sent[a]) - 1).start()
+        k = len(self.sent[a]) - 1
+        self.when(self.limits(source, to)[1:], lambda: self.copy(a, k).start())
 
     def own(self, a):
         return pltpu.make_async_copy(self.ins[a], self.spot(a, OWN), self.own_sem.at[a])
 
     def arrived(self, a, source):
-        self.place.arrived(self.spot(a, source), self.recv_sem.at[a, self.index(source)])
+        self.place.arrived(self.spot(a, source), self.recv(a, source))
+
+    def onward(self, a, source):
+        order = self.orders[a]
+        came = max([order.index(axis) for axis in range(3) if source[axis]], default=-1)
+        to = []
+        if came >= 0 and order[came] == 0:
+            to.append(self.RIGHT if source[0] < 0 else self.LEFT)
+        for axis in order[came + 1 :]:
+            to += ((self.LEFT, self.RIGHT), (self.Y,), (self.X,))[axis]
+        return to + [self.CORE]
 
     def begin(self, a):
-        for to in self.place.partners():
+        for to in self.onward(a, OWN):
             self.send(a, OWN, to)
         self.own(a).start()
 
-    def middle(self, a, z):
-        at = (z, 0, 0, 0)
-        if z:
-            self.arrived(a, at)
-            for to in (self.first[a], self.second[a], ALONG_CORE):
-                self.send(a, at, to)
-        source = self.place.plus(at, self.first[a])
-        self.arrived(a, source)
-        for to in (self.second[a], ALONG_CORE):
-            self.send(a, source, to)
-
-    def late(self, a, z):
-        for step in (self.second[a], self.place.plus(self.first[a], self.second[a])):
-            source = self.place.plus((z, 0, 0, 0), step)
-            self.arrived(a, source)
-            self.send(a, source, ALONG_CORE)
+    def level(self, a, hops):
+        for rest in ((0, 0), (1, 0), (0, 1), (1, 1)):
+            distance = hops - sum(rest)
+            if not 0 <= distance < self.place.sizes[0]:
+                continue
+            for steps in dict.fromkeys((-distance, distance)):
+
+                def run(source=(steps,) + rest + (0,)):
+                    self.arrived(a, source)
+                    for to in self.onward(a, source):
+                        self.send(a, source, to)
+
+                self.when([self.exists(steps) if steps else None], run)
+
+    def levels(self):
+        return range(1, self.place.sizes[0] + 2)
 
     def finish(self, a):
-        for z in near_first(self.place.sizes[0]):
+        place = self.place
+        for z in range(place.sizes[0]):
             for y in range(2):
                 for x in range(2):
-                    self.arrived(a, (z, y, x, 1))
+                    source = (z - place.at[0], y, x, 1)
+                    place.arrived(self.spot(a, source), self.recv(a, source))
         for k in range(len(self.sent[a])):
-            self.copy(a, k).wait_send()
+            self.when(self.limits(*self.sent[a][k]), lambda k=k: self.copy(a, k).wait_send())
         self.own(a).wait()
 
 
 def gather_sems(n, n_hi):
-    sends = (n_hi - 1) + 3 + (n_hi - 1) * 3 + n_hi * 2 + n_hi * 2
+    sends = 5 + (8 * n_hi - 5) * 4
     dma = pltpu.SemaphoreType.DMA
     return [dma((n, sends)), dma((n, n_hi * 8)), dma((n,))]
+
+
+def piece_width(columns):
+    return next(w for w in (1024, 768, 512, 384, 256, 128) if columns % w == 0)
 
 
 class Scatter:
@@ -193,34 +228,51 @@
         self.first = [ALONG_X if order == "xyz" else ALONG_Y for order in orders]
         self.second = [ALONG_Y if order == "xyz" else ALONG_X for order in orders]
         self.started = []
-        self.loads = {}
 
     def step(self, a, z, two, one):
         y, x = (two, one) if self.second[a] == ALONG_Y else (one, two)
         return (z, y, x, 0)
 
-    def send(self, src, dst, send, recv, to):
-        self.started.append(self.place.copy(src, dst, send, recv, self.place.device(to)))
+    def send(self, ends, device):
+        def build():
+            src, dst, send, recv = ends()
+            return pltpu.make_async_remote_copy(
+                src_ref=src,
+                dst_ref=dst,
+                send_sem=send,
+                recv_sem=recv,
+                device_id=device(),
+                device_id_type=MESH,
+            )
+
+        build().start()
+        self.started.append(build)
+
+    def load(self, a, z, two, one):
+        s = (z * 2 + two) * 2 + one
+        return pltpu.make_async_copy(
+            self.ins[a].at[self.place.number(self.step(a, z, two, one))],
+            self.accs[a].at[s],
+            self.load_sem.at[a, s],
+        )
 
     def begin(self, z, a):
         for two, one in ((1, 1), (0, 1), (1, 0), (0, 0)):
             s = (z * 2 + two) * 2 + one
-            step = self.step(a, z, two, one)
+            step = self.step(a, z, two, one)[:3] + (1,)
             self.send(
-                self.ins[a].at[self.place.number(step[:3] + (1,))],
-                self.from_core[a].at[s],
-                self.core_send.at[a, s],
-                self.core_recv.at[a, s],
-                ALONG_CORE,
+                lambda s=s, step=step: (
+                    self.ins[a].at[self.place.number(step)],
+                    self.from_core[a].at[s],
+                    self.core_send.at[a, s],
+                    self.core_recv.at[a, s],
+                ),
+                lambda: self.place.device(ALONG_CORE),
             )
-            load = pltpu.make_async_copy(
-                self.ins[a].at[self.place.number(step)], self.accs[a].at[s], self.load_sem.at[a, s]
-            )
-            load.start()
-            self.loads[a, s] = load
+            self.load(a, z, two, one).start()
 
     def add(self, acc, got):
-        width = min(acc.shape[1], 1024)
+        width = piece_width(acc.shape[1])
 
         def piece(k, carry):
             at = pl.ds(pl.multiple_of(k * width, width), width)
@@ -233,16 +285,18 @@
         for two, one in ((1, 1), (0, 1), (1, 0), (0, 0)):
             k = z * 2 + two
             s = k * 2 + one
-            self.loads[a, s].wait()
+            self.load(a, z, two, one).wait()
             self.place.arrived(self.from_core[a].at[s], self.core_recv.at[a, s])
             self.add(self.accs[a].at[s], self.from_core[a].at[s])
             if one:
                 self.send(
-                    self.accs[a].at[s],
-                    self.from_first[a].at[k],
-                    self.first_send.at[a, k],
-                    self.first_recv.at[a, k],
-                    self.first[a],
+                    lambda s=s, k=k: (
+                        self.accs[a].at[s],
+                        self.from_first[a].at[k],
+                        self.first_send.at[a, k],
+                        self.first_recv.at[a, k],
+                    ),
+                    lambda: self.place.device(self.first[a]),
                 )
 
     def one(self, z, a):
@@ -253,11 +307,13 @@
             self.add(acc, self.from_first[a].at[k])
             if two:
                 self.send(
-                    acc,
-                    self.from_second[a].at[z],
-                    self.second_send.at[a, z],
-                    self.second_recv.at[a, z],
-                    self.second[a],
+                    lambda k=k: (
+                        self.accs[a].at[k * 2],
+                        self.from_second[a].at[z],
+                        self.second_send.at[a, z],
+                        self.second_recv.at[a, z],
+                    ),
+                    lambda: self.place.device(self.second[a]),
                 )
 
     def two(self, z, a):
@@ -266,18 +322,20 @@
         self.add(acc, self.from_second[a].at[z])
         if z:
             self.send(
-                acc,
-                self.from_z[a].at[z - 1],
-                self.z_send.at[a, z - 1],
-                self.z_recv.at[a, z - 1],
-                (z, 0, 0, 0),
+                lambda: (
+                    self.accs[a].at[z * 4],
+                    self.from_z[a].at[z - 1],
+                    self.z_send.at[a, z - 1],
+                    self.z_recv.at[a, z - 1],
+                ),
+                lambda: self.place.device((z, 0, 0, 0)),
             )
 
     def last(self, a):
         for z in range(1, self.n_hi):
             self.place.arrived(self.from_z[a].at[z - 1], self.z_recv.at[a, z - 1])
         out, acc, got = self.outs[a], self.accs[a].at[0], self.from_z[a]
-        width = min(out.shape[1], 1024)
+        width = piece_width(out.shape[1])
 
         def piece(k, carry):
             at = pl.ds(pl.multiple_of(k * width, width), width)
@@ -297,18 +355,20 @@
         total[...] = source[...]
         self.small_send(0)
 
-    def small_send(self, k):
-        _, total, buffer = self.small
+    def small_device(self, k):
         step = self.small_steps()[k]
         z, y, x, core = self.place.at
         if isinstance(step, int):
-            device = ((z + step - 2 * step * ((z // step) % 2)) * 2 + y, x * 2 + core)
-        else:
-            device = self.place.device(step)
+            return ((z + step - 2 * step * ((z // step) % 2)) * 2 + y, x * 2 + core)
+        return self.place.device(step)
+
+    def small_send(self, k):
+        _, total, buffer = self.small
         buffer[0, k] = total[...]
         send, recv = self.small_sems
-        self.started.append(
-            self.place.copy(buffer.at[0, k], buffer.at[1, k], send.at[k], recv.at[k], device)
+        self.send(
+            lambda: (buffer.at[0, k], buffer.at[1, k], send.at[k], recv.at[k]),
+            lambda: self.small_device(k),
         )
 
     def small_next(self, k):
@@ -319,8 +379,8 @@
             self.small_send(k + 1)
 
     def finish(self):
-        for copy in self.started:
-            copy.wait_send()
+        for build in self.started:
+            build().wait_send()
 
 
 def scatter_buffers(shapes, n_hi):
@@ -389,7 +449,11 @@
     )(*arrays, small)
 
 
-def pick_scores(queries, table_ref, chosen):
+FIRST_STOP, LAST_STOP = 2, 62
+AHEAD = 0
+
+
+def pick_scores(queries, table_ref, chosen, pause):
     slots, step = table_ref.shape[1], 256
     low, high = chosen & 7, chosen >> 3
     picked = jnp.zeros(chosen.shape, F32)
@@ -398,10 +462,12 @@
         for row in range(0, step, 8):
             got = jnp.take_along_axis(scores[row : row + 8], low, axis=0)
             picked = jnp.where(high == (at + row) // 8, got, picked)
+        if at + step == slots // 2:
+            pause()
     return picked * SCALE
 
 
-def recall_values(scores, table_ref, chosen, lse_ref, p_ref):
+def recall_values(scores, table_ref, chosen, lse_ref, p_ref, pause):
     slots, tokens, step = table_ref.shape[1], chosen.shape[1], 256
     top = jnp.max(scores, axis=0, keepdims=True)
     weights = jnp.exp(scores - top)
@@ -421,6 +487,8 @@
             dense = jnp.where(rows == mine[j : j + 1], probs[j : j + 1], dense)
         p_ref[0, pl.ds(at, step), :] = dense
         out = out + dot(values_t[:, at : at + step], dense)
+        if at + step == slots // 2:
+            pause()
     return out.T.astype(BF)
 
 
@@ -437,7 +505,6 @@
     place = Place(n_hi)
     early = Gather(place, orders[:2], early_in, (wq, norms), sems[:3])
     late = Gather(place, orders[2:], late_in, late_out, sems[3:])
-    zs = near_first(n_hi)
     rows = x_ref.shape[0]
 
     def ask(src, slot, to):
@@ -458,15 +525,14 @@
         place.greet()
         for a in range(2):
             early.begin(a)
+        for a in range(AHEAD):
+            late.begin(a)
         x = x_ref[...].astype(F32)
         center = x - jnp.mean(x, axis=-1, keepdims=True)
         scaled = center * lax.rsqrt(jnp.mean(center * center, axis=-1, keepdims=True) + EPSILON)
-        for z in zs:
+        for hops in early.levels():
             for a in range(2):
-                early.middle(a, z)
-        for z in zs:
-            for a in range(2):
-                early.late(a, z)
+                early.level(a, hops)
         for a in range(2):
             early.finish(a)
         keep().start()
@@ -487,32 +553,29 @@
             q_ref[:, pl.ds(at, 256)] = dot(normed, weights).astype(BF)
         ask(q_ref, 1, ALONG_CORE).start()
         ask(q_ref, 2, ALONG_X).start()
-        for a in range(n):
+        for a in range(AHEAD, n):
             late.begin(a)
         asked[0] = q_ref[...]
         place.arrived(asked.at[1], q_recv.at[1])
 
-    events = []
-    for a in range(n + 1):
-        for z in zs:
-            if a < n:
-                events.append(functools.partial(late.middle, a, z))
-            if a > 0:
-                events.append(functools.partial(late.late, a - 1, z))
+    events = [
+        functools.partial(late.level, a, hops) for hops in late.levels() for a in range(n)
+    ]
     ticks = 2 * H
-
-    def slot(at):
-        count = 2 * ticks - 2
-        mine = events[len(events) * (at - 2) // count : len(events) * (at - 1) // count]
-        if at >= 2 and mine:
-
-            @pl.when(tick == at // 2)
-            def _():
-                for event in mine:
-                    event()
-
-    for at in range(0, 2 * ticks, 2):
-        slot(at)
+    stops = 4 * ticks
+    stop_of = [FIRST_STOP + k * (LAST_STOP - FIRST_STOP) // len(events) for k in range(len(events))]
+
+    def pause(part):
+        for at in range(part, stops, 4):
+            mine = [event for event, stop in zip(events, stop_of) if stop == at]
+            if mine:
+
+                @pl.when(tick == at // 4)
+                def _():
+                    for event in mine:
+                        event()
+
+    pause(0)
 
     @pl.when(tick == H)
     def _():
@@ -520,16 +583,15 @@
 
     queries = asked[pl.ds(phase * 2, 2), :, pl.ds(pl.multiple_of(head * HD, HD), HD)]
     chosen = slot_ref[0]
-    scores = pick_scores(queries.reshape(2 * rows, HD), table_ref, chosen)
+    scores = pick_scores(queries.reshape(2 * rows, HD), table_ref, chosen, lambda: pause(1))
 
     @pl.when(tick == H - 2)
     def _():
         place.arrived(asked.at[2], q_recv.at[2])
         ask(asked.at[2], 3, ALONG_CORE).start()
 
-    for at in range(1, 2 * ticks, 2):
-        slot(at)
-    out_ref[...] = recall_values(scores, table_ref, chosen, lse_ref, p_ref)
+    pause(2)
+    out_ref[...] = recall_values(scores, table_ref, chosen, lse_ref, p_ref, lambda: pause(3))
 
     @pl.when(tick == ticks - 1)
     def _():
@@ -598,51 +660,12 @@
     )(x, table, chosen, *early, *late)
 
 
-def recall_grad_kernel(ga_ref, gb_ref, mem_ref, p_ref, delta_ref, share_ref, outa_ref, outb_ref):
-    slots, tokens = p_ref.shape[1], p_ref.shape[2]
-    half = tokens // 2
-    grads = jnp.concatenate([ga_ref[...], gb_ref[...]], axis=0)
-    delta = delta_ref[0]
-    keys_t = mem_ref[0, :, pl.ds(0, HD)].T
-    step = 512
-    out = jnp.zeros((HD, tokens), F32)
-    for at in range(0, slots, step):
-        along = dot(mem_ref[0, pl.ds(at, step), pl.ds(HD, HD)], grads, NT)
-        scores = (along - delta).astype(BF) * p_ref[0, pl.ds(at, step), :]
-        out = out + dot(keys_t[:, at : at + step], scores)
-    out = (out * (share_ref[0] * SCALE)).T.astype(BF)
-    outa_ref[...] = out[:half]
-    outb_ref[...] = out[half:]
-
-
 def head_columns(rows, first=0):
     return pl.BlockSpec((rows, HD), lambda h: (0, first + h))
 
 
 def per_head(*shape):
     return pl.BlockSpec((1,) + shape, lambda h: (h,) + (0,) * len(shape))
-
-
-def recall_grad(grad_a, grad_b, table, probs, first, delta, share):
-    rows, slots = grad_a.shape[0], table.shape[1]
-    return pl.pallas_call(
-        recall_grad_kernel,
-        grid=(H,),
-        in_specs=[
-            head_columns(rows),
-            head_columns(rows),
-            per_head(slots, 2 * HD),
-            pl.BlockSpec((1, slots, 2 * rows), lambda h: (first + h, 0, 0)),
-            per_head(1, 2 * rows),
-            per_head(1, 2 * rows),
-        ],
-        out_specs=[head_columns(rows), head_columns(rows)],
-        out_shape=[jax.ShapeDtypeStruct(grad_a.shape, BF)] * 2,
-        compiler_params=pltpu.CompilerParams(vmem_limit_bytes=48 << 20),
-        cost_estimate=pl.CostEstimate(
-            flops=8 * rows * slots * HD * H, bytes_accessed=64 << 20, transcendentals=0
-        ),
-    )(grad_a, grad_b, table, probs, delta, share)
 
 
 def near_buckets():
@@ -711,10 +734,9 @@
         out_ref[pl.ds(step * at, step), :] = out.T
 
 
-def segment_grad_kernel(
-    open_ref, g_ref, q_ref, kc_ref, kn_ref, vc_ref, vn_ref, p_ref, gq_ref, gk_ref, gv_ref, diag_ref, tot_ref
+def segment_grad(
+    g_ref, q_ref, kc_ref, kn_ref, vc_ref, vn_ref, p_ref, put_q, gk_ref, gv_ref, diag_ref, tot_ref
 ):
-    closed = 1.0 - open_ref[pl.program_id(0)]
     cache_t, keys_t = kc_ref[...].T, kn_ref[...].T
     on_diagonal = jnp.zeros((NEAR, NEAR), F32)
     beside = jnp.zeros((NEAR, NEAR), F32)
@@ -723,7 +745,7 @@
     grad_keys, grad_values = [], []
     for at in range(W // step):
         count = 2 * (at + 1)
-        grads = (closed * g_ref[pl.ds(step * at, step), :]).astype(BF)
+        grads = g_ref[pl.ds(step * at, step), :]
         queries = q_ref[pl.ds(step * at, step), :]
         grad_probs = jnp.concatenate(
             [dot(vc_ref[...], grads, NT), dot(vn_ref[pl.ds(0, NEAR * count), :], grads, NT)], axis=0
@@ -734,7 +756,7 @@
         grad_scores = product - wide * jnp.sum(product, axis=0, keepdims=True)
         low = grad_scores.astype(BF)
         grad_q = dot(cache_t, low[:W]) + dot(keys_t[:, : NEAR * count], low[W:])
-        gq_ref[pl.ds(step * at, step), :] = (grad_q * SCALE).T
+        put_q(step * at, (grad_q * SCALE).T)
         grad_keys.append(dot(low[W:], queries) * SCALE)
         grad_values.append(dot(probs[W:], grads))
         if at == 0:
@@ -788,39 +810,352 @@
     )(length, near, queries, cache, keys_values, cache, keys_values)
 
 
-def segment_backward(gate_open, grad_mixed, queries, keys_values, cache, probs):
+def recall_back(grads, table_ref, p_ref, delta, share):
+    slots, step = table_ref.shape[1], 512
+    keys_t = table_ref[0, :, pl.ds(0, HD)].T
+    out = jnp.zeros((HD, grads.shape[0]), F32)
+    for at in range(0, slots, step):
+        along = dot(table_ref[0, pl.ds(at, step), pl.ds(HD, HD)], grads, NT)
+        scores = (along - delta).astype(BF) * p_ref[0, pl.ds(at, step), :]
+        out = out + dot(keys_t[:, at : at + step], scores)
+    return (out * (share * SCALE)).T.astype(BF)
+
+
+def attend_grad_kernel(n_hi, orders, *refs):
+    n = len(orders)
+    grec_ref, aux_ref, glocal_ref, q_ref, kc_ref, kn_ref, vc_ref, vn_ref, plocal_ref = refs[:9]
+    table_ref, p_ref, lse_ref = refs[9:12]
+    grads_in, rest = refs[12 : 12 + n], refs[12 + n :]
+    gq_ref, gk_ref, gv_ref, diag_ref, tot_ref = rest[:5]
+    sums_out, rest = rest[5 : 5 + n], rest[5 + n :]
+    asked, aux, back, returned, glocal_q = rest[:5]
+    ask_send, ask_recv, aux_send, aux_recv, back_send, back_recv = rest[5:11]
+    buffers = [rest[11 + k * n : 11 + (k + 1) * n] for k in range(5)]
+    place = Place(n_hi)
+    scatter = Scatter(place, orders, grads_in, sums_out, buffers, rest[11 + 5 * n :])
+    tick = pl.program_id(0)
+    ticks = 3 * H
+    order = near_first(n_hi)[::-1]
+
+    def remote(src, dst, send, recv, to):
+        return pltpu.make_async_remote_copy(
+            src_ref=src,
+            dst_ref=dst,
+            send_sem=send,
+            recv_sem=recv,
+            device_id=place.device(to),
+            device_id_type=MESH,
+        )
+
+    def ask(slot, to):
+        first = slot < 3
+        return [
+            remote(
+                grec_ref if first else asked.at[2],
+                asked.at[slot],
+                ask_send.at[slot],
+                ask_recv.at[slot],
+                to,
+            ),
+            remote(
+                aux_ref if first else aux.at[2],
+                aux.at[slot],
+                aux_send.at[slot],
+                aux_recv.at[slot],
+                to,
+            ),
+        ]
+
+    def asked_arrived(slot):
+        place.arrived(asked.at[slot], ask_recv.at[slot])
+        place.arrived(aux.at[slot], aux_recv.at[slot])
+
+    def give(slot, to):
+        return remote(
+            back.at[(1, 3, 2)[slot]], returned.at[slot], back_send.at[slot], back_recv.at[slot], to
+        )
+
+    @pl.when(tick == 0)
+    def _():
+        place.greet()
+        for slot, to in ((1, ALONG_CORE), (2, ALONG_X)):
+            for copy in ask(slot, to):
+                copy.start()
+        for z in order:
+            for a in range(n):
+                scatter.begin(z, a)
+        asked[0] = grec_ref[...]
+        aux[0] = aux_ref[...]
+
+    events = []
+    for k in range(n_hi + 2):
+        for delay, event in enumerate((scatter.core, scatter.one, scatter.two)):
+            if 0 <= k - delay < n_hi:
+                events += [functools.partial(event, order[k - delay], a) for a in range(n)]
+    for at in range(1, ticks):
+        mine = events[len(events) * (at - 1) // (ticks - 1) : len(events) * at // (ticks - 1)]
+
+        @pl.when(tick == at)
+        def _(mine=mine):
+            for event in mine:
+                event()
+
+    @pl.when(tick < H)
+    def _():
+        segment_grad(
+            glocal_ref, q_ref, kc_ref, kn_ref, vc_ref, vn_ref, plocal_ref,
+            lambda at, value: glocal_q.__setitem__(
+                (pl.ds(at, value.shape[0]), pl.ds(pl.multiple_of(tick * HD, HD), HD)), value
+            ),
+            gk_ref, gv_ref, diag_ref, tot_ref,
+        )
+
+    @pl.when(tick == H)
+    def _():
+        asked_arrived(1)
+
+    @pl.when(tick == H + 2)
+    def _():
+        asked_arrived(2)
+        for copy in ask(3, ALONG_CORE):
+            copy.start()
+
+    @pl.when(tick == 2 * H)
+    def _():
+        asked_arrived(3)
+        give(0, ALONG_CORE).start()
+
+    @pl.when(tick >= H)
+    def _():
+        phase = tick // H - 1
+        head = tick % H
+        lanes = pl.ds(pl.multiple_of(head * HD, HD), HD)
+        pair = pl.ds(phase * 2, 2)
+        grads = asked[pair, :, lanes].reshape(-1, HD)
+        delta = jnp.concatenate([aux[phase * 2 + k, pl.ds(head, 1), :] for k in range(2)], axis=1)
+        total = jnp.concatenate(
+            [aux[phase * 2 + k, pl.ds(H + head, 1), :] for k in range(2)], axis=1
+        )
+        share = jnp.exp(lse_ref[0] - total)
+        result = recall_back(grads, table_ref, p_ref, delta, share)
+        back[pair, :, lanes] = result.reshape(2, -1, HD)
+
+    @pl.when(tick == ticks - 1)
+    def _():
+        give(1, ALONG_CORE).start()
+        place.arrived(returned.at[1], back_recv.at[1])
+        back[2] = (back[2].astype(F32) + returned[1].astype(F32)).astype(BF)
+        give(2, ALONG_X).start()
+        for a in range(n):
+            scatter.last(a)
+        place.arrived(returned.at[0], back_recv.at[0])
+        place.arrived(returned.at[2], back_recv.at[2])
+        gq_ref[...] = (
+            glocal_q[...]
+            + back[0].astype(F32)
+            + returned[0].astype(F32)
+            + returned[2].astype(F32)
+        ).astype(BF)
+        scatter.finish()
+        for slot, to in ((1, ALONG_CORE), (2, ALONG_X), (3, ALONG_CORE)):
+            for copy in ask(slot, to):
+                copy.wait_send()
+        for slot, to in ((0, ALONG_CORE), (1, ALONG_CORE), (2, ALONG_X)):
+            give(slot, to).wait_send()
+
+
+def attend_grad(
+    grad_recalled, aux, grad_local, queries, keys_values, cache, probs_local, table, probs, lses,
+    grads, orders, collective_id,
+):
+    n, n_hi = len(grads), lax.axis_size("dp") // 2
+    (rows, width), slots = queries.shape, table.shape[1]
+    shapes = [g.shape[1:] for g in grads]
+    dma = pltpu.SemaphoreType.DMA
+
+    def column(first=0):
+        return pl.BlockSpec((rows, HD), lambda t: (0, first + jnp.minimum(t, H - 1)))
+
+    def head(*shape):
+        return pl.BlockSpec((1,) + shape, lambda t: (jnp.minimum(t, H - 1),) + (0,) * len(shape))
+
+    def later(t):
+        return jnp.maximum(t - H, 0)
+
     return pl.pallas_call(
-        segment_grad_kernel,
-        grid=(H,),
+        functools.partial(attend_grad_kernel, n_hi, orders),
+        grid=(3 * H,),
         in_specs=[
-            SCALARS,
-            head_columns(W),
-            head_columns(W),
-            head_columns(W),
-            head_columns(W),
-            head_columns(W, H),
-            head_columns(W, H),
-            per_head(2 * W, W),
-        ],
-        out_specs=[
-            head_columns(W),
-            head_columns(W),
-            head_columns(W),
-            per_head(1, 2 * NEAR),
-            per_head(8, 2 * NEAR),
-        ],
+            IN_VMEM,
+            IN_VMEM,
+            column(),
+            column(),
+            column(),
+            column(),
+            column(H),
+            column(H),
+            head(2 * W, W),
+            pl.BlockSpec((1, slots, 2 * HD), lambda t: (later(t) % H, 0, 0)),
+            pl.BlockSpec((1, slots, 2 * rows), lambda t: (later(t), 0, 0)),
+            pl.BlockSpec((1, 1, 2 * rows), lambda t: (later(t) % H, 0, later(t) // H)),
+        ]
+        + [ANYWHERE] * n,
+        out_specs=[IN_VMEM, column(), column(), head(1, 2 * NEAR), head(8, 2 * NEAR)]
+        + [IN_VMEM] * n,
         out_shape=[
-            jax.ShapeDtypeStruct((W, H * HD), F32),
-            jax.ShapeDtypeStruct((W, H * HD), BF),
-            jax.ShapeDtypeStruct((W, H * HD), BF),
+            jax.ShapeDtypeStruct((rows, width), BF),
+            jax.ShapeDtypeStruct((rows, width), BF),
+            jax.ShapeDtypeStruct((rows, width), BF),
             jax.ShapeDtypeStruct((H, 1, 2 * NEAR), F32),
             jax.ShapeDtypeStruct((H, 8, 2 * NEAR), F32),
+        ]
+        + [jax.ShapeDtypeStruct(shape, F32) for shape in shapes],
+        scratch_shapes=[
+            pltpu.VMEM((4, rows, width), BF),
+            pltpu.VMEM((4,) + aux.shape, F32),
+            pltpu.VMEM((4, rows, width), BF),
+            pltpu.VMEM((3, rows, width), BF),
+            pltpu.VMEM((rows, width), F32),
+        ]
+        + [dma((4,))] * 4
+        + [dma((3,))] * 2
+        + scatter_buffers(shapes, n_hi)
+        + scatter_sems(n, n_hi),
+        compiler_params=pltpu.CompilerParams(
+            collective_id=collective_id, has_side_effects=True, vmem_limit_bytes=62 << 20
+        ),
+        cost_estimate=pl.CostEstimate(
+            flops=16 * rows * slots * HD * H, bytes_accessed=128 << 20, transcendentals=0
+        ),
+    )(
+        grad_recalled, aux, grad_local, queries, cache, keys_values, cache, keys_values,
+        probs_local, table, probs, lses, *grads,
+    )
+
+
+def feed_kernel(
+    parts_ref, lse_ref, local_ref, x_ref, cot_ref, gate_ref, norms_ref, wo_ref, up_ref, down_ref,
+    out_ref, gatt_ref, gwo_ref, gup_ref, gdown_ref, glocal_ref, grec_ref, aux_ref, sums_ref,
+    recalled, mixed_t, attended, scaled, inverse, normed, normed_t, acc, gacc,
+):
+    step, last = pl.program_id(0), pl.num_programs(0) - 1
+    rows, width = x_ref.shape
+    gate = gate_ref[...]
+
+    @pl.when(step == 0)
+    def _():
+        lses = [lse_ref[k] for k in range(3)]
+        top = functools.reduce(jnp.maximum, lses)
+        total = top + jnp.log(sum(jnp.exp(lse - top) for lse in lses))
+        aux_ref[H:, :] = total
+        shares = [jnp.exp(lse - total).T for lse in lses]
+        for h in range(H):
+            at = pl.ds(h * HD, HD)
+            recalled[:, at] = sum(
+                shares[k][:, h : h + 1] * parts_ref[k, :, at].astype(F32) for k in range(3)
+            )
+        mixed = (gate * recalled[...] + (1.0 - gate) * local_ref[...]).astype(BF)
+        mixed_t[...] = mixed.T
+        here = x_ref[...].astype(F32) + dot(mixed, wo_ref[...])
+        attended[...] = here
+        center = here - jnp.mean(here, axis=-1, keepdims=True)
+        inv = lax.rsqrt(jnp.mean(center * center, axis=-1, keepdims=True) + EPSILON)
+        inverse[...] = inv
+        scaled[...] = center * inv
+        n2 = (scaled[...] * norms_ref[1:2] + norms_ref[3:4]).astype(BF)
+        normed[...] = n2
+        normed_t[...] = n2.T
+        acc[...] = jnp.zeros(acc.shape, F32)
+        gacc[...] = jnp.zeros(gacc.shape, F32)
+
+    up = dot(normed[...], up_ref[...])
+    root = np.sqrt(2 / np.pi).astype(np.float32)
+    square = up * up
+    bend = jnp.tanh(root * (up + 0.044715 * (square * up)))
+    hidden = (0.5 * up * (1.0 + bend)).astype(BF)
+    slope = 0.5 * (1.0 + bend) + 0.5 * up * (1.0 - bend * bend) * (
+        root * (1.0 + (3 * 0.044715) * square)
+    )
+    grad_up = (dot(cot_ref[...], down_ref[...], NT) * slope).astype(BF)
+    acc[...] += dot(hidden, down_ref[...])
+    gacc[...] += dot(grad_up, up_ref[...], NT)
+    gdown_ref[...] = dot(hidden.T, cot_ref[...]).astype(BF)
+    gup_ref[...] = dot(normed_t[...], grad_up).astype(BF)
+
+    @pl.when(step == last)
+    def _():
+        out_ref[...] = (attended[...] + acc[...]).astype(BF)
+        grad = gacc[...]
+        sums_ref[0:1] = jnp.sum(grad * scaled[...], axis=0, keepdims=True)
+        sums_ref[1:2] = jnp.sum(grad, axis=0, keepdims=True)
+        grad = grad * norms_ref[1:2]
+        mean_grad = jnp.mean(grad, axis=-1, keepdims=True)
+        mean_cross = jnp.mean(grad * scaled[...], axis=-1, keepdims=True)
+        grad = cot_ref[...].astype(F32) + inverse[...] * (
+            grad - mean_grad - scaled[...] * mean_cross
+        )
+        gatt_ref[...] = grad
+        low = grad.astype(BF)
+        gwo_ref[...] = dot(mixed_t[...], low).astype(BF)
+        gmixed = dot(low, wo_ref[...], NT)
+        sums_ref[2:3] = jnp.sum(gmixed * (recalled[...] - local_ref[...]), axis=0, keepdims=True)
+        sums_ref[3:] = jnp.zeros((5, width), F32)
+        glocal_ref[...] = ((1.0 - gate) * gmixed).astype(BF)
+        grec = (gate * gmixed).astype(BF)
+        grec_ref[...] = grec
+        product = grec.astype(F32) * recalled[...]
+        delta = [
+            jnp.sum(product[:, h * HD : (h + 1) * HD], axis=1, keepdims=True) for h in range(H)
+        ]
+        aux_ref[:H, :] = jnp.concatenate(delta, axis=1).T
+
+
+def feed(parts, lses, local_out, x, cotangent, gate_row, norm_rows, w_out, w_up, w_down):
+    rows, width = x.shape
+    hidden = w_up.shape[1]
+    block = 512
+    full = jax.ShapeDtypeStruct
+    return pl.pallas_call(
+        feed_kernel,
+        grid=(hidden // block,),
+        in_specs=[IN_VMEM] * 8
+        + [
+            pl.BlockSpec((width, block), lambda k: (0, k)),
+            pl.BlockSpec((block, width), lambda k: (k, 0)),
         ],
-        compiler_params=pltpu.CompilerParams(vmem_limit_bytes=32 << 20),
+        out_specs=[IN_VMEM] * 3
+        + [
+            pl.BlockSpec((width, block), lambda k: (0, k)),
+            pl.BlockSpec((block, width), lambda k: (k, 0)),
+        ]
+        + [IN_VMEM] * 4,
+        out_shape=[
+            full((rows, width), BF),
+            full((rows, width), F32),
+            full((width, width), BF),
+            full((width, hidden), BF),
+            full((hidden, width), BF),
+            full((rows, width), BF),
+            full((rows, width), BF),
+            full((2 * H, rows), F32),
+            full((8, width), F32),
+        ],
+        scratch_shapes=[
+            pltpu.VMEM((rows, width), F32),
+            pltpu.VMEM((width, rows), BF),
+            pltpu.VMEM((rows, width), F32),
+            pltpu.VMEM((rows, width), F32),
+            pltpu.VMEM((rows, 1), F32),
+            pltpu.VMEM((rows, width), BF),
+            pltpu.VMEM((width, rows), BF),
+            pltpu.VMEM((rows, width), F32),
+            pltpu.VMEM((rows, width), F32),
+        ],
+        compiler_params=pltpu.CompilerParams(vmem_limit_bytes=56 << 20),
         cost_estimate=pl.CostEstimate(
-            flops=16 * W * W * HD * H, bytes_accessed=20 << 20, transcendentals=0
+            flops=12 * rows * width * hidden, bytes_accessed=36 << 20, transcendentals=0
         ),
-    )(gate_open, grad_mixed, queries, cache, keys_values, cache, keys_values, probs)
+    )(parts, lses, local_out, x, cotangent, gate_row, norm_rows, w_out, w_up, w_down)
 
 
 def norm_forward(values, gain_row, shift_row):
@@ -894,7 +1229,7 @@
         chosen,
         (w_qkv[:, :width], norms),
         (w_qkv[:, width:], w_out, w_up, w_down),
-        ("zyx", "zxy", "zxy", "zyx", "zyx", "zxy"),
+        ("zyx", "zxy", "xyz", "xyz", "zyx", "zxy"),
         0,
     )
     full_q, full_kv, full_out, full_up, full_down = [f.reshape(-1, f.shape[2]) for f in full]
@@ -914,71 +1249,37 @@
     other_out, other_lse = swap((out_cross, lse_far[:, count:]), 1)
     pair_out, pair_lse = combine((out_x, other_out), (lse_far[:, :count], other_lse))
     far_out, far_lse = swap((pair_out.astype(BF), pair_lse), 2)
-    recalled, total_lse = combine((own_out, core_out, far_out), (own_lse, core_lse, far_lse))
-
     gate_open = jax.nn.sigmoid(gate_bias)
-    gate_row = jnp.repeat(gate_open, HD)[None]
-    mixed_low = (gate_row * recalled + (1.0 - gate_row) * local_out).astype(BF)
-    attended = inputs + dot(mixed_low, full_out)
-    normed_two, scaled_two, inverse_two = norm_forward(attended, gain_rows[1], shift_rows[1])
-    normed_two = normed_two.astype(BF)
-    up_pre = dot(normed_two, full_up)
-    hidden = jax.nn.gelu(up_pre).astype(BF)
-    output = attended + dot(hidden, full_down)
-
-    grad_output = cotangent.astype(F32)
-    grad_down = jnp.einsum("tf,td->fd", hidden, cotangent, preferred_element_type=F32)
-    grad_hidden = dot(cotangent, full_down, NT)
-    grad_up_pre = jax.vjp(jax.nn.gelu, up_pre)[1](grad_hidden)[0].astype(BF)
-    grad_up = jnp.einsum("td,tf->df", normed_two, grad_up_pre, preferred_element_type=F32)
-    grad_normed_two = dot(grad_up_pre, full_up, NT)
-    grad_attended = grad_output + norm_backward(
-        grad_normed_two, scaled_two, inverse_two, gain_rows[1]
-    )
-    attended_low = grad_attended.astype(BF)
-    grad_wout = jnp.einsum("td,te->de", mixed_low, attended_low, preferred_element_type=F32)
-    grad_mixed = dot(attended_low, full_out, NT)
-    grad_gate = (
-        jnp.sum((grad_mixed * (recalled - local_out)).reshape(count, H, HD), axis=(0, 2))
-        * gate_open
-        * (1.0 - gate_open)
-    )
-    grad_recalled = (gate_row * grad_mixed).astype(BF)
-    delta = jnp.sum(
-        (grad_recalled.astype(F32) * recalled).reshape(count, H, HD), axis=-1
-    ).T
-    sent = (grad_recalled, jnp.concatenate([delta, total_lse], axis=0))
-    sent_core, sent_x = swap(sent, 1), swap(sent, 2)
-    sent_cross = swap(sent_x, 1)
-
-    grad_query_local, grad_keys, grad_values, diagonals, totals = segment_backward(
-        gate_open, grad_mixed, queries, keys_values, xl_cache, probs_local
+    output, grad_attended, grad_wout, grad_up, grad_down, grad_local, grad_recalled, aux, sums = feed(
+        jnp.stack([own_out, core_out, far_out]),
+        jnp.stack([own_lse, core_lse, far_lse]),
+        local_out,
+        tokens,
+        cotangent,
+        jnp.repeat(gate_open, HD)[None],
+        norm_rows,
+        full_out,
+        full_up,
+        full_down,
+    )
+    grad_gate = jnp.sum(sums[2].reshape(H, HD), axis=1) * gate_open * (1.0 - gate_open)
+    grad_query, grad_keys, grad_values, diagonals, totals, share_out, share_up, share_down = attend_grad(
+        grad_recalled,
+        aux,
+        grad_local,
+        queries,
+        keys_values,
+        xl_cache,
+        probs_local,
+        table,
+        probs_all,
+        lse_all,
+        [g.reshape(devices, -1, g.shape[1]) for g in (grad_wout, grad_up, grad_down)],
+        ("yxz", "yxz", "xyz"),
+        1,
     )
     grad_table = table_gradient(diagonals, totals)
-
-    def recall_back(left, right, lse, first):
-        delta_rows = jnp.concatenate([left[1][:H], right[1][:H]], axis=1)
-        total_rows = jnp.concatenate([left[1][H:], right[1][H:]], axis=1)
-        return recall_grad(
-            left[0],
-            right[0],
-            table,
-            probs_all,
-            first,
-            delta_rows[:, None],
-            jnp.exp(lse - total_rows)[:, None],
-        )
-
-    back_x, back_cross = recall_back(sent_x, sent_cross, lse_far, H)
-    back_own, back_core = recall_back(sent, sent_core, lse_chip, 0)
-    pair_back = (back_x.astype(F32) + swap(back_cross, 1).astype(F32)).astype(BF)
-    grad_query = (
-        grad_query_local
-        + back_own.astype(F32)
-        + swap(back_core, 1).astype(F32)
-        + swap(pair_back, 2).astype(F32)
-    )
-    grad_qkv_low = jnp.concatenate([grad_query.astype(BF), grad_keys, grad_values], axis=1)
+    grad_qkv_low = jnp.concatenate([grad_query, grad_keys, grad_values], axis=1)
     grad_wqkv = jnp.einsum("td,te->de", normed_one, grad_qkv_low, preferred_element_type=F32)
     grad_normed_one = dot(grad_qkv_low[:, :width], full_q, NT) + dot(
         grad_qkv_low[:, width:], full_kv, NT
@@ -989,29 +1290,31 @@
     grad_norms = jnp.stack(
         [
             jnp.sum(grad_normed_one * scaled_one, axis=0),
-            jnp.sum(grad_normed_two * scaled_two, axis=0),
+            sums[0],
             jnp.sum(grad_normed_one, axis=0),
-            jnp.sum(grad_normed_two, axis=0),
+            sums[1],
         ]
     )
     rest = jnp.pad(jnp.concatenate([grad_table.reshape(-1), grad_gate]), (0, 1024 - 264))
     small = jnp.concatenate([grad_norms.reshape(-1, 128), rest.reshape(-1, 128)], axis=0)
-    share_qkv, share_out, share_up, share_down, small = scatter_sums(
+    half = grad_wqkv.shape[1] // 2
+    share_left, share_right, small = scatter_sums(
         [
-            g.astype(BF).reshape(devices, -1, g.shape[1])
-            for g in (grad_wqkv, grad_wout, grad_up, grad_down)
+            g.astype(BF).reshape(devices, -1, half)
+            for g in (grad_wqkv[:, :half], grad_wqkv[:, half:])
         ],
-        ("yxz", "xyz", "xyz", "yxz"),
+        ("yxz", "xyz"),
         small,
         2,
     )
+    share_qkv = jnp.concatenate([share_left, share_right], axis=1)
     share_norms = lax.dynamic_slice_in_dim(
         small[:32].reshape(4, width), number * own, own, axis=1
     )
     rest = small[32:].reshape(-1)
     table_total, gate_total = rest[: BUCKETS * H].reshape(BUCKETS, H), rest[BUCKETS * H :][:H]
     return (
-        output.astype(BF),
+        output,
         grad_tokens,
         share_norms[:2],
         share_norms[2:],

time: 610 us -> 483 us (0.79)
  matrix products: 93.2 us -> 16 us
  waiting for transfers between devices: 23.8 us -> 2.29 us
  Pallas kernels: 408 us -> 399 us
  local copies, waits for them, and re-layouts: 45.1 us -> 36.3 us
    pallas_call x3 -> x2, Pallas kernels: 58 us -> 187 us  [the longest x1 141 us: attend_grad(): pl.pallas_call(functools.partial(attend_grad_kernel, n_hi, orders), grid=...]
    pallas_call x1, Pallas kernels: 125 us -> 42.6 us  [scatter_sums(): pl.pallas_call(functools.partial(scatter_kernel, n_hi, orders), out_shape...]
    pallas_call x1, Pallas kernels: 211 us -> 155 us  [attend(): pl.pallas_call(functools.partial(attend_kernel, n_hi, orders), grid=(2, H...]
    dot_general x9 -> x3, matrix products: 61.7 us -> 9.84 us  [dot(): return lax.dot_general(left, right, dims, preferred_element_type=F32)]
    dot_general x3 -> x0, matrix products: 25.5 us -> none  [the longest x1 13.2 us: local(): jnp.einsum('tf,td->fd', hidden, cotangent, preferred_element_type=F32)]
    ppermute x15 -> x6, waiting for transfers between devices: 23.8 us -> 2.29 us  [swap(): lax.ppermute(v, 'mem', [(i, i ^ turn) for i in range(lax.axis_size('mem'))])]
    unnamed x135 -> x71, local copies, waits for them, and re-layouts: 30.3 us -> 18.2 us
    slice x1 -> x2, local copies, waits for them, and re-layouts: 0.01 us -> 6.76 us  [the longest x1 5.88 us: local(): grad_wqkv[:, half:]]
  transfers between devices with their start and end apart: 15 -> 6, of which waited for: 4 -> 2; matrix products, arithmetic and copies ran while one was open for 12% -> 3% of each run, Pallas kernels for 12% -> 3%
where the time goes in v4:
time: 483 us; the launch traced here: 474 us
  Pallas kernels  399 us (83%)
  local copies, waits for them, and re-layouts  36.3 us (8%)
  matrix products  16 us (3%)
  other arithmetic  15.1 us (3%)
    pallas_call x1, Pallas kernels, attend(): pl.pallas_call(functools.partial(attend_kernel, n_hi, orders), grid=(2, H...  155 us
    pallas_call x1, Pallas kernels, attend_grad(): pl.pallas_call(functools.partial(attend_grad_kernel, n_hi, orders), grid=...  141 us
    pallas_call x1, Pallas kernels, feed(): pl.pallas_call(feed_kernel, grid=(hidden // block,), in_specs=[IN_VMEM] *...  46.8 us
    pallas_call x1, Pallas kernels, scatter_sums(): pl.pallas_call(functools.partial(scatter_kernel, n_hi, orders), out_shape...  42.6 us
    unnamed x71, local copies, waits for them, and re-layouts  18.2 us
    pallas_call x1, Pallas kernels, segment_forward(): pl.pallas_call(segment_kernel, grid=(H,), in_specs=[SCALARS, per_head(1,...  13.8 us
    dot_general x3, matrix products, dot(): return lax.dot_general(left, right, dims, preferred_element_type=F32)  9.84 us
  transfers between devices with their start and end apart: 6, of which 2 were waited for; matrix products, arithmetic and copies ran while one was open for 3% of the time, Pallas kernels for 3%

profile of v4, /device:TPU:0, one launch (start us, length us, event | category | flops | bytes accessed | tf_op | source)
XLA Modules:
  0.0 474.4 jit_solution(4285859304094230495)
XLA Ops:
  0.7 0.9 slice.80.refs_5_
  2.5 8.4 %copy.55 = bf16[2048,8,256]{2,0,1:T(8,128)(2,1)} copy(bf16[2048,8,256]{2,1,0:T(8,128)(2,1)} %param.27) | data formatting | bytes 16777216 | tf_op args[10]
  11.9 155.3 %shard_map.240 = (bf16[512,1024]{1,0:T(8,128)(2,1)}, bf16[512,1024]{1,0:T(8,128)(2,1)}, f32[16,1024]{1,0:T(8,128)S(1)}, bf16[2048,1024]{1,0:T(8,128)(2,1)}, f32[...) custom-call(bf16[512,1024]{1,0:T(8,128)(2,1)} %x_ref.1, ...), custom_call_target="tpu_custom_call" | custom-call | flops 17179869184 | bytes 134217728 | tf_op jit(solution)/shard_map/pallas_call | solution.py:616
  167.9 3.6 slice_bitcast_fusion
  174.1 0.9 collective-permute-done.2
  176.2 3.6 fusion.17
  179.8 1.5 collective-permute-start.3
  181.3 2.3 convolution_convert_fusion.1.kn_ref.vn_ref.refs_5_.refs_7_
  184.3 13.8 %shard_map.241 = (f32[512,1024]{1,0:T(8,128)S(1)}, bf16[8,1024,512]{2,1,0:T(8,128)(2,1)S(1)}) custom-call(s32[1]{0:T(128)S(6)} %copy.59.len_ref, f32[8,1,256]{2,1,0:T(1,128)S(1)} %broadcast_in_dim.44.near_ref, bf16[512,1024]{1,0:T(8,128)(2,1)S(1)} %copy-done.3, bf16[512,2048]{1,0:T(8,128)(2,1)S(1)} %copy-done, ...), custom_call_target="tpu_custom_call" | custom-call | flops 2147483648 | bytes 20971520 | tf_op jit(solution)/shard_map/pallas_call | solution.py:789
  198.2 1.3 copy-done.1
  199.5 3.3 copy-done.2
  202.8 1.3 copy-done.6
  204.2 1.4 collective-permute-done.5
  206.2 3.2 pad_maximum_fusion.parts_ref
  210.1 46.8 %shard_map.242 = (bf16[512,1024]{1,0:T(8,128)(2,1)}, f32[512,1024]{1,0:T(8,128)}, bf16[1024,1024]{1,0:T(8,128)(2,1)}, bf16[1024,4096]{1,0:T(8,128)(2,1)}, bf16[4...) custom-call(bf16[3,512,1024]{2,1,0:T(8,128)(2,1)} %pad_maximum_fusio, ...), custom_call_target="tpu_custom_call" | custom-call | flops 25769803776 | bytes 37748736 | tf_op jit(solution)/shard_map/pallas_call | solution.py:1118
  256.9 0.9 fusion.38
  257.8 140.6 %shard_map.243 = (bf16[512,1024]{1,0:T(8,128)(2,1)}, bf16[512,1024]{1,0:T(8,128)(2,1)}, bf16[512,1024]{1,0:T(8,128)(2,1)}, f32[8,1,256]{2,1,0:T(1,128)}, f32[8,8...) custom-call(bf16[512,1024]{1,0:T(8,128)(2,1)} %get-tuple-element.55.refs_0_, ...), custom_call_target="tpu_custom_call" | custom-call | flops 17179869184 | bytes 134217728 | tf_op jit(solution)/shard_map/pallas_call | solution.py:985
  398.5 3.3 fusion.40
  401.9 6.0 %convolution_convert_fusion = bf16[1024,3072]{1,0:T(8,128)(2,1)} fusion(bf16[512,1024]{1,0:T(8,128)(2,1)S(1)} %copy-done.32, bf16[512,1024]{1,0:T(8,128)(2,1)S(1)} %copy-done.26, bf16[512,1024]{1,0:T(8,128)(2,1)S(1)} %copy-done.25, bf16[512,1024]{1,0:T(8,128)(2,1)S(1)} %copy-done.27), kind=kOutput, calls=%fused_computation.1 | convolution fusion | flops 3233808384 | bytes 10485760 | tf_op jit(solution)/shard_map/td,te->de/dot_general | solution.py:1283
  408.0 4.2 fusion.14
  413.0 5.9 %fusion.37 = (bf16[1024,1536]{1,0:T(8,128)(2,1)}, bf16[1024,1536]{1,0:T(8,128)(2,1)}) fusion(bf16[1024,3072]{1,0:T(8,128)(2,1)} %convolution_convert_fusion), kind=kLoop, calls=%fused_computation.83 | loop fusion | bytes 12582912 | tf_op jit(solution)/shard_map/slice | solution.py:1304
  419.5 42.6 %shard_map.244 = (f32[32,1536]{1,0:T(8,128)}, f32[32,1536]{1,0:T(8,128)}, f32[40,128]{1,0:T(8,128)}) custom-call(bf16[32,32,1536]{2,1,0:T(8,128)(2,1)} %bitcast.72, bf16[32,32,1536]{2,1,0:T(8,128)(2,1)} %bitcast.71, f32[40,128]{1,0:T(8,128)} %pad_maximum_fusion.3.refs_2_), custom_call_target="tpu_custom_call" | custom-call | tf_op jit(solution)/shard_map/pallas_call | solution.py:436
  466.2 1.8 pad_maximum_fusion.1
  468.0 3.7 fusion.13
  (129 shorter events, 15.3 us)
Async XLA Ops:
  2.5 8.4 %copy-start.23 = (bf16[2,32]{1,0:T(2,128)(2,1)S(1)}, bf16[2,32]{1,0:T(2,128)(2,1)}, u32[]{:S(2)}) copy-start(bf16[2,32]{1,0:T(2,128)(2,1)} %param.19) | copy-start | bytes 388
  2.5 8.4 %copy-start.24 = (bf16[2,32]{1,0:T(2,128)(2,1)S(1)}, bf16[2,32]{1,0:T(2,128)(2,1)}, u32[]{:S(2)}) copy-start(bf16[2,32]{1,0:T(2,128)(2,1)} %param.18) | copy-start | bytes 388
  2.5 8.6 %copy-start.15 = (s32[2048,8,8]{0,2,1:T(8,128)S(1)}, s32[2048,8,8]{0,2,1:T(8,128)}, u32[]{:S(2)}) copy-start(s32[2048,8,8]{0,2,1:T(8,128)} %param.28) | copy-start | bytes 1572868
  167.2 4.3 copy-start.4
  167.2 36.9 %copy-start.5 = (f32[16,1024]{1,0:T(8,128)}, f32[16,1024]{1,0:T(8,128)S(1)}, u32[]{:S(2)}) copy-start(f32[16,1024]{1,0:T(8,128)S(1)} %get-tuple-element.49.norms_ref) | copy-start | bytes 196612
  167.3 6.5 %collective-permute-start.1 = (f32[8,512]{1,0:T(8,128)S(1)}, f32[8,512]{1,0:T(8,128)S(1)}, u32[]{:S(2)}, u32[]{:S(2)}) collective-permute-start(f32[8,512]{1,0:T(8,128)S(1)} %slice.104), channel_id=1, source_target_pairs={{0,1},{1,0},{2,3},{3,2},{4,5},{5,4},{6,7},{7,6},{8,9},{9,8},{10,11... | collective-permute-start | bytes 49160 | tf_op jit(solution)/shard_map/ppermute | solution.py:1177
  167.4 36.7 %collective-permute-start.4 = (f32[8,512]{1,0:T(8,128)S(1)}, f32[8,512]{1,0:T(8,128)S(1)}, u32[]{:S(2)}, u32[]{:S(2)}) collective-permute-start(f32[8,512]{1,0:T(8,128)S(1)} %get-tuple-element.127), channel_id=1, source_target_pairs={{0,1},{1,0},{2,3},{3,2},{4,5},{5,4},{6,7},{7,6},{8,9},{9,8},{10,11... | collective-permute-start | bytes 49160 | tf_op jit(solution)/shard_map/ppermute | solution.py:1177
  167.9 4.3 copy-start.19
  171.5 3.5 collective-permute-start.2
  171.6 34.6 %collective-permute-start = (bf16[512,1024]{1,0:T(8,128)(2,1)}, bf16[512,1024]{1,0:T(8,128)(2,1)}, u32[]{:S(2)}, u32[]{:S(2)}) collective-permute-start(bf16[512,1024]{1,0:T(8,128)(2,1)} %get-tuple-element.116), channel_id=1, source_target_pairs={{0,1},{1,0},{2,3},{3,2},{4,5},{5,4},{6,7},{7,6},{8,9},{9,8},{10,11... | collective-permute-start | bytes 3145736 | tf_op jit(solution)/shard_map/ppermute | solution.py:1177
  176.2 5.1 %copy-start.28 = (f32[8]{0:T(128)S(1)}, f32[8]{0:T(128)}, u32[]{:S(2)}) copy-start(f32[8]{0:T(128)} %param.25) | copy-start | bytes 100
  176.2 5.1 %copy-start.29 = (bf16[32,32,2048]{2,1,0:T(8,128)(2,1)S(1)}, bf16[32,32,2048]{2,1,0:T(8,128)(2,1)}, u32[]{:S(2)}) copy-start(bf16[32,32,2048]{2,1,0:T(8,128)(2,1)} %get-tuple-element.47) | copy-start | bytes 12582916
  176.2 5.1 %copy-start.31 = (bf16[512,1024]{1,0:T(8,128)(2,1)S(1)}, bf16[512,1024]{1,0:T(8,128)(2,1)}, u32[]{:S(2)}) copy-start(bf16[512,1024]{1,0:T(8,128)(2,1)} %get-tuple-element.46) | copy-start | bytes 3145732
  179.8 26.4 %collective-permute-start.3 = (bf16[512,1024]{1,0:T(8,128)(2,1)}, bf16[512,1024]{1,0:T(8,128)(2,1)S(1)}, u32[]{:S(2)}, u32[]{:S(2)}) collective-permute-start(bf16[512,1024]{1,0:T(8,128)(2,1)} %fusion.17), channel_id=1, source_target_pairs={{0,2},{1,3},{2,0},{3,1},{4,6},{5,7},{6,4},{7,5},{8,10},{9,11},{10,... | collective-permute-start | bytes 3145736 | tf_op jit(solution)/shard_map/ppermute | solution.py:1177
  183.7 21.9 %collective-permute-start.5 = (f32[8,512]{1,0:T(8,128)S(1)}, f32[8,512]{1,0:T(8,128)S(1)}, u32[]{:S(2)}, u32[]{:S(2)}) collective-permute-start(f32[8,512]{1,0:T(8,128)S(1)} %get-tuple-element.111), channel_id=1, source_target_pairs={{0,2},{1,3},{2,0},{3,1},{4,6},{5,7},{6,4},{7,5},{8,10},{9,11},{10,... | collective-permute-start | bytes 49160 | tf_op jit(solution)/shard_map/ppermute | solution.py:1177
  401.8 6.1 %copy-start.11 = (bf16[512,1024]{1,0:T(8,128)(2,1)S(1)}, bf16[512,1024]{1,0:T(8,128)(2,1)}, u32[]{:S(2)}) copy-start(bf16[512,1024]{1,0:T(8,128)(2,1)} %x_ref.1) | copy-start | bytes 3145732
  401.9 6.1 %copy-start.30 = (bf16[32,32,2048]{2,1,0:T(8,128)(2,1)S(1)}, bf16[32,32,2048]{2,1,0:T(8,128)(2,1)}, u32[]{:S(2)}) copy-start(bf16[32,32,2048]{2,1,0:T(8,128)(2,1)} %get-tuple-element.47) | copy-start | bytes 12582916
  407.9 4.3 copy-start.21
  407.9 4.5 copy-start.18
  407.9 4.6 copy-start.17
  408.0 4.6 copy-start.22
  419.5 48.4 %copy-start.12 = (f32[512,1024]{1,0:T(8,128)S(1)}, f32[512,1024]{1,0:T(8,128)}, u32[]{:S(2)}) copy-start(f32[512,1024]{1,0:T(8,128)} %get-tuple-element.54) | copy-start | bytes 6291460
  468.0 4.4 copy-start.14
  468.0 5.2 %copy-start.13 = (f32[128,1024]{1,0:T(8,128)S(1)}, f32[128,1024]{1,0:T(8,128)}, u32[]{:S(2)}) copy-start(f32[128,1024]{1,0:T(8,128)} %get-tuple-element.154) | copy-start | bytes 1572868
  (15 other events, 37.8 us)

commit v5 on v4

--- a/solution.py
+++ b/solution.py
@@ -449,8 +449,7 @@
     )(*arrays, small)
 
 
-FIRST_STOP, LAST_STOP = 2, 62
-AHEAD = 0
+FIRST_STOP, FIRST_SPAN, LAST_SPAN = 2, 60, 88
 
 
 def pick_scores(queries, table_ref, chosen, pause):
@@ -467,12 +466,12 @@
     return picked * SCALE
 
 
-def recall_values(scores, table_ref, chosen, lse_ref, p_ref, pause):
+def recall_values(scores, table_ref, chosen, put_lse, p_ref, pause):
     slots, tokens, step = table_ref.shape[1], chosen.shape[1], 256
     top = jnp.max(scores, axis=0, keepdims=True)
     weights = jnp.exp(scores - top)
     total = jnp.sum(weights, axis=0, keepdims=True)
-    lse_ref[0] = top + jnp.log(total)
+    put_lse(top + jnp.log(total))
     times = jnp.ones_like(weights)
     for turn in range(1, 8):
         times = times + jnp.where(pltpu.roll(chosen, turn, 0) == chosen, 1.0, 0.0)
@@ -492,41 +491,79 @@
     return out.T.astype(BF)
 
 
+def rows_of(blocks, at, count):
+    block = blocks[:, :, pl.ds(at, count)]
+    if block.shape[1] % 16:
+        block = block.astype(F32)
+    return block.reshape(-1, count).astype(BF)
+
+
+def combined(outs, lses):
+    top = functools.reduce(jnp.maximum, lses)
+    total = top + jnp.log(sum(jnp.exp(lse - top) for lse in lses))
+    shares = [jnp.exp(lse - total).T for lse in lses]
+    heads = [
+        sum(
+            share[:, h : h + 1] * out[:, h * HD : (h + 1) * HD].astype(F32)
+            for share, out in zip(shares, outs)
+        )
+        for h in range(H)
+    ]
+    return heads, total
+
+
 def attend_kernel(n_hi, orders, *refs):
     n = len(orders) - 2
-    x_ref, table_ref, slot_ref = refs[:3]
-    early_in, late_in = refs[3:5], refs[5 : 5 + n]
-    normed_ref, q_ref, norms_ref, out_ref, lse_ref, p_ref, full_q = refs[5 + n : 12 + n]
-    late_out = refs[12 + n : 12 + 2 * n]
-    wq, norms, asked, keep_sem, q_send, q_recv = refs[12 + 2 * n : 18 + 2 * n]
-    sems = refs[18 + 2 * n :]
+    len_ref, near_ref, x_ref, table_ref, slot_ref, kc_ref, vc_ref = refs[:7]
+    early_in, late_in, refs = refs[7:9], refs[9 : 9 + n], refs[9 + n :]
+    normed_ref, q_ref, kv_ref, norms_ref, lse_ref, p_ref, local_ref, plocal_ref = refs[:8]
+    parts_ref, lses_ref, full_q, full_kv = refs[8:12]
+    late_out, refs = refs[12 : 11 + n], refs[11 + n :]
+    wq, wkv, norms, asked, outs, landed, lses, landed_lses = refs[:8]
+    keep_sem, q_send, q_recv, back_send, back_recv, lse_send, lse_recv = refs[8:15]
+    sems = refs[15:]
     phase, head = pl.program_id(0), pl.program_id(1)
     tick = phase * H + head
+    ticks = 2 * H
     place = Place(n_hi)
     early = Gather(place, orders[:2], early_in, (wq, norms), sems[:3])
-    late = Gather(place, orders[2:], late_in, late_out, sems[3:])
-    rows = x_ref.shape[0]
-
-    def ask(src, slot, to):
+    late = Gather(place, orders[2:], late_in, (wkv,) + tuple(late_out), sems[3:])
+    rows, width = x_ref.shape
+    lanes = pl.ds(pl.multiple_of(head * HD, HD), HD)
+
+    def remote(src, dst, send, recv, to):
         return pltpu.make_async_remote_copy(
             src_ref=src,
-            dst_ref=asked.at[slot],
-            send_sem=q_send.at[slot],
-            recv_sem=q_recv.at[slot],
+            dst_ref=dst,
+            send_sem=send,
+            recv_sem=recv,
             device_id=place.device(to),
             device_id_type=MESH,
         )
 
-    def keep():
-        return pltpu.make_async_copy(wq, full_q, keep_sem)
+    def ask(slot, to):
+        src = q_ref if slot < 3 else asked.at[2]
+        return remote(src, asked.at[slot], q_send.at[slot], q_recv.at[slot], to)
+
+    def give(slot, to):
+        part = (1, 3, 2)[slot]
+        return [
+            remote(outs.at[part], landed.at[slot], back_send.at[slot], back_recv.at[slot], to),
+            remote(lses.at[part], landed_lses.at[slot], lse_send.at[slot], lse_recv.at[slot], to),
+        ]
+
+    def given(slot):
+        place.arrived(landed.at[slot], back_recv.at[slot])
+        place.arrived(landed_lses.at[slot], lse_recv.at[slot])
+
+    def keep(k):
+        return pltpu.make_async_copy((wq, wkv)[k], (full_q, full_kv)[k], keep_sem.at[k])
 
     @pl.when(tick == 0)
     def _():
         place.greet()
         for a in range(2):
             early.begin(a)
-        for a in range(AHEAD):
-            late.begin(a)
         x = x_ref[...].astype(F32)
         center = x - jnp.mean(x, axis=-1, keepdims=True)
         scaled = center * lax.rsqrt(jnp.mean(center * center, axis=-1, keepdims=True) + EPSILON)
@@ -535,137 +572,210 @@
                 early.level(a, hops)
         for a in range(2):
             early.finish(a)
-        keep().start()
+        keep(0).start()
         share = norms.shape[0] // H
-        lanes = [
+        groups = [
             functools.reduce(jnp.add, [norms[g * share + k].astype(F32) for k in range(share)])
             for g in range(H)
         ]
-        norm_rows = jnp.concatenate(lanes, axis=1)
+        norm_rows = jnp.concatenate(groups, axis=1)
         norms_ref[...] = norm_rows
         normed = (scaled * norm_rows[0:1] + norm_rows[2:3]).astype(BF)
         normed_ref[...] = normed
-        for at in range(0, wq.shape[2], 256):
-            weights = wq[:, :, pl.ds(at, 256)]
-            if weights.shape[1] % 16:
-                weights = weights.astype(F32)
-            weights = weights.reshape(-1, 256).astype(BF)
-            q_ref[:, pl.ds(at, 256)] = dot(normed, weights).astype(BF)
-        ask(q_ref, 1, ALONG_CORE).start()
-        ask(q_ref, 2, ALONG_X).start()
-        for a in range(AHEAD, n):
+        for at in range(0, width, 256):
+            q_ref[:, pl.ds(at, 256)] = dot(normed, rows_of(wq, at, 256)).astype(BF)
+        ask(1, ALONG_CORE).start()
+        ask(2, ALONG_X).start()
+        for a in range(n):
             late.begin(a)
         asked[0] = q_ref[...]
         place.arrived(asked.at[1], q_recv.at[1])
 
-    events = [
-        functools.partial(late.level, a, hops) for hops in late.levels() for a in range(n)
-    ]
-    ticks = 2 * H
-    stops = 4 * ticks
-    stop_of = [FIRST_STOP + k * (LAST_STOP - FIRST_STOP) // len(events) for k in range(len(events))]
-
-    def pause(part):
-        for at in range(part, stops, 4):
-            mine = [event for event, stop in zip(events, stop_of) if stop == at]
+    events = []
+    for level, hops in enumerate(late.levels()):
+        for a in range(n):
+            span = FIRST_SPAN if a == 0 else LAST_SPAN
+            stop = FIRST_STOP + (level * n + a) * span // (n * len(late.levels()))
+            events.append((min(stop, 4 * ticks - 1 if a == 0 else 12 * H - 1), (a, hops)))
+
+    def pause(part, first=0, end=4 * ticks):
+        for at in range(first + part, end, 4):
+            mine = [event for stop, event in events if stop == at]
             if mine:
 
                 @pl.when(tick == at // 4)
-                def _():
+                def _(mine=mine):
                     for event in mine:
-                        event()
-
-    pause(0)
+                        late.level(*event)
 
     @pl.when(tick == H)
     def _():
+        for copy in give(0, ALONG_CORE):
+            copy.start()
         place.arrived(asked.at[3], q_recv.at[3])
 
-    queries = asked[pl.ds(phase * 2, 2), :, pl.ds(pl.multiple_of(head * HD, HD), HD)]
-    chosen = slot_ref[0]
-    scores = pick_scores(queries.reshape(2 * rows, HD), table_ref, chosen, lambda: pause(1))
-
-    @pl.when(tick == H - 2)
-    def _():
-        place.arrived(asked.at[2], q_recv.at[2])
-        ask(asked.at[2], 3, ALONG_CORE).start()
-
-    pause(2)
-    out_ref[...] = recall_values(scores, table_ref, chosen, lse_ref, p_ref, lambda: pause(3))
-
-    @pl.when(tick == ticks - 1)
-    def _():
-        for a in range(n):
+    @pl.when(phase < 2)
+    def _():
+        pause(0)
+        queries = asked[pl.ds(phase * 2, 2), :, lanes].reshape(2 * rows, HD)
+        chosen = slot_ref[0]
+        scores = pick_scores(queries, table_ref, chosen, lambda: pause(1))
+
+        @pl.when(tick == H - 2)
+        def _():
+            place.arrived(asked.at[2], q_recv.at[2])
+            ask(3, ALONG_CORE).start()
+
+        pause(2)
+
+        def put_lse(row):
+            lse_ref[0] = row
+            for k in range(2):
+                lses[phase * 2 + k, pl.ds(head, 1), :] = row[:, k * rows : (k + 1) * rows]
+
+        out = recall_values(scores, table_ref, chosen, put_lse, p_ref, lambda: pause(3))
+        outs[pl.ds(phase * 2, 2), :, lanes] = out.reshape(2, rows, HD)
+
+    @pl.when(tick == ticks)
+    def _():
+        for copy in give(1, ALONG_CORE):
+            copy.start()
+        late.finish(0)
+        keep(1).start()
+        for at in range(0, 2 * width, 256):
+            kv_ref[:, pl.ds(at, 256)] = dot(normed_ref[...], rows_of(wkv, at, 256)).astype(BF)
+        given(1)
+        heads, total = combined((outs[2], landed[1]), (lses[2], landed_lses[1]))
+        for h in range(H):
+            outs[2, :, pl.ds(h * HD, HD)] = heads[h].astype(BF)
+        lses[2] = total
+        for copy in give(2, ALONG_X):
+            copy.start()
+
+    @pl.when(phase == 2)
+    def _():
+        for part in range(4):
+            pause(part, 4 * ticks, 12 * H)
+        fresh = pl.ds(pl.multiple_of(width + head * HD, HD), HD)
+        segment_forward(
+            len_ref[0],
+            near_ref[0],
+            q_ref[:, lanes],
+            kc_ref[...],
+            kv_ref[:, lanes],
+            vc_ref[...],
+            kv_ref[:, fresh],
+            local_ref,
+            plocal_ref,
+        )
+
+    @pl.when(tick == ticks + H - 1)
+    def _():
+        given(0)
+        given(2)
+        for k, (part, lse) in enumerate(
+            ((outs[0], lses[0]), (landed[0], landed_lses[0]), (landed[2], landed_lses[2]))
+        ):
+            parts_ref[k] = part
+            lses_ref[k] = lse
+        for a in range(1, n):
             late.finish(a)
-        ask(q_ref, 1, ALONG_CORE).wait_send()
-        ask(q_ref, 2, ALONG_X).wait_send()
-        ask(asked.at[2], 3, ALONG_CORE).wait_send()
-        keep().wait()
-
-
-def attend(x, table, chosen, early, late, orders, collective_id):
+        for slot, to in ((1, ALONG_CORE), (2, ALONG_X), (3, ALONG_CORE)):
+            ask(slot, to).wait_send()
+        for slot, to in ((0, ALONG_CORE), (1, ALONG_CORE), (2, ALONG_X)):
+            for copy in give(slot, to):
+                copy.wait_send()
+        for k in range(2):
+            keep(k).wait()
+
+
+def attend(length, near, x, table, chosen, cache, early, late, orders, collective_id):
     n, n_hi = len(late), lax.axis_size("dp") // 2
     devices = n_hi * 8
     (rows, width), slots = x.shape, table.shape[1]
-    whole = pl.BlockSpec((rows, width), lambda p, h: (0, 0))
     dma = pltpu.SemaphoreType.DMA
+    shape = jax.ShapeDtypeStruct
 
     def gathered(a):
-        return jax.ShapeDtypeStruct((devices,) + a.shape, a.dtype)
+        return shape((devices,) + a.shape, a.dtype)
+
+    def asked_head(p, h):
+        return jnp.where(p < 2, h, H - 1)
+
+    def segment_head(p, h):
+        return jnp.where(p < 2, 0, h)
+
+    def column(first=0):
+        return pl.BlockSpec((rows, HD), lambda p, h: (0, first + segment_head(p, h)))
 
     return pl.pallas_call(
         functools.partial(attend_kernel, n_hi, orders),
-        grid=(2, H),
+        grid=(3, H),
         in_specs=[
-            whole,
-            pl.BlockSpec((1, slots, 2 * HD), lambda p, h: (h, 0, 0)),
-            pl.BlockSpec((1, 8, 2 * rows), lambda p, h: (h, 0, p)),
+            SCALARS,
+            pl.BlockSpec((1, 1, 2 * NEAR), lambda p, h: (segment_head(p, h), 0, 0)),
+            IN_VMEM,
+            pl.BlockSpec((1, slots, 2 * HD), lambda p, h: (asked_head(p, h), 0, 0)),
+            pl.BlockSpec((1, 8, 2 * rows), lambda p, h: (asked_head(p, h), 0, jnp.minimum(p, 1))),
+            column(),
+            column(H),
         ]
         + [ANYWHERE] * (2 + n),
         out_specs=[
-            whole,
-            whole,
-            pl.BlockSpec((16, width), lambda p, h: (0, 0)),
-            pl.BlockSpec((2 * rows, HD), lambda p, h: (p, h)),
-            pl.BlockSpec((1, 1, 2 * rows), lambda p, h: (h, 0, p)),
-            pl.BlockSpec((1, slots, 2 * rows), lambda p, h: (p * H + h, 0, 0)),
+            IN_VMEM,
+            IN_VMEM,
+            IN_VMEM,
+            IN_VMEM,
+            pl.BlockSpec((1, 1, 2 * rows), lambda p, h: (asked_head(p, h), 0, jnp.minimum(p, 1))),
+            pl.BlockSpec(
+                (1, slots, 2 * rows), lambda p, h: (jnp.minimum(p * H + h, 2 * H - 1), 0, 0)
+            ),
+            column(),
+            pl.BlockSpec((1, 2 * W, W), lambda p, h: (segment_head(p, h), 0, 0)),
+            IN_VMEM,
+            IN_VMEM,
         ]
         + [ANYWHERE] * (1 + n),
         out_shape=[
-            jax.ShapeDtypeStruct(x.shape, BF),
-            jax.ShapeDtypeStruct(x.shape, BF),
-            jax.ShapeDtypeStruct((16, width), F32),
-            jax.ShapeDtypeStruct((4 * rows, width), BF),
-            jax.ShapeDtypeStruct((H, 1, 4 * rows), F32),
-            jax.ShapeDtypeStruct((2 * H, slots, 2 * rows), BF),
+            shape((rows, width), BF),
+            shape((rows, width), BF),
+            shape((rows, 2 * width), BF),
+            shape((16, width), F32),
+            shape((H, 1, 4 * rows), F32),
+            shape((2 * H, slots, 2 * rows), BF),
+            shape((rows, width), F32),
+            shape((H, 2 * W, W), BF),
+            shape((3, rows, width), BF),
+            shape((3, H, rows), F32),
             gathered(early[0]),
         ]
         + [gathered(a) for a in late],
         scratch_shapes=[
             pltpu.VMEM((devices,) + early[0].shape, BF),
+            pltpu.VMEM((devices,) + late[0].shape, BF),
             pltpu.VMEM((devices,) + early[1].shape, BF),
             pltpu.VMEM((4, rows, width), BF),
-            dma(()),
+            pltpu.VMEM((4, rows, width), BF),
+            pltpu.VMEM((3, rows, width), BF),
+            pltpu.VMEM((4, H, rows), F32),
+            pltpu.VMEM((3, H, rows), F32),
+            dma((2,)),
             dma((4,)),
             dma((4,)),
+            dma((3,)),
+            dma((3,)),
+            dma((3,)),
+            dma((3,)),
         ]
         + gather_sems(2, n_hi)
         + gather_sems(n, n_hi),
         compiler_params=pltpu.CompilerParams(
-            collective_id=collective_id, has_side_effects=True, vmem_limit_bytes=52 << 20
+            collective_id=collective_id, has_side_effects=True, vmem_limit_bytes=60 << 20
         ),
         cost_estimate=pl.CostEstimate(
             flops=16 * rows * slots * HD * H, bytes_accessed=128 << 20, transcendentals=0
         ),
-    )(x, table, chosen, *early, *late)
-
-
-def head_columns(rows, first=0):
-    return pl.BlockSpec((rows, HD), lambda h: (0, first + h))
-
-
-def per_head(*shape):
-    return pl.BlockSpec((1,) + shape, lambda h: (h,) + (0,) * len(shape))
+    )(length, near, x, table, chosen, cache, cache, *early, *late)
 
 
 def near_buckets():
@@ -694,10 +804,9 @@
     return (sums + far[:, None] * (np.arange(BUCKETS) == BUCKETS - 1)).T
 
 
-def segment_kernel(len_ref, near_ref, q_ref, kc_ref, kn_ref, vc_ref, vn_ref, out_ref, p_ref):
-    length = len_ref[0]
+def segment_forward(length, near, q, cached_keys, keys, cached_values, values, out_ref, p_ref):
     band = pltpu.roll(
-        jnp.broadcast_to(near_ref[0], (NEAR, 2 * NEAR)), 0, 1, stride=1, stride_axis=0
+        jnp.broadcast_to(near, (NEAR, 2 * NEAR)), 0, 1, stride=1, stride_axis=0
     )
     key_ids = lax.broadcasted_iota(jnp.int32, (NEAR, NEAR), 0)
     query_ids = lax.broadcasted_iota(jnp.int32, (NEAR, NEAR), 1)
@@ -705,16 +814,16 @@
     beside = band[:, NEAR:]
     masked = jnp.full((NEAR, NEAR), NEGATIVE, F32)
     zero = jnp.zeros((NEAR, NEAR), F32)
-    cache_t, values_t = vc_ref[...].T, vn_ref[...].T
+    cache_t, values_t = cached_values.T, values.T
     step = 2 * NEAR
     for at in range(W // step):
         count = 2 * (at + 1)
-        queries = q_ref[pl.ds(step * at, step), :]
-        cached = dot(kc_ref[...], queries, NT) * SCALE
+        queries = q[step * at : step * (at + 1)]
+        cached = dot(cached_keys, queries, NT) * SCALE
         if at == 0:
             last = cached[W - NEAR :] + jnp.concatenate([beside, zero], axis=1)
             cached = jnp.concatenate([cached[: W - NEAR], last], axis=0)
-        fresh = dot(kn_ref[pl.ds(0, NEAR * count), :], queries, NT) * SCALE
+        fresh = dot(keys[: NEAR * count], queries, NT) * SCALE
         rows = [cached]
         for k in range(count):
             block = fresh[NEAR * k : NEAR * (k + 1)]
@@ -785,31 +894,6 @@
     tot_ref[0] = total
 
 
-def segment_forward(queries, keys_values, cache, near, length):
-    return pl.pallas_call(
-        segment_kernel,
-        grid=(H,),
-        in_specs=[
-            SCALARS,
-            per_head(1, 2 * NEAR),
-            head_columns(W),
-            head_columns(W),
-            head_columns(W),
-            head_columns(W, H),
-            head_columns(W, H),
-        ],
-        out_specs=[head_columns(W), per_head(2 * W, W)],
-        out_shape=[
-            jax.ShapeDtypeStruct((W, H * HD), F32),
-            jax.ShapeDtypeStruct((H, 2 * W, W), BF),
-        ],
-        compiler_params=pltpu.CompilerParams(vmem_limit_bytes=32 << 20),
-        cost_estimate=pl.CostEstimate(
-            flops=8 * W * W * HD * H, bytes_accessed=20 << 20, transcendentals=0
-        ),
-    )(length, near, queries, cache, keys_values, cache, keys_values)
-
-
 def recall_back(grads, table_ref, p_ref, delta, share):
     slots, step = table_ref.shape[1], 512
     keys_t = table_ref[0, :, pl.ds(0, HD)].T
@@ -886,6 +970,7 @@
                 scatter.begin(z, a)
         asked[0] = grec_ref[...]
         aux[0] = aux_ref[...]
+        asked_arrived(1)
 
     events = []
     for k in range(n_hi + 2):
@@ -900,34 +985,20 @@
             for event in mine:
                 event()
 
-    @pl.when(tick < H)
-    def _():
-        segment_grad(
-            glocal_ref, q_ref, kc_ref, kn_ref, vc_ref, vn_ref, plocal_ref,
-            lambda at, value: glocal_q.__setitem__(
-                (pl.ds(at, value.shape[0]), pl.ds(pl.multiple_of(tick * HD, HD), HD)), value
-            ),
-            gk_ref, gv_ref, diag_ref, tot_ref,
-        )
-
-    @pl.when(tick == H)
-    def _():
-        asked_arrived(1)
-
-    @pl.when(tick == H + 2)
+    @pl.when(tick == H - 2)
     def _():
         asked_arrived(2)
         for copy in ask(3, ALONG_CORE):
             copy.start()
 
-    @pl.when(tick == 2 * H)
+    @pl.when(tick == H)
     def _():
         asked_arrived(3)
         give(0, ALONG_CORE).start()
 
-    @pl.when(tick >= H)
-    def _():
-        phase = tick // H - 1
+    @pl.when(tick < 2 * H)
+    def _():
+        phase = tick // H
         head = tick % H
         lanes = pl.ds(pl.multiple_of(head * HD, HD), HD)
         pair = pl.ds(phase * 2, 2)
@@ -940,12 +1011,30 @@
         result = recall_back(grads, table_ref, p_ref, delta, share)
         back[pair, :, lanes] = result.reshape(2, -1, HD)
 
-    @pl.when(tick == ticks - 1)
+    @pl.when(tick == 2 * H)
     def _():
         give(1, ALONG_CORE).start()
+
+    @pl.when(tick == 2 * H + 1)
+    def _():
         place.arrived(returned.at[1], back_recv.at[1])
         back[2] = (back[2].astype(F32) + returned[1].astype(F32)).astype(BF)
         give(2, ALONG_X).start()
+
+    @pl.when(tick >= 2 * H)
+    def _():
+        lanes = pl.ds(pl.multiple_of((tick - 2 * H) * HD, HD), HD)
+
+        def put_q(at, value):
+            glocal_q[pl.ds(at, value.shape[0]), lanes] = value
+
+        segment_grad(
+            glocal_ref, q_ref, kc_ref, kn_ref, vc_ref, vn_ref, plocal_ref,
+            put_q, gk_ref, gv_ref, diag_ref, tot_ref,
+        )
+
+    @pl.when(tick == ticks - 1)
+    def _():
         for a in range(n):
             scatter.last(a)
         place.arrived(returned.at[0], back_recv.at[0])
@@ -974,13 +1063,16 @@
     dma = pltpu.SemaphoreType.DMA
 
     def column(first=0):
-        return pl.BlockSpec((rows, HD), lambda t: (0, first + jnp.minimum(t, H - 1)))
+        return pl.BlockSpec((rows, HD), lambda t: (0, first + segment_head(t)))
 
     def head(*shape):
-        return pl.BlockSpec((1,) + shape, lambda t: (jnp.minimum(t, H - 1),) + (0,) * len(shape))
-
-    def later(t):
-        return jnp.maximum(t - H, 0)
+        return pl.BlockSpec((1,) + shape, lambda t: (segment_head(t),) + (0,) * len(shape))
+
+    def segment_head(t):
+        return jnp.maximum(t - 2 * H, 0)
+
+    def asked(t):
+        return jnp.minimum(t, 2 * H - 1)
 
     return pl.pallas_call(
         functools.partial(attend_grad_kernel, n_hi, orders),
@@ -995,9 +1087,9 @@
             column(H),
             column(H),
             head(2 * W, W),
-            pl.BlockSpec((1, slots, 2 * HD), lambda t: (later(t) % H, 0, 0)),
-            pl.BlockSpec((1, slots, 2 * rows), lambda t: (later(t), 0, 0)),
-            pl.BlockSpec((1, 1, 2 * rows), lambda t: (later(t) % H, 0, later(t) // H)),
+            pl.BlockSpec((1, slots, 2 * HD), lambda t: (asked(t) % H, 0, 0)),
+            pl.BlockSpec((1, slots, 2 * rows), lambda t: (asked(t), 0, 0)),
+            pl.BlockSpec((1, 1, 2 * rows), lambda t: (asked(t) % H, 0, asked(t) // H)),
         ]
         + [ANYWHERE] * n,
         out_specs=[IN_VMEM, column(), column(), head(1, 2 * NEAR), head(8, 2 * NEAR)]
@@ -1044,16 +1136,10 @@
 
     @pl.when(step == 0)
     def _():
-        lses = [lse_ref[k] for k in range(3)]
-        top = functools.reduce(jnp.maximum, lses)
-        total = top + jnp.log(sum(jnp.exp(lse - top) for lse in lses))
+        heads, total = combined([parts_ref[k] for k in range(3)], [lse_ref[k] for k in range(3)])
         aux_ref[H:, :] = total
-        shares = [jnp.exp(lse - total).T for lse in lses]
         for h in range(H):
-            at = pl.ds(h * HD, HD)
-            recalled[:, at] = sum(
-                shares[k][:, h : h + 1] * parts_ref[k, :, at].astype(F32) for k in range(3)
-            )
+            recalled[:, pl.ds(h * HD, HD)] = heads[h]
         mixed = (gate * recalled[...] + (1.0 - gate) * local_ref[...]).astype(BF)
         mixed_t[...] = mixed.T
         here = x_ref[...].astype(F32) + dot(mixed, wo_ref[...])
@@ -1172,22 +1258,6 @@
     return inverse * (grad_scaled - mean_grad - scaled * mean_cross)
 
 
-def swap(value, turn):
-    return jax.tree.map(
-        lambda v: lax.ppermute(v, "mem", [(i, i ^ turn) for i in range(lax.axis_size("mem"))]), value
-    )
-
-
-def combine(outs, lses):
-    total = jax.nn.logsumexp(jnp.stack(lses), axis=0)
-    rows = outs[0].shape[0]
-    result = 0.0
-    for out, lse in zip(outs, lses):
-        share = jnp.exp(lse - total).T[:, :, None]
-        result = result + share * out.reshape(rows, H, HD).astype(F32)
-    return result.reshape(rows, H * HD), total
-
-
 def local(
     tokens,
     norm_gains,
@@ -1223,10 +1293,25 @@
         lax.dynamic_index_in_dim(slot_rows, me ^ turn, 0, keepdims=False) for turn in range(groups)
     ]
     chosen = jnp.stack(picks).transpose(2, 3, 0, 1).reshape(H, -1, groups * count)
-    normed_one, queries, norm_rows, out_all, lse_all, probs_all, *full = attend(
+    (
+        normed_one,
+        queries,
+        keys_values,
+        norm_rows,
+        lse_all,
+        probs_all,
+        local_out,
+        probs_local,
+        parts,
+        lses,
+        *full,
+    ) = attend(
+        seg_len,
+        near_bias(rel_table),
         tokens,
         table,
         chosen,
+        xl_cache,
         (w_qkv[:, :width], norms),
         (w_qkv[:, width:], w_out, w_up, w_down),
         ("zyx", "zxy", "xyz", "xyz", "zyx", "zxy"),
@@ -1234,25 +1319,13 @@
     )
     full_q, full_kv, full_out, full_up, full_down = [f.reshape(-1, f.shape[2]) for f in full]
     gain_rows, shift_rows = norm_rows[:2], norm_rows[2:4]
-    out_own, out_core, out_x, out_cross = jnp.split(out_all, groups)
-    lse_chip, lse_far = lse_all[:, 0, : 2 * count], lse_all[:, 0, 2 * count :]
 
     inputs = tokens.astype(F32)
     _, scaled_one, inverse_one = norm_forward(inputs, gain_rows[0], shift_rows[0])
-    keys_values = dot(normed_one, full_kv).astype(BF)
-    local_out, probs_local = segment_forward(
-        queries, keys_values, xl_cache, near_bias(rel_table), seg_len
-    )
-
-    own_lse, own_out = lse_chip[:, :count], out_own
-    core_out, core_lse = swap((out_core, lse_chip[:, count:]), 1)
-    other_out, other_lse = swap((out_cross, lse_far[:, count:]), 1)
-    pair_out, pair_lse = combine((out_x, other_out), (lse_far[:, :count], other_lse))
-    far_out, far_lse = swap((pair_out.astype(BF), pair_lse), 2)
     gate_open = jax.nn.sigmoid(gate_bias)
     output, grad_attended, grad_wout, grad_up, grad_down, grad_local, grad_recalled, aux, sums = feed(
-        jnp.stack([own_out, core_out, far_out]),
-        jnp.stack([own_lse, core_lse, far_lse]),
+        parts,
+        lses,
         local_out,
         tokens,
         cotangent,

time: 483 us -> 448 us (0.928); the launches traced: 474 us -> 445 us
  local copies, waits for them, and re-layouts: 36.3 us -> 22.7 us
    pallas_call x2 -> x1, Pallas kernels: 169 us -> 178 us  [attend(): pl.pallas_call(functools.partial(attend_kernel, n_hi, orders), grid=(3, H...]
    pallas_call x1, Pallas kernels: 141 us -> 132 us  [attend_grad(): pl.pallas_call(functools.partial(attend_grad_kernel, n_hi, orders), grid=...]
    unnamed x71 -> x39, local copies, waits for them, and re-layouts: 18.2 us -> 11.3 us
    dot_general x3 -> x2, matrix products: 9.84 us -> 7.61 us  [dot(): return lax.dot_general(left, right, dims, preferred_element_type=F32)]
  transfers between devices with their start and end apart: 6 -> 0, of which waited for: 2 -> 0; matrix products, arithmetic and copies ran while one was open for 3% -> 0% of each run, Pallas kernels for 3% -> 0%
where the time goes in v5:
time: 448 us; the launch traced here: 445 us
  Pallas kernels  397 us (89%)
  local copies, waits for them, and re-layouts  22.7 us (5%)
  matrix products  12.8 us (3%)
  other arithmetic  10.8 us (2%)
    pallas_call x1, Pallas kernels, attend(): pl.pallas_call(functools.partial(attend_kernel, n_hi, orders), grid=(3, H...  178 us
    pallas_call x1, Pallas kernels, attend_grad(): pl.pallas_call(functools.partial(attend_grad_kernel, n_hi, orders), grid=...  132 us
    pallas_call x1, Pallas kernels, feed(): pl.pallas_call(feed_kernel, grid=(hidden // block,), in_specs=[IN_VMEM] *...  46.7 us
    pallas_call x1, Pallas kernels, scatter_sums(): pl.pallas_call(functools.partial(scatter_kernel, n_hi, orders), out_shape...  40.2 us
    unnamed x39, local copies, waits for them, and re-layouts  11.3 us

profile of v5, /device:TPU:0, one launch (start us, length us, event | category | flops | bytes accessed | tf_op | source)
XLA Modules:
  0.0 445.0 jit_solution(2154344565875745521)
XLA Ops:
  0.7 0.7 fusion.28
  1.4 0.7 fusion.29.refs_8_
  2.0 1.1 broadcast_subtract_fusion
  3.2 0.8 pad_add_fusion
  4.0 8.3 %copy.39 = bf16[2048,8,256]{2,0,1:T(8,128)(2,1)} copy(bf16[2048,8,256]{2,1,0:T(8,128)(2,1)} %param.27) | data formatting | bytes 16777216 | tf_op args[10]
  15.4 178.2 %shard_map.240 = (bf16[512,1024]{1,0:T(8,128)(2,1)}, bf16[512,1024]{1,0:T(8,128)(2,1)}, bf16[512,2048]{1,0:T(8,128)(2,1)}, f32[16,1024]{1,0:T(8,128)}, f32[8,1,2...) custom-call(s32[1]{0:T(128)S(6)} %copy.43.refs_0_, ...), custom_call_target="tpu_custom_call" | custom-call | flops 17179869184 | bytes 134217728 | tf_op jit(solution)/shard_map/pallas_call | solution.py:711
  193.6 0.7 broadcast_in_dim.38
  194.3 46.7 %shard_map.241 = (bf16[512,1024]{1,0:T(8,128)(2,1)}, f32[512,1024]{1,0:T(8,128)}, bf16[1024,1024]{1,0:T(8,128)(2,1)}, bf16[1024,4096]{1,0:T(8,128)(2,1)}, bf16[4...) custom-call(bf16[3,512,1024]{2,1,0:T(8,128)(2,1)} %get-tuple-element, ...), custom_call_target="tpu_custom_call" | custom-call | flops 25769803776 | bytes 37748736 | tf_op jit(solution)/shard_map/pallas_call | solution.py:1204
  241.0 131.9 %shard_map.242 = (bf16[512,1024]{1,0:T(8,128)(2,1)}, bf16[512,1024]{1,0:T(8,128)(2,1)}, bf16[512,1024]{1,0:T(8,128)(2,1)}, f32[8,1,256]{2,1,0:T(1,128)}, f32[8,8...) custom-call(bf16[512,1024]{1,0:T(8,128)(2,1)} %get-tuple-element.54.refs_0_, ...), custom_call_target="tpu_custom_call" | custom-call | flops 17179869184 | bytes 134217728 | tf_op jit(solution)/shard_map/pallas_call | solution.py:1077
  372.9 3.3 fusion.36
  376.3 0.9 slice.64
  377.9 4.3 fusion.14
  382.2 0.9 fusion.34
  384.6 5.0 %convolution_convert_fusion = bf16[1024,3072]{1,0:T(8,128)(2,1)S(1)} fusion(bf16[512,1024]{1,0:T(8,128)(2,1)} %get-tuple-element.70, bf16[512,1024]{1,0:T(8,128)(2,1)} %get-tuple-element.68, bf16[512,1024]{1,0:T(8,128)(2,1)S(1)} %copy-done.13, bf16[512,1024]{1,0:T(8,128)(2,1)S(1)} %copy-done.12), kind=kOutput, calls=%fused_computation.1 | convolution fusion | flops 3233808384 | bytes 10485760 | tf_op jit(solution)/shard_map/td,te->de/dot_general | solution.py:1356
  389.6 3.2 fusion.33
  392.8 40.2 %shard_map.243 = (f32[32,1536]{1,0:T(8,128)}, f32[32,1536]{1,0:T(8,128)}, f32[40,128]{1,0:T(8,128)}) custom-call(bf16[32,32,1536]{2,1,0:T(8,128)(2,1)} %bitcast.38, bf16[32,32,1536]{2,1,0:T(8,128)(2,1)} %bitcast.37, f32[40,128]{1,0:T(8,128)} %pad_maximum_fusion.1.refs_2_), custom_call_target="tpu_custom_call" | custom-call | tf_op jit(solution)/shard_map/pallas_call | solution.py:436
  433.0 1.8 pad_maximum_fusion
  434.8 0.7 slice.71
  436.2 0.7 slice.74
  436.9 0.7 copy.37
  437.6 0.7 slice_bitcast_fusion
  438.8 3.7 fusion.13
  443.2 0.8 copy.45
  444.0 0.8 copy.46
  (67 shorter events, 6.5 us)
Async XLA Ops:
  4.0 8.4 %copy-start.4 = (bf16[32,3072]{1,0:T(8,128)(2,1)S(1)}, bf16[32,3072]{1,0:T(8,128)(2,1)}, u32[]{:S(2)}) copy-start(bf16[32,3072]{1,0:T(8,128)(2,1)} %param.20) | copy-start | bytes 589828
  4.0 9.7 %copy-start.8 = (f32[32,8]{0,1:T(8,128)S(1)}, f32[32,8]{0,1:T(8,128)}, u32[]{:S(2)}) copy-start(f32[32,8]{0,1:T(8,128)} %param.24) | copy-start | bytes 3076
  4.0 10.0 %copy-start.9 = (pred[128,32]{0,1:T(32,128)(4,1)S(1)}, pred[128,32]{0,1:T(32,128)(4,1)}, u32[]{:S(2)}) copy-start(pred[128,32]{0,1:T(32,128)(4,1)} %constant.86.clone) | copy-start | bytes 12292
  15.4 178.2 %copy-start.15 = (f32[8]{0:T(128)S(1)}, f32[8]{0:T(128)}, u32[]{:S(2)}) copy-start(f32[8]{0:T(128)} %param.25) | copy-start | bytes 100
  372.9 4.3 copy-start
  372.9 4.9 %copy-start.16 = (bf16[32,32,2048]{2,1,0:T(8,128)(2,1)S(1)}, bf16[32,32,2048]{2,1,0:T(8,128)(2,1)}, u32[]{:S(2)}) copy-start(bf16[32,32,2048]{2,1,0:T(8,128)(2,1)} %get-tuple-element.69) | copy-start | bytes 12582916
  376.2 1.6 copy-start.13
  376.2 1.6 copy-start.14
  377.8 5.3 %copy-start.10 = (f32[8,1,256]{2,1,0:T(1,128)S(1)}, f32[8,1,256]{2,1,0:T(1,128)}, u32[]{:S(2)}) copy-start(f32[8,1,256]{2,1,0:T(1,128)} %get-tuple-element.72) | copy-start | bytes 24580
  377.8 5.5 %copy-start.7 = (f32[8,8,256]{2,1,0:T(8,128)S(1)}, f32[8,8,256]{2,1,0:T(8,128)}, u32[]{:S(2)}) copy-start(f32[8,8,256]{2,1,0:T(8,128)} %get-tuple-element.73) | copy-start | bytes 196612
  377.9 5.6 %copy-start.6 = (f32[128,32]{1,0:T(8,128)S(1)}, f32[128,32]{1,0:T(8,128)}, u32[]{:S(2)}) copy-start(f32[128,32]{1,0:T(8,128)} %constant.87.clone) | copy-start | bytes 49156
  377.9 5.6 %copy-start.11 = (f32[32]{0:T(128)S(1)}, f32[32]{0:T(128)}, u32[]{:S(2)}) copy-start(f32[32]{0:T(128)} %constant.96) | copy-start | bytes 388
  377.9 6.7 %copy-start.12 = (bf16[512,1024]{1,0:T(8,128)(2,1)S(1)}, bf16[512,1024]{1,0:T(8,128)(2,1)}, u32[]{:S(2)}) copy-start(bf16[512,1024]{1,0:T(8,128)(2,1)} %get-tuple-element.65) | copy-start | bytes 3145732
  392.8 46.0 %copy-start.1 = (f32[512,1024]{1,0:T(8,128)S(1)}, f32[512,1024]{1,0:T(8,128)}, u32[]{:S(2)}) copy-start(f32[512,1024]{1,0:T(8,128)} %get-tuple-element.53) | copy-start | bytes 6291460
  438.8 3.8 copy-start.5
  438.8 4.4 copy-start.3
  438.8 5.2 %copy-start.2 = (f32[128,1024]{1,0:T(8,128)S(1)}, f32[128,1024]{1,0:T(8,128)}, u32[]{:S(2)}) copy-start(f32[128,1024]{1,0:T(8,128)} %get-tuple-element.147) | copy-start | bytes 1572868

commit v6 on v5

--- a/solution.py
+++ b/solution.py
@@ -393,63 +393,7 @@
     return [pltpu.SemaphoreType.DMA((n, count)) for count in counts]
 
 
-def scatter_kernel(n_hi, orders, *refs):
-    n = len(orders)
-    ins, small_in, outs, small_out = refs[:n], refs[n], refs[n + 1 : 2 * n + 1], refs[2 * n + 1]
-    rest = refs[2 * n + 2 :]
-    buffers = [rest[k * n : (k + 1) * n] for k in range(5)]
-    place = Place(n_hi)
-    place.greet()
-    scatter = Scatter(
-        place, orders, ins, outs, buffers, rest[5 * n + 1 :], (small_in, small_out, rest[5 * n])
-    )
-    order = near_first(n_hi)[::-1]
-    rounds = len(scatter.small_steps())
-    for k, z in enumerate(order):
-        for a in range(n):
-            scatter.begin(z, a)
-        if k == 0:
-            scatter.small_begin()
-    for k in range(max(len(order) + 2, rounds)):
-        for a in range(n):
-            if k < len(order):
-                scatter.core(order[k], a)
-        for a in range(n):
-            if 0 <= k - 1 < len(order):
-                scatter.one(order[k - 1], a)
-        for a in range(n):
-            if 0 <= k - 2 < len(order):
-                scatter.two(order[k - 2], a)
-        if k < rounds:
-            scatter.small_next(k)
-    for a in range(n):
-        scatter.last(a)
-    scatter.finish()
-
-
-def scatter_sums(arrays, orders, small, collective_id):
-    n = len(arrays)
-    n_hi = lax.axis_size("dp") // 2
-    shapes = [a.shape[1:] for a in arrays]
-    rounds = 3 + (n_hi - 1).bit_length()
-    dma = pltpu.SemaphoreType.DMA
-    return pl.pallas_call(
-        functools.partial(scatter_kernel, n_hi, orders),
-        out_shape=[jax.ShapeDtypeStruct(shape, F32) for shape in shapes]
-        + [jax.ShapeDtypeStruct(small.shape, F32)],
-        in_specs=[ANYWHERE] * n + [IN_VMEM],
-        out_specs=[IN_VMEM] * (n + 1),
-        scratch_shapes=scatter_buffers(shapes, n_hi)
-        + [pltpu.VMEM((2, rounds) + small.shape, F32)]
-        + scatter_sems(n, n_hi)
-        + [dma((rounds,)), dma((rounds,))],
-        compiler_params=pltpu.CompilerParams(
-            collective_id=collective_id, has_side_effects=True, vmem_limit_bytes=56 << 20
-        ),
-    )(*arrays, small)
-
-
-FIRST_STOP, FIRST_SPAN, LAST_SPAN = 2, 60, 88
+FIRST_STOP, FIRST_SPAN, LAST_SPAN, STOP_EVERY = 2, 60, 88, 2
 
 
 def pick_scores(queries, table_ref, chosen, pause):
@@ -515,7 +459,11 @@
 def attend_kernel(n_hi, orders, *refs):
     n = len(orders) - 2
     len_ref, near_ref, x_ref, table_ref, slot_ref, kc_ref, vc_ref = refs[:7]
-    early_in, late_in, refs = refs[7:9], refs[9 : 9 + n], refs[9 + n :]
+    rows, width = x_ref.shape
+    w_qkv, refs = refs[7], refs[8:]
+    early_in = (w_qkv.at[:, pl.ds(0, width)], refs[0])
+    late_in = (w_qkv.at[:, pl.ds(width, 2 * width)],) + tuple(refs[1:n])
+    refs = refs[n:]
     normed_ref, q_ref, kv_ref, norms_ref, lse_ref, p_ref, local_ref, plocal_ref = refs[:8]
     parts_ref, lses_ref, full_q, full_kv = refs[8:12]
     late_out, refs = refs[12 : 11 + n], refs[11 + n :]
@@ -528,7 +476,6 @@
     place = Place(n_hi)
     early = Gather(place, orders[:2], early_in, (wq, norms), sems[:3])
     late = Gather(place, orders[2:], late_in, (wkv,) + tuple(late_out), sems[3:])
-    rows, width = x_ref.shape
     lanes = pl.ds(pl.multiple_of(head * HD, HD), HD)
 
     def remote(src, dst, send, recv, to):
@@ -596,6 +543,7 @@
         for a in range(n):
             span = FIRST_SPAN if a == 0 else LAST_SPAN
             stop = FIRST_STOP + (level * n + a) * span // (n * len(late.levels()))
+            stop = stop // STOP_EVERY * STOP_EVERY
             events.append((min(stop, 4 * ticks - 1 if a == 0 else 12 * H - 1), (a, hops)))
 
     def pause(part, first=0, end=4 * ticks):
@@ -689,10 +637,11 @@
             keep(k).wait()
 
 
-def attend(length, near, x, table, chosen, cache, early, late, orders, collective_id):
-    n, n_hi = len(late), lax.axis_size("dp") // 2
+def attend(length, near, x, table, chosen, cache, w_qkv, norms, late, orders, collective_id):
+    n, n_hi = len(late) + 1, lax.axis_size("dp") // 2
     devices = n_hi * 8
     (rows, width), slots = x.shape, table.shape[1]
+    own = w_qkv.shape[0]
     dma = pltpu.SemaphoreType.DMA
     shape = jax.ShapeDtypeStruct
 
@@ -720,7 +669,7 @@
             column(),
             column(H),
         ]
-        + [ANYWHERE] * (2 + n),
+        + [ANYWHERE] * (1 + n),
         out_specs=[
             IN_VMEM,
             IN_VMEM,
@@ -747,13 +696,14 @@
             shape((H, 2 * W, W), BF),
             shape((3, rows, width), BF),
             shape((3, H, rows), F32),
-            gathered(early[0]),
+            shape((devices, own, width), BF),
+            shape((devices, own, 2 * width), BF),
         ]
         + [gathered(a) for a in late],
         scratch_shapes=[
-            pltpu.VMEM((devices,) + early[0].shape, BF),
-            pltpu.VMEM((devices,) + late[0].shape, BF),
-            pltpu.VMEM((devices,) + early[1].shape, BF),
+            pltpu.VMEM((devices, own, width), BF),
+            pltpu.VMEM((devices, own, 2 * width), BF),
+            pltpu.VMEM((devices,) + norms.shape, BF),
             pltpu.VMEM((4, rows, width), BF),
             pltpu.VMEM((4, rows, width), BF),
             pltpu.VMEM((3, rows, width), BF),
@@ -775,7 +725,7 @@
         cost_estimate=pl.CostEstimate(
             flops=16 * rows * slots * HD * H, bytes_accessed=128 << 20, transcendentals=0
         ),
-    )(length, near, x, table, chosen, cache, cache, *early, *late)
+    )(length, near, x, table, chosen, cache, cache, w_qkv, norms, *late)
 
 
 def near_buckets():
@@ -1244,18 +1194,128 @@
     )(parts, lses, local_out, x, cotangent, gate_row, norm_rows, w_out, w_up, w_down)
 
 
-def norm_forward(values, gain_row, shift_row):
-    center = values - jnp.mean(values, axis=-1, keepdims=True)
-    inverse = lax.rsqrt(jnp.mean(center * center, axis=-1, keepdims=True) + EPSILON)
-    scaled = center * inverse
-    return (scaled * gain_row + shift_row, scaled, inverse)
-
-
-def norm_backward(grad_normed, scaled, inverse, gain_row):
-    grad_scaled = grad_normed * gain_row
-    mean_grad = jnp.mean(grad_scaled, axis=-1, keepdims=True)
-    mean_cross = jnp.mean(grad_scaled * scaled, axis=-1, keepdims=True)
-    return inverse * (grad_scaled - mean_grad - scaled * mean_cross)
+def close_kernel(n_hi, orders, *refs):
+    n = len(orders)
+    normed_ref, gq_ref, gk_ref, gv_ref, x_ref, gatt_ref, norms_ref, sums_ref, rest_ref = refs[:9]
+    q_hbm, kv_hbm, share_ref, tokens_ref, small_ref = refs[9:14]
+    wq, wkv, small_in, small_buffer, load_sem = refs[14:19]
+    grads = refs[19 : 19 + n]
+    rest = refs[19 + n :]
+    buffers = [rest[k * n : (k + 1) * n] for k in range(5)]
+    place = Place(n_hi)
+    devices, rows, columns = grads[0].shape
+    outs = [share_ref.at[:, pl.ds(a * columns, columns)] for a in range(n)]
+    scatter = Scatter(
+        place, orders, grads, outs, buffers, rest[5 * n :], (small_in, small_ref, small_buffer)
+    )
+    place.greet()
+    loads = [
+        pltpu.make_async_copy(src, dst, load_sem.at[k])
+        for k, (src, dst) in enumerate(((q_hbm, wq), (kv_hbm, wkv)))
+    ]
+    for load in loads:
+        load.start()
+    sources = (gq_ref, gk_ref, gv_ref)
+    width = x_ref.shape[1]
+    step = 256
+    order = near_first(n_hi)[::-1]
+    normed_t = normed_ref[...].T
+    for a in range(n):
+        for at in range(0, columns, step):
+            source, first = divmod(a * columns + at, width)
+            grad = dot(normed_t, sources[source][:, pl.ds(first, step)])
+            grads[a][:, :, pl.ds(at, step)] = grad.reshape(devices, rows, step).astype(BF)
+        for z in order:
+            scatter.begin(z, a)
+    tokens = x_ref.shape[0]
+    piece = tokens // 4
+    sums = [0.0, 0.0]
+
+    def norm_piece(k):
+        at = pl.ds(k * piece, piece)
+        x = x_ref[at, :].astype(F32)
+        center = x - jnp.mean(x, axis=-1, keepdims=True)
+        inverse = lax.rsqrt(jnp.mean(center * center, axis=-1, keepdims=True) + EPSILON)
+        scaled = center * inverse
+        grad = (
+            dot(gq_ref[at, :], wq[...], NT)
+            + dot(gk_ref[at, :], wkv[:, pl.ds(0, width)], NT)
+            + dot(gv_ref[at, :], wkv[:, pl.ds(width, width)], NT)
+        )
+        sums[0] = sums[0] + jnp.sum(grad * scaled, axis=0, keepdims=True)
+        sums[1] = sums[1] + jnp.sum(grad, axis=0, keepdims=True)
+        grad = grad * norms_ref[0:1]
+        mean_grad = jnp.mean(grad, axis=-1, keepdims=True)
+        mean_cross = jnp.mean(grad * scaled, axis=-1, keepdims=True)
+        tokens_ref[at, :] = gatt_ref[at, :] + inverse * (grad - mean_grad - scaled * mean_cross)
+
+    def small_go():
+        lanes = width // 8
+        for k, row in enumerate((sums[0], sums_ref[0:1], sums[1], sums_ref[1:2])):
+            for g in range(8):
+                small_in[8 * k + g : 8 * k + g + 1] = row[:, g * lanes : (g + 1) * lanes]
+        small_in[32:] = rest_ref[...]
+        scatter.small_begin()
+
+    for z in order:
+        for a in range(n):
+            scatter.core(z, a)
+    for load in loads:
+        load.wait()
+    for k in range(4):
+        norm_piece(k)
+        if k == 1:
+            for a in range(n):
+                scatter.one(order[0], a)
+    small_go()
+    rounds = len(scatter.small_steps())
+    for k in range(max(n_hi + 1, rounds)):
+        for a in range(n):
+            if 0 < k < n_hi:
+                scatter.one(order[k], a)
+        for a in range(n):
+            if 0 <= k - 1 < n_hi:
+                scatter.two(order[k - 1], a)
+        if k < rounds:
+            scatter.small_next(k)
+    for a in range(n):
+        scatter.last(a)
+    scatter.finish()
+
+
+def close(
+    normed, grads, x, grad_attended, norm_rows, sums, rest, full_q, full_kv, rows, orders, collective_id
+):
+    n, n_hi = len(orders), lax.axis_size("dp") // 2
+    width = x.shape[1]
+    columns = 3 * width // n
+    rounds = 3 + (n_hi - 1).bit_length()
+    dma = pltpu.SemaphoreType.DMA
+    small = (40, width // 8)
+    return pl.pallas_call(
+        functools.partial(close_kernel, n_hi, orders),
+        out_shape=[
+            jax.ShapeDtypeStruct((rows, 3 * width), F32),
+            jax.ShapeDtypeStruct(x.shape, F32),
+            jax.ShapeDtypeStruct(small, F32),
+        ],
+        in_specs=[IN_VMEM] * 9 + [ANYWHERE] * 2,
+        out_specs=[IN_VMEM] * 3,
+        scratch_shapes=[
+            pltpu.VMEM(full_q.shape, BF),
+            pltpu.VMEM(full_kv.shape, BF),
+            pltpu.VMEM(small, F32),
+            pltpu.VMEM((2, rounds) + small, F32),
+            dma((2,)),
+        ]
+        + [pltpu.VMEM((n_hi * 8, rows, columns), BF)] * n
+        + scatter_buffers([(rows, columns)] * n, n_hi)
+        + scatter_sems(n, n_hi)
+        + [dma((rounds,)), dma((rounds,))],
+        compiler_params=pltpu.CompilerParams(
+            collective_id=collective_id, has_side_effects=True, vmem_limit_bytes=56 << 20
+        ),
+    )(normed, *grads, x, grad_attended, norm_rows, sums, rest, full_q, full_kv)
 
 
 def local(
@@ -1283,10 +1343,12 @@
     devices = lax.axis_size("dp") * groups
     number = lax.axis_index("dp") * groups + me
     own = norm_gains.shape[1]
-    norms = jnp.pad(
-        jnp.concatenate([norm_gains, norm_shifts], axis=0), ((0, 12), (0, 128 - own))
+    per = 128 // own
+    norms = jnp.tile(
+        jnp.pad(jnp.concatenate([norm_gains, norm_shifts], axis=0), ((0, 12), (0, 0))), (1, per)
     )
-    norms = jnp.roll(norms, number % (128 // own) * own, axis=1)
+    here = lax.broadcasted_iota(jnp.int32, norms.shape, 1) // own == number % per
+    norms = jnp.where(here, norms, jnp.zeros_like(norms))
     table = memory.transpose(1, 0, 2)
     slot_rows = (slot_index - me * slot_count).reshape(groups, count, H, -1)
     picks = [
@@ -1312,16 +1374,13 @@
         table,
         chosen,
         xl_cache,
-        (w_qkv[:, :width], norms),
-        (w_qkv[:, width:], w_out, w_up, w_down),
+        w_qkv,
+        norms,
+        (w_out, w_up, w_down),
         ("zyx", "zxy", "xyz", "xyz", "zyx", "zxy"),
         0,
     )
     full_q, full_kv, full_out, full_up, full_down = [f.reshape(-1, f.shape[2]) for f in full]
-    gain_rows, shift_rows = norm_rows[:2], norm_rows[2:4]
-
-    inputs = tokens.astype(F32)
-    _, scaled_one, inverse_one = norm_forward(inputs, gain_rows[0], shift_rows[0])
     gate_open = jax.nn.sigmoid(gate_bias)
     output, grad_attended, grad_wout, grad_up, grad_down, grad_local, grad_recalled, aux, sums = feed(
         parts,
@@ -1348,39 +1407,25 @@
         probs_all,
         lse_all,
         [g.reshape(devices, -1, g.shape[1]) for g in (grad_wout, grad_up, grad_down)],
-        ("yxz", "yxz", "xyz"),
+        ("xyz", "yxz", "yxz"),
         1,
     )
     grad_table = table_gradient(diagonals, totals)
-    grad_qkv_low = jnp.concatenate([grad_query, grad_keys, grad_values], axis=1)
-    grad_wqkv = jnp.einsum("td,te->de", normed_one, grad_qkv_low, preferred_element_type=F32)
-    grad_normed_one = dot(grad_qkv_low[:, :width], full_q, NT) + dot(
-        grad_qkv_low[:, width:], full_kv, NT
-    )
-    grad_tokens = grad_attended + norm_backward(
-        grad_normed_one, scaled_one, inverse_one, gain_rows[0]
-    )
-    grad_norms = jnp.stack(
-        [
-            jnp.sum(grad_normed_one * scaled_one, axis=0),
-            sums[0],
-            jnp.sum(grad_normed_one, axis=0),
-            sums[1],
-        ]
-    )
     rest = jnp.pad(jnp.concatenate([grad_table.reshape(-1), grad_gate]), (0, 1024 - 264))
-    small = jnp.concatenate([grad_norms.reshape(-1, 128), rest.reshape(-1, 128)], axis=0)
-    half = grad_wqkv.shape[1] // 2
-    share_left, share_right, small = scatter_sums(
-        [
-            g.astype(BF).reshape(devices, -1, half)
-            for g in (grad_wqkv[:, :half], grad_wqkv[:, half:])
-        ],
+    share_qkv, grad_tokens, small = close(
+        normed_one,
+        (grad_query, grad_keys, grad_values),
+        tokens,
+        grad_attended,
+        norm_rows,
+        sums,
+        rest.reshape(8, -1),
+        full_q,
+        full_kv,
+        w_qkv.shape[0],
         ("yxz", "xyz"),
-        small,
         2,
     )
-    share_qkv = jnp.concatenate([share_left, share_right], axis=1)
     share_norms = lax.dynamic_slice_in_dim(
         small[:32].reshape(4, width), number * own, own, axis=1
     )

time: 448 us -> 445 us (level)
  Pallas kernels: 397 us -> 410 us
  matrix products: 12.8 us -> 0.16 us
    pallas_call x1, Pallas kernels: 40.2 us -> 55.2 us  [close(): pl.pallas_call(functools.partial(close_kernel, n_hi, orders), out_shape=[...]
    dot_general x3 -> x0, matrix products: 12.6 us -> none  [the longest x2 7.61 us: dot(): return lax.dot_general(left, right, dims, preferred_element_type=F32)]
    slice x5 -> x1, local copies, waits for them, and re-layouts: 6.24 us -> 0.76 us  [local(): sums[2].reshape(H, HD)]
    unnamed x39 -> x21, local copies, waits for them, and re-layouts: 11.3 us -> 15.2 us
where the time goes in v6:
time: 445 us; the launch traced here: 442 us
  Pallas kernels  410 us (92%)
  local copies, waits for them, and re-layouts  21.9 us (5%)
  other arithmetic  8.04 us (2%)
    pallas_call x1, Pallas kernels, attend(): pl.pallas_call(functools.partial(attend_kernel, n_hi, orders), grid=(3, H...  177 us
    pallas_call x1, Pallas kernels, attend_grad(): pl.pallas_call(functools.partial(attend_grad_kernel, n_hi, orders), grid=...  131 us
    pallas_call x1, Pallas kernels, close(): pl.pallas_call(functools.partial(close_kernel, n_hi, orders), out_shape=[...  55.2 us
    pallas_call x1, Pallas kernels, feed(): pl.pallas_call(feed_kernel, grid=(hidden // block,), in_specs=[IN_VMEM] *...  46.7 us
    unnamed x21, local copies, waits for them, and re-layouts  15.2 us

profile of v6, /device:TPU:0, one launch (start us, length us, event | category | flops | bytes accessed | tf_op | source)
XLA Modules:
  0.0 441.7 jit_solution(12628653499834412748)
XLA Ops:
  1.3 0.9 slice_reduce_fusion
  2.2 0.7 add_divide_fusion
  2.9 0.7 broadcast_in_dim.38
  3.5 0.8 broadcast_subtract_fusion.1
  4.3 0.7 fusion.3
  5.8 0.8 select_reduce_fusion
  7.2 1.1 broadcast_subtract_fusion
  8.3 0.8 pad_add_fusion
  9.1 8.3 %copy.39 = bf16[2048,8,256]{2,0,1:T(8,128)(2,1)} copy(bf16[2048,8,256]{2,1,0:T(8,128)(2,1)} %param.27) | data formatting | bytes 16777216 | tf_op args[10]
  17.5 176.8 %shard_map.240 = (bf16[512,1024]{1,0:T(8,128)(2,1)}, bf16[512,1024]{1,0:T(8,128)(2,1)}, bf16[512,2048]{1,0:T(8,128)(2,1)}, f32[16,1024]{1,0:T(8,128)}, f32[8,1,2...) custom-call(s32[1]{0:T(128)S(6)} %copy.45.refs_0_, ...), custom_call_target="tpu_custom_call" | custom-call | flops 17179869184 | bytes 134217728 | tf_op jit(solution)/shard_map/pallas_call | solution.py:660
  194.3 46.7 %shard_map.241 = (bf16[512,1024]{1,0:T(8,128)(2,1)}, f32[512,1024]{1,0:T(8,128)}, bf16[1024,1024]{1,0:T(8,128)(2,1)}, bf16[1024,4096]{1,0:T(8,128)(2,1)}, bf16[4...) custom-call(bf16[3,512,1024]{2,1,0:T(8,128)(2,1)} %get-tuple-element, ...), custom_call_target="tpu_custom_call" | custom-call | flops 25769803776 | bytes 37748736 | tf_op jit(solution)/shard_map/pallas_call | solution.py:1154
  241.0 131.2 %shard_map.242 = (bf16[512,1024]{1,0:T(8,128)(2,1)}, bf16[512,1024]{1,0:T(8,128)(2,1)}, bf16[512,1024]{1,0:T(8,128)(2,1)}, f32[8,1,256]{2,1,0:T(1,128)}, f32[8,8...) custom-call(bf16[512,1024]{1,0:T(8,128)(2,1)} %get-tuple-element.54.refs_0_, ...), custom_call_target="tpu_custom_call" | custom-call | flops 17179869184 | bytes 134217728 | tf_op jit(solution)/shard_map/pallas_call | solution.py:1027
  372.2 1.0 reduce_sum.37
  373.2 0.8 slice.36
  374.1 0.9 slice_reduce_fusion.1
  376.0 55.2 %shard_map.243 = (f32[32,3072]{1,0:T(8,128)}, f32[512,1024]{1,0:T(8,128)}, f32[40,128]{1,0:T(8,128)}) custom-call(bf16[512,1024]{1,0:T(8,128)(2,1)} %get-tuple-element.53.refs_0_, bf16[512,1024]{1,0:T(8,128)(2,1)} %get-tuple-element.65.refs_1_, bf16[512,1024]{1,0:T(8,128)(2,1)} %get-tuple-element.66.refs_2_, bf16[512,1024]{1,0:T(8,128)(2,1)} %get-tuple-element.67.refs_3_, ...), custom_call_target="tpu_custom_call" | custom-call | tf_op jit(solution)/shard_map/pallas_call | solution.py:1295
  431.2 0.8 slice.40
  432.0 0.7 slice_bitcast_fusion
  432.6 0.7 slice.37
  434.6 0.7 copy.37
  435.3 3.2 copy.46
  438.5 0.7 copy.47
  439.9 0.8 copy.49
  440.7 0.8 copy.50
  (36 shorter events, 4.5 us)
Async XLA Ops:
  241.0 133.1 %copy-start.6 = (f32[8]{0:T(128)S(1)}, f32[8]{0:T(128)}, u32[]{:S(2)}) copy-start(f32[8]{0:T(128)} %param.25) | copy-start | bytes 100
  241.0 134.1 %copy-start.4 = (f32[128,32]{1,0:T(8,128)S(1)}, f32[128,32]{1,0:T(8,128)}, u32[]{:S(2)}) copy-start(f32[128,32]{1,0:T(8,128)} %constant.76.clone) | copy-start | bytes 49156
  241.0 134.1 %copy-start.5 = (f32[32]{0:T(128)S(1)}, f32[32]{0:T(128)}, u32[]{:S(2)}) copy-start(f32[32]{0:T(128)} %constant.85) | copy-start | bytes 388
  431.2 7.3 %copy-start.2 = (f32[32,3072]{1,0:T(8,128)S(1)}, f32[32,3072]{1,0:T(8,128)}, u32[]{:S(2)}) copy-start(f32[32,3072]{1,0:T(8,128)} %get-tuple-element.134) | copy-start | bytes 1179652
  431.2 8.1 %copy-start.3 = (f32[32,1024]{1,0:T(8,128)S(1)}, f32[32,1024]{1,0:T(8,128)}, u32[]{:S(2)}) copy-start(f32[32,1024]{1,0:T(8,128)} %get-tuple-element.135) | copy-start | bytes 393220
  431.2 8.7 %copy-start.1 = (f32[32,4096]{1,0:T(8,128)S(1)}, f32[32,4096]{1,0:T(8,128)}, u32[]{:S(2)}) copy-start(f32[32,4096]{1,0:T(8,128)} %get-tuple-element.136) | copy-start | bytes 1572868
  435.3 5.4 %copy-start = (f32[128,1024]{1,0:T(8,128)S(1)}, f32[128,1024]{1,0:T(8,128)}, u32[]{:S(2)}) copy-start(f32[128,1024]{1,0:T(8,128)} %get-tuple-element.137) | copy-start | bytes 1572868
